TPU v7x, 512 devices: a whole 4x4x16 slice. The times are simulated.
512 devices in a mesh: dp: 32 (over x, z_lo), group: 8 (over z_hi, y), half: 2 (over core).
Axes of the slice: x: 4, y: 4, z: 16 (z_hi: 2, z_lo: 8; z = z_hi * 8 + z_lo), core: 2. Of those that a mesh axis runs over, the one named last changes fastest.
Arguments:
- activations: bfloat16 [8192, 8192], P('dp', ('group', 'half')), may hold values from -6 to 6
- output_grads: bfloat16 [8192, 28672], P('dp', ('group', 'half')), may hold values from -6 to 6
- out_factors: bfloat16 [1024, 28672], P('dp', ('group', 'half')), may hold values from -0.005859375 to 0.005859375
- in_factors: bfloat16 [1024, 8192], P('dp', ('group', 'half')), may hold values from -0.0625 to 0.0625
- basis: bfloat16 [8192, 8192], P(('group', 'half'), 'dp'), may hold values from -0.0625 to 0.0625
- eigvals: float32 [8192], P('dp'), may hold values from 0.1 to 10
Outputs:
- influence: float32 [8192, 32], P(('dp', 'group', 'half'))
All inputs are finite; a program needn't handle non-finite values.
Results may differ from a plain program's by a relative error of at most 0.0038.
Values may be sent and summed in bfloat16 or wider, within the bound.
No kernel may reach another device: no remote copies, remote signals or barrier semaphores. Data moves between devices by JAX's collectives and lax.ppermute only.
A program may use at most 64 MiB of HBM per device.

v0:
```python
import jax
import jax.numpy as jnp
from jax import lax
from jax.sharding import PartitionSpec as P

RANK = 32


DAMP = 0.01


def passed_along(shard, axis, by):
    size = lax.axis_size(axis)
    return lax.ppermute(shard, axis, [(i, (i + by) % size) for i in range(size)])


def on_device(activations, output_grads, out_factors, in_factors, basis, eigvals):
    partial_rot = jnp.dot(
        lax.all_gather(in_factors, "dp", axis=0, tiled=True),
        basis,
        preferred_element_type=jnp.float32,
    )
    rotated = lax.psum(partial_rot, ("group", "half"))
    scaled = (rotated / (eigvals + DAMP)[None, :]).astype(jnp.bfloat16)
    precond = lax.psum_scatter(
        lax.dot_general(
            scaled, basis, (((1,), (1,)), ((), ())), preferred_element_type=jnp.float32
        ),
        "dp",
        scatter_dimension=0,
        tiled=True,
    ).astype(jnp.bfloat16)
    tile_rows = out_factors.shape[0]
    boundary = out_factors.shape[1]
    cycle_size = lax.axis_size("dp")
    position = lax.axis_index("dp")
    packed = jnp.concatenate([out_factors, precond], axis=1)
    empty_acc = jnp.zeros((activations.shape[0], tile_rows * cycle_size), jnp.float32)

    def absorb(totals, tile_now, start):
        input_side = lax.dot_general(
            activations,
            tile_now[:, boundary:],
            (((1,), (1,)), ((), ())),
            preferred_element_type=jnp.float32,
        )
        output_side = lax.dot_general(
            output_grads,
            tile_now[:, :boundary],
            (((1,), (1,)), ((), ())),
            preferred_element_type=jnp.float32,
        )
        return (
            lax.dynamic_update_slice_in_dim(totals[0], input_side, start, 1),
            lax.dynamic_update_slice_in_dim(totals[1], output_side, start, 1),
        )

    totals = absorb((empty_acc, empty_acc), packed, position * tile_rows)

    def advance(s, carry):
        sums, moving = carry
        moving = passed_along(moving, "dp", 1)
        anchor = (position - s) % cycle_size
        return (absorb(sums, moving, anchor * tile_rows), moving)

    totals, _ = lax.fori_loop(1, cycle_size, advance, (totals, packed))
    input_part, output_part = (
        lax.psum_scatter(totals[0], ("group", "half"), scatter_dimension=0, tiled=True),
        lax.psum_scatter(totals[1], ("group", "half"), scatter_dimension=0, tiled=True),
    )
    paired = input_part * output_part
    shares = paired.reshape(paired.shape[0], -1, RANK)
    return jnp.sum(shares, axis=2)


def solution(mesh):
    return jax.shard_map(
        on_device,
        mesh=mesh,
        in_specs=(
            P("dp", ("group", "half")),
            P("dp", ("group", "half")),
            P("dp", ("group", "half")),
            P("dp", ("group", "half")),
            P(("group", "half"), "dp"),
            P("dp"),
        ),
        out_specs=P(("dp", "group", "half"), None),
        check_vma=False,
    )
```

profile of v0, /device:TPU:2, one launch (start us, length us, event | category | flops | bytes accessed | tf_op | source)
XLA Modules:
  0.0 1491.4 jit_solution(3388345380910052806)
XLA Ops:
  7.3 211.5 %all-gather.2.cloned.1.call-done = bf16[1024,512]{1,0:T(8,128)(2,1)} async-done(((bf16[32,512]{1,0:T(8,128)(2,1)}), bf16[1024,512]{1,0:T(8,128)(2,1)}) %all-gather.2.cloned.1.call-update) | async-done | bytes 1048592 | tf_op jit(solution)/shard_map/all_gather | solution.py:19
  218.8 2.6 fusion.5
  221.5 275.2 %all-reduce.2.cloned.1.call-done = f32[1024,256]{1,0:T(8,128)} async-done(((f32[1024,256]{1,0:T(8,128)}), f32[1024,256]{1,0:T(8,128)}) %all-reduce.2.cloned.1.call-update) | async-done | bytes 1048592 | tf_op jit(solution)/shard_map/psum | solution.py:23
  496.7 3.0 fusion.3
  502.2 223.5 %reduce-scatter.8.cloned.1.call-done = f32[32,512]{1,0:T(8,128)} async-done(((f32[1024,512]{1,0:T(8,128)}), f32[32,512]{1,0:T(8,128)}) %reduce-scatter.8.cloned.1.call-update) | async-done | bytes 65552 | tf_op jit(solution)/shard_map/reduce_scatter | solution.py:25
  726.8 492.8 %while.19 = (s32[]{:T(128)}, f32[256,1024]{0,1:T(8,128)S(1)}, f32[256,1024]{0,1:T(8,128)}, bf16[32,2304]{1,0:T(8,128)(2,1)S(1)}, bf16[256,512]{1,0:T(8,128)(2,1)...) while((s32[]{:T(128)}, f32[256,1024]{0,1:T(8,128)S(1)}, ...), condition=%wide.region_3.4_spmd, body=%wide.region_2.3_spmd.sunk | while | flops 37748752 | bytes 2277708 | solution.py:66
  726.8 1.9 collective-permute-start
  728.8 12.6 collective-permute-done
  742.6 1.9 collective-permute-start
  744.5 12.6 collective-permute-done
  758.3 1.9 collective-permute-start
  760.3 12.6 collective-permute-done
  776.1 13.7 collective-permute-done
  790.9 1.9 collective-permute-start
  792.9 13.5 collective-permute-done
  807.6 1.9 collective-permute-start
  809.6 12.7 collective-permute-done
  823.5 1.9 collective-permute-start
  825.4 12.6 collective-permute-done
  839.2 1.9 collective-permute-start
  841.2 12.6 collective-permute-done
  855.0 1.9 collective-permute-start
  856.9 12.6 collective-permute-done
  870.7 1.9 collective-permute-start
  872.7 12.6 collective-permute-done
  886.5 1.9 collective-permute-start
  888.4 12.6 collective-permute-done
  902.2 1.9 collective-permute-start
  904.2 12.6 collective-permute-done
  918.0 1.9 collective-permute-start
  920.0 12.6 collective-permute-done
  933.7 1.9 collective-permute-start
  935.7 12.6 collective-permute-done
  949.5 1.9 collective-permute-start
  951.5 12.6 collective-permute-done
  967.2 12.6 collective-permute-done
  981.0 1.9 collective-permute-start
  983.0 13.5 collective-permute-done
  997.7 1.9 collective-permute-start
  999.7 13.7 collective-permute-done
  1016.5 12.9 collective-permute-done
  1032.6 12.6 collective-permute-done
  1046.3 1.9 collective-permute-start
  1048.3 12.6 collective-permute-done
  1062.1 1.9 collective-permute-start
  1064.1 12.6 collective-permute-done
  1077.8 1.9 collective-permute-start
  1079.8 12.6 collective-permute-done
  1093.6 1.9 collective-permute-start
  1095.6 12.6 collective-permute-done
  1109.4 1.9 collective-permute-start
  1111.3 12.6 collective-permute-done
  1125.1 1.9 collective-permute-start
  1127.1 12.6 collective-permute-done
  1140.9 1.9 collective-permute-start
  1142.8 12.6 collective-permute-done
  1156.6 1.9 collective-permute-start
  1158.6 12.6 collective-permute-done
  1174.4 12.6 collective-permute-done
  1190.1 12.6 collective-permute-done
  1205.9 12.6 collective-permute-done
  1219.6 2.6 copy.10
  1223.7 155.7 %reduce-scatter.12.cloned.1.call-done = f32[16,1024]{1,0:T(8,128)} async-done(((f32[256,1024]{1,0:T(8,128)}), f32[16,1024]{1,0:T(8,128)}) %reduce-scatter.12.cloned.1.call-update) | async-done | bytes 65552
  1380.4 102.6 %reduce-scatter.10.cloned.1.call-done = f32[16,1024]{1,0:T(8,128)} async-done(((f32[256,1024]{1,0:T(8,128)}), f32[16,1024]{1,0:T(8,128)}) %reduce-scatter.10.cloned.1.call-update) | async-done | bytes 65552
  (132 shorter events, 59.0 us)
Async XLA Ops:
  6.5 212.2 %copy-start = (bf16[512,256]{1,0:T(8,128)(2,1)S(1)}, bf16[512,256]{1,0:T(8,128)(2,1)}, u32[]{:S(2)}) copy-start(bf16[512,256]{1,0:T(8,128)(2,1)} %param.12) | copy-start | bytes 786436
  6.5 214.9 %copy-start.4 = (f32[256]{0:T(256)S(1)}, f32[256]{0:T(256)}, u32[]{:S(2)}) copy-start(f32[256]{0:T(256)} %param.13) | copy-start | bytes 3076
  6.5 212.2 %all-gather.2.cloned.1.call-start = ((), (), s32[]{:S(2)}) async-start(), calls=%async_computation.3 | async-start | bytes 1081344 | tf_op jit(solution)/shard_map/all_gather | solution.py:19
  7.3 489.4 %all-reduce.2.cloned.1.call-start = ((), (), s32[]{:S(2)}) async-start(), calls=%async_computation.4 | async-start | bytes 2097152 | tf_op jit(solution)/shard_map/psum | solution.py:23
  221.4 504.3 %reduce-scatter.8.cloned.1.call-start = ((), (), s32[]{:S(2)}) async-start(), calls=%async_computation.5 | async-start | bytes 2162688 | tf_op jit(solution)/shard_map/reduce_scatter | solution.py:25
  499.7 1.4 copy-start.1
  499.7 1.5 copy-start.3
  499.8 226.9 %copy-start.2 = (bf16[256,512]{1,0:T(8,128)(2,1)S(1)}, bf16[256,512]{1,0:T(8,128)(2,1)}, u32[]{:S(2)}) copy-start(bf16[256,512]{1,0:T(8,128)(2,1)} %param.8) | copy-start | bytes 786436
  499.8 879.6 %reduce-scatter.12.cloned.1.call-start = ((), (), s32[]{:S(2)}) async-start(), calls=%async_computation.7 | async-start | bytes 1114112
  726.8 14.6 collective-permute-start
  742.6 14.6 collective-permute-start
  758.3 14.6 collective-permute-start
  774.1 15.7 %collective-permute-start = (bf16[32,2304]{1,0:T(8,128)(2,1)S(1)}, bf16[32,2304]{1,0:T(8,128)(2,1)S(1)}, u32[]{:S(2)}, u32[]{:S(2)}) collective-permute-start(bf16[32,2304]{1,0:T(8,128)(2,1)S(1)} %get-tuple-element.257), channel_id=1, source_target_pairs={{0,16},{16,32},{32,48},{48,64},{64,80},{80,96},{96,112},{112,128},... | collective-permute-start | bytes 442376 | tf_op jit(solution)/shard_map/while/body/eval_jaxpr/ppermute | solution.py:14
  790.9 15.5 %collective-permute-start = (bf16[32,2304]{1,0:T(8,128)(2,1)S(1)}, bf16[32,2304]{1,0:T(8,128)(2,1)S(1)}, u32[]{:S(2)}, u32[]{:S(2)}) collective-permute-start(bf16[32,2304]{1,0:T(8,128)(2,1)S(1)} %get-tuple-element.257), channel_id=1, source_target_pairs={{0,16},{16,32},{32,48},{48,64},{64,80},{80,96},{96,112},{112,128},... | collective-permute-start | bytes 442376 | tf_op jit(solution)/shard_map/while/body/eval_jaxpr/ppermute | solution.py:14
  807.6 14.7 collective-permute-start
  823.5 14.6 collective-permute-start
  839.2 14.6 collective-permute-start
  855.0 14.6 collective-permute-start
  870.7 14.6 collective-permute-start
  886.5 14.6 collective-permute-start
  902.2 14.6 collective-permute-start
  918.0 14.6 collective-permute-start
  933.7 14.6 collective-permute-start
  949.5 14.6 collective-permute-start
  965.2 14.6 collective-permute-start
  981.0 15.5 %collective-permute-start = (bf16[32,2304]{1,0:T(8,128)(2,1)S(1)}, bf16[32,2304]{1,0:T(8,128)(2,1)S(1)}, u32[]{:S(2)}, u32[]{:S(2)}) collective-permute-start(bf16[32,2304]{1,0:T(8,128)(2,1)S(1)} %get-tuple-element.257), channel_id=1, source_target_pairs={{0,16},{16,32},{32,48},{48,64},{64,80},{80,96},{96,112},{112,128},... | collective-permute-start | bytes 442376 | tf_op jit(solution)/shard_map/while/body/eval_jaxpr/ppermute | solution.py:14
  997.7 15.7 %collective-permute-start = (bf16[32,2304]{1,0:T(8,128)(2,1)S(1)}, bf16[32,2304]{1,0:T(8,128)(2,1)S(1)}, u32[]{:S(2)}, u32[]{:S(2)}) collective-permute-start(bf16[32,2304]{1,0:T(8,128)(2,1)S(1)} %get-tuple-element.257), channel_id=1, source_target_pairs={{0,16},{16,32},{32,48},{48,64},{64,80},{80,96},{96,112},{112,128},... | collective-permute-start | bytes 442376 | tf_op jit(solution)/shard_map/while/body/eval_jaxpr/ppermute | solution.py:14
  1014.5 14.9 collective-permute-start
  1030.6 14.6 collective-permute-start
  1046.3 14.6 collective-permute-start
  1062.1 14.6 collective-permute-start
  1077.8 14.6 collective-permute-start
  1093.6 14.6 collective-permute-start
  1109.4 14.6 collective-permute-start
  1125.1 14.6 collective-permute-start
  1140.9 14.6 collective-permute-start
  1156.6 14.6 collective-permute-start
  1172.4 14.6 collective-permute-start
  1188.1 14.6 collective-permute-start
  1203.9 14.6 collective-permute-start
  1222.2 260.8 %reduce-scatter.10.cloned.1.call-start = ((), (), s32[]{:S(2)}) async-start(), calls=%async_computation.6 | async-start | bytes 1114112
Sparse Core Ops, SparseCore 0:
  9.4 209.2 all-gather.1
  221.7 274.9 all-reduce.1
  499.9 225.7 reduce-scatter.7
  1222.3 156.9 reduce-scatter.11
  1384.6 98.3 reduce-scatter.9
where the time goes:
time: 1490 us
  waiting for transfers between devices  1360 us (91%)
  starting transfers between devices  60.5 us (4%)
  matrix products  43.3 us (3%)
    ppermute x31, waiting for transfers between devices, passed_along(): lax.ppermute(shard, axis, [(i, (i + by) % size) for i in range(size)])  395 us
    psum x1, waiting for transfers between devices, on_device(): rotated = lax.psum(partial_rot, ('group', 'half'))  275 us
    unnamed x7, waiting for transfers between devices  259 us
    reduce_scatter x1, waiting for transfers between devices, on_device(): lax.psum_scatter(lax.dot_general(scaled, basis, (((1,), (1,)), ((), ())),...  223 us
    all_gather x1, waiting for transfers between devices, on_device(): lax.all_gather(in_factors, 'dp', axis=0, tiled=True)  211 us
    ppermute x31, starting transfers between devices, passed_along(): lax.ppermute(shard, axis, [(i, (i + by) % size) for i in range(size)])  60.3 us
    dot_general x32, matrix products, absorb(): lax.dot_general(output_grads, tile_now[:, :boundary], (((1,), (1,)), ((),...  32.7 us
  transfers between devices with their start and end apart: 36, of which 36 were waited for; matrix products, arithmetic and copies ran while one was open for 0% of the time, Pallas kernels for 0%

commit v1 on v0

v1 whole, which is shorter than its diff:
```python
import jax
import jax.numpy as jnp
from jax import lax
from jax.experimental import pallas as pl
from jax.experimental.pallas import tpu as pltpu
from jax.sharding import Mesh, PartitionSpec as P

RANK = 32
DAMP = 0.01

X, ZL, ZH, Y, C = 4, 8, 2, 4, 2
BF = jnp.bfloat16
F32 = jnp.float32


def from_next(v, axis, by):
    n = lax.axis_size(axis)
    return lax.ppermute(v, axis, [(i, (i - by) % n) for i in range(n)])


def from_xor(v, axis, bit):
    return lax.ppermute(v, axis, [(i, i ^ bit) for i in range(lax.axis_size(axis))])


def scatter(v, axis):
    return lax.all_to_all(v, axis, 0, 0, tiled=True)


def gather(v, axis):
    return scatter(jnp.broadcast_to(v[None], (lax.axis_size(axis),) + v.shape), axis)


def out_kernel(pos, g_ref, o0, o1, o2, o3, out_ref, rows):
    x, zl, y, c = pos[0], pos[1], pos[2], pos[3]
    order = (0, 4, 2, 6, 1, 5, 3, 7)
    for dx, src in enumerate((o0, o1, o2, o3)):
        at_x = lax.rem(x + dx, X)
        for slot, j in enumerate(order):
            owner = jnp.bitwise_xor(zl, j)
            dy = lax.rem(lax.div(owner, 2) - y + Y, Y)
            dc = jnp.bitwise_xor(jnp.bitwise_and(owner, 1), c)
            dst = ((dc * Y + dy) * X + at_x) * RANK
            rows[pl.ds(pl.multiple_of(dst, RANK), RANK), :] = src[pl.ds(slot * RANK, RANK), :]

    @pl.loop(0, 4)
    def _(i):
        at = pl.ds(pl.multiple_of(i * 256, 256), 256)
        out_ref[at, :] = lax.dot_general(
            rows[at, :], g_ref[...], (((1,), (1,)), ((), ())), preferred_element_type=F32
        )


def output_part(pos, output_grads, blocks):
    ff = output_grads.shape[1]
    vmem = pl.BlockSpec(memory_space=pltpu.VMEM)
    return pl.pallas_call(
        out_kernel,
        out_shape=jax.ShapeDtypeStruct((1024, 256), F32),
        in_specs=[pl.BlockSpec(memory_space=pltpu.SMEM)] + [vmem] * 5,
        out_specs=vmem,
        scratch_shapes=[pltpu.VMEM((1024, ff), BF)],
        compiler_params=pltpu.CompilerParams(vmem_limit_bytes=24 * 2**20),
        cost_estimate=pl.CostEstimate(
            flops=2 * 1024 * 256 * ff, bytes_accessed=2 * 1280 * ff + 4 * 1024 * 256, transcendentals=0
        ),
    )(pos, output_grads, *blocks)


def on_device(activations, output_grads, out_factors, in_factors, basis, eigvals):
    x, zl = lax.axis_index("x"), lax.axis_index("zl")
    y, c = lax.axis_index("y"), lax.axis_index("c")

    both = jnp.concatenate([basis, activations[:, :256], activations[:, 256:]], axis=0)
    over_y = jnp.stack([both] + [from_next(both, "y", s) for s in (1, 2, 3)])
    over_c = jnp.stack([over_y, from_xor(over_y, "c", 1)])
    basis_all = over_c[:, :, :512].reshape(4096, 256)
    acts_all = over_c[:, :, 512:].reshape(16, 256, 256).transpose(1, 0, 2).reshape(256, 4096)

    f8 = scatter(gather(in_factors, "zl"), ("y", "c"))
    f_here = jnp.concatenate(
        [
            lax.dynamic_index_in_dim(f8, ((y + dy) % Y) * 2 + (c ^ dc), 0, keepdims=False)
            for dc in (0, 1)
            for dy in range(Y)
        ],
        axis=1,
    )
    f_all = gather(f_here, "x").reshape(128, 4096)
    rot = jnp.dot(f_all, basis_all, preferred_element_type=F32)
    rotated = rot + from_xor(rot, "zh", 1)
    scaled = (rotated / (eigvals + DAMP)[None, :]).astype(BF)

    pt = lax.dot_general(basis_all, scaled, (((1,), (1,)), ((), ())), preferred_element_type=F32)
    s1 = jnp.sum(scatter(pt.astype(BF).reshape(X, 1024, 128), "x").astype(F32), axis=0)
    s2 = jnp.sum(scatter(s1.astype(BF).reshape(ZL, 128, 128), "zl").astype(F32), axis=0)
    precond = gather(gather(s2.astype(BF), "zl").reshape(1024, 128), "x").reshape(4096, 128)
    input_side = jnp.dot(acts_all, precond, preferred_element_type=F32)

    o = out_factors
    for bit in (4, 2, 1):
        o = jnp.concatenate([o, from_xor(o, "zl", bit)], axis=0)
    blocks = [o] + [from_next(o, "x", s) for s in (1, 2, 3)]
    pos = jnp.stack([x, zl, y, c]).astype(jnp.int32)
    part = output_part(pos, output_grads, blocks)
    part = part[:512] + from_xor(part[512:], "c", 1)
    part = part[:128] + sum(from_next(part[s * 128:(s + 1) * 128], "y", -s) for s in (1, 2, 3))
    output_side = part + from_xor(part, "zh", 1)

    paired = input_side.T * output_side
    shares = jnp.sum(paired.reshape(X, RANK, 256), axis=1)
    pieces = shares.reshape(X, 16, 16).transpose(1, 0, 2)
    got = scatter(pieces, ("zh", "y", "c")).reshape(ZH, Y * C, X, 16)
    return jnp.sum(got, axis=0).transpose(2, 1, 0).reshape(16, X * ZL)


def solution(mesh):
    fine = Mesh(mesh.devices.reshape(X, ZL, ZH, Y, C), ("x", "zl", "zh", "y", "c"))
    dp, feats = ("x", "zl"), ("zh", "y", "c")
    return jax.shard_map(
        on_device,
        mesh=fine,
        in_specs=(P(dp, feats), P(dp, feats), P(dp, feats), P(dp, feats), P(feats, dp), P(dp)),
        out_specs=P(dp + feats, None),
        check_vma=False,
    )
```

time: 1490 us -> 249 us (0.17)
  the two profiles are of different devices: /device:TPU:2 before, /device:TPU:161 now
where the time goes in v1:
time: 249 us; the launch traced here: 247 us
  starting transfers between devices  113 us (45%)
  waiting for transfers between devices  79.4 us (32%)
  blocking collectives  23.7 us (10%)
  local copies, waits for them, and re-layouts  13.4 us (5%)
  other arithmetic  9.96 us (4%)
  matrix products  3.9 us (2%)
  Pallas kernels  3.57 us (1%)
    all_to_all x7, starting transfers between devices, scatter(): return lax.all_to_all(v, axis, 0, 0, tiled=True)  54.9 us
    ppermute x9, waiting for transfers between devices, from_next(): return lax.ppermute(v, axis, [(i, (i - by) % n) for i in range(n)])  40.2 us
    ppermute x7, starting transfers between devices, from_xor(): lax.ppermute(v, axis, [(i, i ^ bit) for i in range(lax.axis_size(axis))])  31.4 us
    ppermute x9, starting transfers between devices, from_next(): return lax.ppermute(v, axis, [(i, (i - by) % n) for i in range(n)])  26.7 us
    ppermute x7, waiting for transfers between devices, from_xor(): lax.ppermute(v, axis, [(i, i ^ bit) for i in range(lax.axis_size(axis))])  25.7 us
    all_to_all x1, blocking collectives, scatter(): return lax.all_to_all(v, axis, 0, 0, tiled=True)  23.7 us
    all_to_all x7, waiting for transfers between devices, scatter(): return lax.all_to_all(v, axis, 0, 0, tiled=True)  13.5 us
  transfers between devices with their start and end apart: 23, of which 12 were waited for; matrix products, arithmetic and copies ran while one was open for 9% of the time, Pallas kernels for 1%

profile of v1, /device:TPU:161, one launch (start us, length us, event | category | flops | bytes accessed | tf_op | source)
XLA Modules:
  0.0 247.4 jit_solution(11909462155313996143)
XLA Ops:
  0.0 1.0 fusion.5
  1.0 1.0 fusion.2
  2.0 3.2 %collective-permute-start.2 = (bf16[1024,256]{1,0:T(8,128)(2,1)S(1)}, bf16[1024,256]{1,0:T(8,128)(2,1)S(1)}, u32[]{:S(2)}, u32[]{:S(2)}) collective-permute-start(bf16[1024,256]{1,0:T(8,128)(2,1)S(1)} %get-tuple-element.13), channel_id=1, source_target_pairs={{0,2},{2,4},{4,6},{6,0},{1,3},{3,5},{5,7},{7,1},{8,10},{10,12},{12... | collective-permute-start | bytes 1572872 | tf_op jit(solution)/shard_map/ppermute | solution.py:18
  5.2 4.5 %collective-permute-start.1 = (bf16[1024,256]{1,0:T(8,128)(2,1)S(1)}, bf16[1024,256]{1,0:T(8,128)(2,1)}, u32[]{:S(2)}, u32[]{:S(2)}) collective-permute-start(bf16[1024,256]{1,0:T(8,128)(2,1)S(1)} %get-tuple-element.13), channel_id=1, source_target_pairs={{0,4},{2,6},{4,0},{6,2},{1,5},{3,7},{5,1},{7,3},{8,12},{10,14},{12... | collective-permute-start | bytes 1572872 | tf_op jit(solution)/shard_map/ppermute | solution.py:18
  9.8 3.0 %collective-permute-start = (bf16[1024,256]{1,0:T(8,128)(2,1)S(1)}, bf16[1024,256]{1,0:T(8,128)(2,1)S(1)}, u32[]{:S(2)}, u32[]{:S(2)}) collective-permute-start(bf16[1024,256]{1,0:T(8,128)(2,1)S(1)} %get-tuple-element.13), channel_id=1, source_target_pairs={{0,6},{2,0},{4,2},{6,4},{1,7},{3,1},{5,3},{7,5},{8,14},{10,8},{12,... | collective-permute-start | bytes 1572872 | tf_op jit(solution)/shard_map/ppermute | solution.py:18
  12.8 0.7 broadcast_in_dim.10
  13.5 10.3 %all-to-all-start = ((bf16[8,32,512]{2,1,0:T(8,128)(2,1)}), bf16[8,32,512]{2,1,0:T(8,128)(2,1)}, u32[]{:S(2)}, u32[]{:S(2)}) async-start(bf16[8,32,512]{2,1,0:T(8,128)(2,1)} %broadcast_in_dim.10), calls=%async_computation | async-start | bytes 524288 | tf_op jit(solution)/shard_map/all_to_all | solution.py:26
  23.8 0.0 collective-permute-done.2
  23.8 6.7 %collective-permute-done.1 = bf16[1024,256]{1,0:T(8,128)(2,1)} collective-permute-done((bf16[1024,256]{1,0:T(8,128)(2,1)S(1)}, bf16[1024,256]{1,0:T(8,128)(2,1)}, u32[]{:S(2)}, u32[]{:S(2)}) %collective-permute-start.1) | collective-permute-done | bytes 524320 | tf_op jit(solution)/shard_map/ppermute | solution.py:18
  30.5 1.3 collective-permute-done
  31.8 0.8 copy-done.5
  32.6 2.9 %pad_maximum_fusion.1 = (bf16[4,1024,256]{2,1,0:T(8,128)(2,1)S(1)}, bf16[1,4,1024,256]{3,2,1,0:T(8,128)(2,1)}) fusion(bf16[1,1024,256]{2,1,0:T(8,128)(2,1)S(1)} %bitcast.57, bf16[1,1024,256]{2,1,0:T(8,128)(2,1)} %bitcast.2, bf16[1,1024,256]{2,1,0:T(8,128)(2,1)} %bitcast.58, bf16[1,1024,256]{2,1,0:T(8,128)(2,1)S(1)} %get-tuple-element.12), kind=kLoop, calls=%fused_computation.5 | loop fusion | flops 3145728 | bytes 6291456 | tf_op jit(solution)/shard_map/stack | solution.py:74
  35.4 3.5 %collective-permute-start.3 = (bf16[4,1024,256]{2,1,0:T(8,128)(2,1)S(1)}, bf16[4,1024,256]{2,1,0:T(8,128)(2,1)}, u32[]{:S(2)}, u32[]{:S(2)}) collective-permute-start(bf16[4,1024,256]{2,1,0:T(8,128)(2,1)S(1)} %get-tuple-element.7), channel_id=1, source_target_pairs={{0,1},{1,0},{2,3},{3,2},{4,5},{5,4},{6,7},{7,6},{8,9},{9,8},{10,11... | collective-permute-start | bytes 6291464 | tf_op jit(solution)/shard_map/ppermute | solution.py:22
  38.9 4.5 %all-to-all-start.1 = ((bf16[8,32,512]{2,1,0:T(8,128)(2,1)}), bf16[8,32,512]{2,1,0:T(8,128)(2,1)S(1)}, u32[]{:S(2)}, u32[]{:S(2)}) async-start(bf16[8,32,512]{2,1,0:T(8,128)(2,1)} %all-to-all-done), calls=%async_computation.1 | async-start | bytes 524288 | tf_op jit(solution)/shard_map/all_to_all | solution.py:26
  43.4 6.5 %all-to-all-done.1 = bf16[8,32,512]{2,1,0:T(8,128)(2,1)S(1)} async-done(((bf16[8,32,512]{2,1,0:T(8,128)(2,1)}), bf16[8,32,512]{2,1,0:T(8,128)(2,1)S(1)}, u32[]{:S(2)}, u32[]{:S(2)}) %all-to-all-start.1) | async-done | bytes 262176 | tf_op jit(solution)/shard_map/all_to_all | solution.py:26
  50.0 1.1 broadcast_in_dim.11
  51.1 4.0 %all-to-all-start.2 = ((bf16[4,32,4096]{2,1,0:T(8,128)(2,1)}), bf16[4,32,4096]{2,1,0:T(8,128)(2,1)S(1)}, u32[]{:S(2)}, u32[]{:S(2)}) async-start(bf16[4,32,4096]{2,1,0:T(8,128)(2,1)} %broadcast_in_dim.11), calls=%async_computation.2 | async-start | bytes 2097152 | tf_op jit(solution)/shard_map/all_to_all | solution.py:26
  55.1 3.5 %collective-permute-start.5 = (bf16[32,1792]{1,0:T(8,128)(2,1)S(1)}, bf16[32,1792]{1,0:T(8,128)(2,1)S(1)}, u32[]{:S(2)}, u32[]{:S(2)}) collective-permute-start(bf16[32,1792]{1,0:T(8,128)(2,1)S(1)} %copy-done.3), channel_id=1, source_target_pairs={{0,64},{16,80},{32,96},{48,112},{64,0},{80,16},{96,32},{112,48},{1... | collective-permute-start | bytes 344072 | tf_op jit(solution)/shard_map/ppermute | solution.py:22
  58.6 3.3 %pad_maximum_fusion = (bf16[2,4,512,256]{3,2,1,0:T(8,128)(2,1)}, bf16[2,4,512,256]{3,2,1,0:T(8,128)(2,1)S(1)}) fusion(bf16[1,4,1024,256]{3,2,1,0:T(8,128)(2,1)} %bitcast.5, bf16[1,4,1024,256]{3,2,1,0:T(8,128)(2,1)} %get-tuple-element.8), kind=kLoop, calls=%fused_computation.4 | loop fusion | flops 8388608 | bytes 8388608 | tf_op jit(solution)/shard_map/stack | solution.py:75
  62.0 7.0 %all-to-all-done.2 = bf16[4,32,4096]{2,1,0:T(8,128)(2,1)S(1)} async-done(((bf16[4,32,4096]{2,1,0:T(8,128)(2,1)}), bf16[4,32,4096]{2,1,0:T(8,128)(2,1)S(1)}, u32[]{:S(2)}, u32[]{:S(2)}) %all-to-all-start.2) | async-done | bytes 1048608 | tf_op jit(solution)/shard_map/all_to_all | solution.py:26
  68.9 0.4 fusion.6
  69.4 9.7 %collective-permute-start.4 = (f32[128,256]{1,0:T(8,128)S(1)}, f32[128,256]{1,0:T(8,128)S(1)}, u32[]{:S(2)}, u32[]{:S(2)}) collective-permute-start(f32[128,256]{1,0:T(8,128)S(1)} %fusion.6), channel_id=1, source_target_pairs={{0,8},{8,0},{1,9},{9,1},{2,10},{10,2},{3,11},{11,3},{4,12},{12,4},... | collective-permute-start | bytes 393224 | tf_op jit(solution)/shard_map/ppermute | solution.py:22
  79.1 0.0 collective-permute-done.5
  79.1 0.7 pad_maximum_fusion.4
  79.8 3.1 %collective-permute-start.6 = (bf16[64,1792]{1,0:T(8,128)(2,1)}, bf16[64,1792]{1,0:T(8,128)(2,1)S(1)}, u32[]{:S(2)}, u32[]{:S(2)}) collective-permute-start(bf16[64,1792]{1,0:T(8,128)(2,1)} %pad_maximum_fusion.4), channel_id=1, source_target_pairs={{0,32},{16,48},{32,0},{48,16},{64,96},{80,112},{96,64},{112,80},{1... | collective-permute-start | bytes 688136 | tf_op jit(solution)/shard_map/ppermute | solution.py:22
  82.9 6.1 %collective-permute-done.4 = f32[128,256]{1,0:T(8,128)S(1)} collective-permute-done((f32[128,256]{1,0:T(8,128)S(1)}, f32[128,256]{1,0:T(8,128)S(1)}, u32[]{:S(2)}, u32[]{:S(2)}) %collective-permute-start.4) | collective-permute-done | bytes 131104 | tf_op jit(solution)/shard_map/ppermute | solution.py:22
  89.0 1.7 convolution_convert_fusion
  90.7 3.5 %all-to-all-start.3 = ((bf16[4,1024,128]{2,1,0:T(8,128)(2,1)}), bf16[4,1024,128]{2,1,0:T(8,128)(2,1)S(1)}, u32[]{:S(2)}, u32[]{:S(2)}) async-start(bf16[4,1024,128]{2,1,0:T(8,128)(2,1)} %bitcast.16), calls=%async_computation.3 | async-start | bytes 2097152 | tf_op jit(solution)/shard_map/all_to_all | solution.py:26
  94.2 7.6 %collective-permute-done.6 = bf16[64,1792]{1,0:T(8,128)(2,1)S(1)} collective-permute-done((bf16[64,1792]{1,0:T(8,128)(2,1)}, bf16[64,1792]{1,0:T(8,128)(2,1)S(1)}, u32[]{:S(2)}, u32[]{:S(2)}) %collective-permute-start.6) | collective-permute-done | bytes 229408 | tf_op jit(solution)/shard_map/ppermute | solution.py:22
  101.8 0.9 pad_maximum_fusion.3
  102.7 1.9 collective-permute-start.7
  104.6 0.0 copy-start
  104.7 0.9 reduce_sum.42
  105.6 16.9 %all-to-all-start.4 = ((bf16[8,128,128]{2,1,0:T(8,128)(2,1)}), bf16[8,128,128]{2,1,0:T(8,128)(2,1)S(1)}, u32[]{:S(2)}, u32[]{:S(2)}) async-start(bf16[8,128,128]{2,1,0:T(8,128)(2,1)} %bitcast.17), calls=%async_computation.4 | async-start | bytes 524288 | tf_op jit(solution)/shard_map/all_to_all | solution.py:26
  122.5 1.0 constant_dynamic-update-slice_fusion.1
  123.5 1.1 constant_dynamic-update-slice_fusion.o0
  124.5 2.8 %collective-permute-start.8 = (bf16[256,1792]{1,0:T(8,128)(2,1)S(1)}, bf16[256,1792]{1,0:T(8,128)(2,1)S(1)}, u32[]{:S(2)}, u32[]{:S(2)}) collective-permute-start(bf16[256,1792]{1,0:T(8,128)(2,1)S(1)} %constant_dynamic-update-slice_fusion.o0), channel_id=1, source_target_pairs={{0,384},{128,0},{256,128},{384,256},{1,385},{129,1},{257,129},{385... | collective-permute-start | bytes 2752520 | tf_op jit(solution)/shard_map/ppermute | solution.py:18
  127.3 3.1 %collective-permute-start.9 = (bf16[256,1792]{1,0:T(8,128)(2,1)S(1)}, bf16[256,1792]{1,0:T(8,128)(2,1)}, u32[]{:S(2)}, u32[]{:S(2)}) collective-permute-start(bf16[256,1792]{1,0:T(8,128)(2,1)S(1)} %constant_dynamic-update-slice_fusion.o0), channel_id=1, source_target_pairs={{0,256},{128,384},{256,0},{384,128},{1,257},{129,385},{257,1},{385... | collective-permute-start | bytes 2752520 | tf_op jit(solution)/shard_map/ppermute | solution.py:18
  130.4 1.9 collective-permute-start.10
  132.4 0.7 broadcast_in_dim.12
  133.2 11.4 %all-to-all-start.5 = ((bf16[8,128,128]{2,1,0:T(8,128)(2,1)}), bf16[8,128,128]{2,1,0:T(8,128)(2,1)S(1)}, u32[]{:S(2)}, u32[]{:S(2)}) async-start(bf16[8,128,128]{2,1,0:T(8,128)(2,1)} %broadcast_in_dim.12), calls=%async_computation.5 | async-start | bytes 524288 | tf_op jit(solution)/shard_map/all_to_all | solution.py:26
  144.6 0.1 pad_add_fusion.pos
  144.7 1.5 collective-permute-done.8.o1
  146.2 0.9 copy-done.1
  147.1 3.1 %collective-permute-done.9.o2 = bf16[256,1792]{1,0:T(8,128)(2,1)} collective-permute-done((bf16[256,1792]{1,0:T(8,128)(2,1)S(1)}, bf16[256,1792]{1,0:T(8,128)(2,1)}, u32[]{:S(2)}, u32[]{:S(2)}) %collective-permute-start.9) | collective-permute-done | bytes 917536 | tf_op jit(solution)/shard_map/ppermute | solution.py:18
  150.3 22.5 %collective-permute-done.10.o3 = bf16[256,1792]{1,0:T(8,128)(2,1)} collective-permute-done((bf16[256,1792]{1,0:T(8,128)(2,1)S(1)}, bf16[256,1792]{1,0:T(8,128)(2,1)}, u32[]{:S(2)}, u32[]{:S(2)}) %collective-permute-start.10) | collective-permute-done | bytes 917536 | tf_op jit(solution)/shard_map/ppermute | solution.py:18
  172.8 1.2 copy-done.2
  173.9 3.6 %shard_map.64 = f32[1024,256]{1,0:T(8,128)S(1)} custom-call(s32[4]{0:T(128)S(1)} %pad_add_fusion.pos, bf16[256,1792]{1,0:T(8,128)(2,1)S(1)} %copy-done, bf16[256,1792]{1,0:T(8,128)(2,1)S(1)} %constant_dynamic-update-slice_fusion.o0, bf16[256,1792]{1,0:T(8,128)(2,1)S(1)} %copy-done.2, bf16[256,1792]{1,0:T(8,128)(2,1)} %collective-permute-done.9.o2, ...), custom_call_target="tpu_custom_call" | custom-call | flops 939524096 | bytes 5636096 | tf_op jit(solution)/shard_map/pallas_call | solution.py:56
  177.6 2.4 collective-permute-start.11
  180.0 1.1 broadcast_in_dim.14
  181.1 4.2 %all-to-all-start.6 = ((bf16[4,1024,128]{2,1,0:T(8,128)(2,1)}), bf16[4,1024,128]{2,1,0:T(8,128)(2,1)}, u32[]{:S(2)}, u32[]{:S(2)}) async-start(bf16[4,1024,128]{2,1,0:T(8,128)(2,1)} %broadcast_in_dim.14), calls=%async_computation.6 | async-start | bytes 2097152 | tf_op jit(solution)/shard_map/all_to_all | solution.py:26
  185.3 0.1 slice_add_fusion
  185.5 2.8 %collective-permute-start.14 = (f32[128,256]{1,0:T(8,128)S(1)}, f32[128,256]{1,0:T(8,128)S(1)}, u32[]{:S(2)}, u32[]{:S(2)}) collective-permute-start(f32[128,256]{1,0:T(8,128)S(1)} %get-tuple-element.10), channel_id=1, source_target_pairs={{0,6},{2,0},{4,2},{6,4},{1,7},{3,1},{5,3},{7,5},{8,14},{10,8},{12,... | collective-permute-start | bytes 393224 | tf_op jit(solution)/shard_map/ppermute | solution.py:18
  188.3 2.5 collective-permute-start.12
  190.8 2.9 %collective-permute-start.13 = (f32[128,256]{1,0:T(8,128)S(1)}, f32[128,256]{1,0:T(8,128)S(1)}, u32[]{:S(2)}, u32[]{:S(2)}) collective-permute-start(f32[128,256]{1,0:T(8,128)S(1)} %get-tuple-element.9), channel_id=1, source_target_pairs={{0,4},{2,6},{4,0},{6,2},{1,5},{3,7},{5,1},{7,3},{8,12},{10,14},{12... | collective-permute-start | bytes 393224 | tf_op jit(solution)/shard_map/ppermute | solution.py:18
  193.7 2.6 %collective-permute-done.12 = f32[128,256]{1,0:T(8,128)S(1)} collective-permute-done((f32[128,256]{1,0:T(8,128)S(1)}, f32[128,256]{1,0:T(8,128)S(1)}, u32[]{:S(2)}, u32[]{:S(2)}) %collective-permute-start.12) | collective-permute-done | bytes 131104 | tf_op jit(solution)/shard_map/ppermute | solution.py:18
  196.3 2.5 collective-permute-done.13
  198.8 7.3 %collective-permute-start.15 = (f32[128,256]{1,0:T(8,128)S(1)}, f32[128,256]{1,0:T(8,128)S(1)}, u32[]{:S(2)}, u32[]{:S(2)}) collective-permute-start(f32[128,256]{1,0:T(8,128)S(1)} %slice_add_fusion.1), channel_id=1, source_target_pairs={{0,8},{8,0},{1,9},{9,1},{2,10},{10,2},{3,11},{11,3},{4,12},{12,4},... | collective-permute-start | bytes 393224 | tf_op jit(solution)/shard_map/ppermute | solution.py:22
  206.1 2.9 %copy.19 = bf16[256,16,256]{0,2,1:T(8,128)(2,1)S(1)} copy(bf16[256,16,256]{2,0,1:T(8,128)(2,1)} %bitcast.54) | data formatting | bytes 4194304 | tf_op jit(solution)/shard_map/transpose | solution.py:77
  209.0 1.7 fusion.7
  210.7 12.1 %collective-permute-done.15 = f32[128,256]{1,0:T(8,128)S(1)} collective-permute-done((f32[128,256]{1,0:T(8,128)S(1)}, f32[128,256]{1,0:T(8,128)S(1)}, u32[]{:S(2)}, u32[]{:S(2)}) %collective-permute-start.15) | collective-permute-done | bytes 131104 | tf_op jit(solution)/shard_map/ppermute | solution.py:22
  222.9 0.1 reshape.46
  223.0 23.7 %all_to_all.40 = f32[16,4,16]{2,1,0:T(4,128)S(1)} all-to-all(f32[16,4,16]{2,1,0:T(4,128)S(1)} %copy.20), channel_id=1, replica_groups=mesh['x'=4,'zl'=8,'zh'=2,'y'=4,'c'=2] {'zh','y','c'}, dimensions={0} | all-to-all | bytes 8192 | tf_op jit(solution)/shard_map/all_to_all | solution.py:26
  246.7 0.7 copy.22
  (40 shorter events, 0.4 us)
Async XLA Ops:
  0.0 12.8 %copy-start.6 = (bf16[32,512]{1,0:T(8,128)(2,1)S(1)}, bf16[32,512]{1,0:T(8,128)(2,1)}, u32[]{:S(2)}) copy-start(bf16[32,512]{1,0:T(8,128)(2,1)} %param.9) | copy-start | bytes 98308
  2.0 21.7 %collective-permute-start.2 = (bf16[1024,256]{1,0:T(8,128)(2,1)S(1)}, bf16[1024,256]{1,0:T(8,128)(2,1)S(1)}, u32[]{:S(2)}, u32[]{:S(2)}) collective-permute-start(bf16[1024,256]{1,0:T(8,128)(2,1)S(1)} %get-tuple-element.13), channel_id=1, source_target_pairs={{0,2},{2,4},{4,6},{6,0},{1,3},{3,5},{5,7},{7,1},{8,10},{10,12},{12... | collective-permute-start | bytes 1572872 | tf_op jit(solution)/shard_map/ppermute | solution.py:18
  5.2 25.3 %collective-permute-start.1 = (bf16[1024,256]{1,0:T(8,128)(2,1)S(1)}, bf16[1024,256]{1,0:T(8,128)(2,1)}, u32[]{:S(2)}, u32[]{:S(2)}) collective-permute-start(bf16[1024,256]{1,0:T(8,128)(2,1)S(1)} %get-tuple-element.13), channel_id=1, source_target_pairs={{0,4},{2,6},{4,0},{6,2},{1,5},{3,7},{5,1},{7,3},{8,12},{10,14},{12... | collective-permute-start | bytes 1572872 | tf_op jit(solution)/shard_map/ppermute | solution.py:18
  9.8 22.0 %collective-permute-start = (bf16[1024,256]{1,0:T(8,128)(2,1)S(1)}, bf16[1024,256]{1,0:T(8,128)(2,1)S(1)}, u32[]{:S(2)}, u32[]{:S(2)}) collective-permute-start(bf16[1024,256]{1,0:T(8,128)(2,1)S(1)} %get-tuple-element.13), channel_id=1, source_target_pairs={{0,6},{2,0},{4,2},{6,4},{1,7},{3,1},{5,3},{7,5},{8,14},{10,8},{12,... | collective-permute-start | bytes 1572872 | tf_op jit(solution)/shard_map/ppermute | solution.py:18
  13.5 25.4 %all-to-all-start = ((bf16[8,32,512]{2,1,0:T(8,128)(2,1)}), bf16[8,32,512]{2,1,0:T(8,128)(2,1)}, u32[]{:S(2)}, u32[]{:S(2)}) async-start(bf16[8,32,512]{2,1,0:T(8,128)(2,1)} %broadcast_in_dim.10), calls=%async_computation | async-start | bytes 524288 | tf_op jit(solution)/shard_map/all_to_all | solution.py:26
  31.8 0.8 copy-start.5
  35.4 23.2 %collective-permute-start.3 = (bf16[4,1024,256]{2,1,0:T(8,128)(2,1)S(1)}, bf16[4,1024,256]{2,1,0:T(8,128)(2,1)}, u32[]{:S(2)}, u32[]{:S(2)}) collective-permute-start(bf16[4,1024,256]{2,1,0:T(8,128)(2,1)S(1)} %get-tuple-element.7), channel_id=1, source_target_pairs={{0,1},{1,0},{2,3},{3,2},{4,5},{5,4},{6,7},{7,6},{8,9},{9,8},{10,11... | collective-permute-start | bytes 6291464 | tf_op jit(solution)/shard_map/ppermute | solution.py:22
  38.9 11.0 %all-to-all-start.1 = ((bf16[8,32,512]{2,1,0:T(8,128)(2,1)}), bf16[8,32,512]{2,1,0:T(8,128)(2,1)S(1)}, u32[]{:S(2)}, u32[]{:S(2)}) async-start(bf16[8,32,512]{2,1,0:T(8,128)(2,1)} %all-to-all-done), calls=%async_computation.1 | async-start | bytes 524288 | tf_op jit(solution)/shard_map/all_to_all | solution.py:26
  43.4 11.7 %copy-start.3 = (bf16[32,1792]{1,0:T(8,128)(2,1)S(1)}, bf16[32,1792]{1,0:T(8,128)(2,1)}, u32[]{:S(2)}) copy-start(bf16[32,1792]{1,0:T(8,128)(2,1)} %param.8) | copy-start | bytes 344068
  43.4 15.2 %copy-start.7 = (f32[256]{0:T(256)S(1)}, f32[256]{0:T(256)}, u32[]{:S(2)}) copy-start(f32[256]{0:T(256)} %param.11) | copy-start | bytes 3076
  51.1 17.8 %all-to-all-start.2 = ((bf16[4,32,4096]{2,1,0:T(8,128)(2,1)}), bf16[4,32,4096]{2,1,0:T(8,128)(2,1)S(1)}, u32[]{:S(2)}, u32[]{:S(2)}) async-start(bf16[4,32,4096]{2,1,0:T(8,128)(2,1)} %broadcast_in_dim.11), calls=%async_computation.2 | async-start | bytes 2097152 | tf_op jit(solution)/shard_map/all_to_all | solution.py:26
  55.1 24.0 %collective-permute-start.5 = (bf16[32,1792]{1,0:T(8,128)(2,1)S(1)}, bf16[32,1792]{1,0:T(8,128)(2,1)S(1)}, u32[]{:S(2)}, u32[]{:S(2)}) collective-permute-start(bf16[32,1792]{1,0:T(8,128)(2,1)S(1)} %copy-done.3), channel_id=1, source_target_pairs={{0,64},{16,80},{32,96},{48,112},{64,0},{80,16},{96,32},{112,48},{1... | collective-permute-start | bytes 344072 | tf_op jit(solution)/shard_map/ppermute | solution.py:22
  69.4 19.6 %collective-permute-start.4 = (f32[128,256]{1,0:T(8,128)S(1)}, f32[128,256]{1,0:T(8,128)S(1)}, u32[]{:S(2)}, u32[]{:S(2)}) collective-permute-start(f32[128,256]{1,0:T(8,128)S(1)} %fusion.6), channel_id=1, source_target_pairs={{0,8},{8,0},{1,9},{9,1},{2,10},{10,2},{3,11},{11,3},{4,12},{12,4},... | collective-permute-start | bytes 393224 | tf_op jit(solution)/shard_map/ppermute | solution.py:22
  79.8 22.0 %collective-permute-start.6 = (bf16[64,1792]{1,0:T(8,128)(2,1)}, bf16[64,1792]{1,0:T(8,128)(2,1)S(1)}, u32[]{:S(2)}, u32[]{:S(2)}) collective-permute-start(bf16[64,1792]{1,0:T(8,128)(2,1)} %pad_maximum_fusion.4), channel_id=1, source_target_pairs={{0,32},{16,48},{32,0},{48,16},{64,96},{80,112},{96,64},{112,80},{1... | collective-permute-start | bytes 688136 | tf_op jit(solution)/shard_map/ppermute | solution.py:22
  90.7 13.9 %all-to-all-start.3 = ((bf16[4,1024,128]{2,1,0:T(8,128)(2,1)}), bf16[4,1024,128]{2,1,0:T(8,128)(2,1)S(1)}, u32[]{:S(2)}, u32[]{:S(2)}) async-start(bf16[4,1024,128]{2,1,0:T(8,128)(2,1)} %bitcast.16), calls=%async_computation.3 | async-start | bytes 2097152 | tf_op jit(solution)/shard_map/all_to_all | solution.py:26
  101.8 3.8 %copy-start.4 = (bf16[64,1792]{1,0:T(8,128)(2,1)}, bf16[64,1792]{1,0:T(8,128)(2,1)S(1)}, u32[]{:S(2)}) copy-start(bf16[64,1792]{1,0:T(8,128)(2,1)S(1)} %collective-permute-done.6) | copy-start | bytes 688132
  102.7 20.8 %collective-permute-start.7 = (bf16[128,1792]{1,0:T(8,128)(2,1)}, bf16[128,1792]{1,0:T(8,128)(2,1)}, u32[]{:S(2)}, u32[]{:S(2)}) collective-permute-start(bf16[128,1792]{1,0:T(8,128)(2,1)} %pad_maximum_fusion.3), channel_id=1, source_target_pairs={{0,16},{16,0},{32,48},{48,32},{64,80},{80,64},{96,112},{112,96},{1... | collective-permute-start | bytes 1376264 | tf_op jit(solution)/shard_map/ppermute | solution.py:22
  104.6 68.1 %copy-start = (bf16[256,1792]{1,0:T(8,128)(2,1)S(1)}, bf16[256,1792]{1,0:T(8,128)(2,1)}, u32[]{:S(2)}) copy-start(bf16[256,1792]{1,0:T(8,128)(2,1)} %g_ref.1) | copy-start | bytes 2752516
  105.6 26.8 %all-to-all-start.4 = ((bf16[8,128,128]{2,1,0:T(8,128)(2,1)}), bf16[8,128,128]{2,1,0:T(8,128)(2,1)S(1)}, u32[]{:S(2)}, u32[]{:S(2)}) async-start(bf16[8,128,128]{2,1,0:T(8,128)(2,1)} %bitcast.17), calls=%async_computation.4 | async-start | bytes 524288 | tf_op jit(solution)/shard_map/all_to_all | solution.py:26
  124.5 21.7 %collective-permute-start.8 = (bf16[256,1792]{1,0:T(8,128)(2,1)S(1)}, bf16[256,1792]{1,0:T(8,128)(2,1)S(1)}, u32[]{:S(2)}, u32[]{:S(2)}) collective-permute-start(bf16[256,1792]{1,0:T(8,128)(2,1)S(1)} %constant_dynamic-update-slice_fusion.o0), channel_id=1, source_target_pairs={{0,384},{128,0},{256,128},{384,256},{1,385},{129,1},{257,129},{385... | collective-permute-start | bytes 2752520 | tf_op jit(solution)/shard_map/ppermute | solution.py:18
  127.3 22.9 %collective-permute-start.9 = (bf16[256,1792]{1,0:T(8,128)(2,1)S(1)}, bf16[256,1792]{1,0:T(8,128)(2,1)}, u32[]{:S(2)}, u32[]{:S(2)}) collective-permute-start(bf16[256,1792]{1,0:T(8,128)(2,1)S(1)} %constant_dynamic-update-slice_fusion.o0), channel_id=1, source_target_pairs={{0,256},{128,384},{256,0},{384,128},{1,257},{129,385},{257,1},{385... | collective-permute-start | bytes 2752520 | tf_op jit(solution)/shard_map/ppermute | solution.py:18
  130.4 42.3 %collective-permute-start.10 = (bf16[256,1792]{1,0:T(8,128)(2,1)S(1)}, bf16[256,1792]{1,0:T(8,128)(2,1)}, u32[]{:S(2)}, u32[]{:S(2)}) collective-permute-start(bf16[256,1792]{1,0:T(8,128)(2,1)S(1)} %constant_dynamic-update-slice_fusion.o0), channel_id=1, source_target_pairs={{0,128},{128,256},{256,384},{384,0},{1,129},{129,257},{257,385},{3... | collective-permute-start | bytes 2752520 | tf_op jit(solution)/shard_map/ppermute | solution.py:18
  133.2 46.8 %all-to-all-start.5 = ((bf16[8,128,128]{2,1,0:T(8,128)(2,1)}), bf16[8,128,128]{2,1,0:T(8,128)(2,1)S(1)}, u32[]{:S(2)}, u32[]{:S(2)}) async-start(bf16[8,128,128]{2,1,0:T(8,128)(2,1)} %broadcast_in_dim.12), calls=%async_computation.5 | async-start | bytes 524288 | tf_op jit(solution)/shard_map/all_to_all | solution.py:26
  146.2 0.9 copy-start.1
  172.8 1.2 copy-start.2
  177.6 7.8 %collective-permute-start.11 = (f32[512,256]{1,0:T(8,128)S(1)}, f32[512,256]{1,0:T(8,128)S(1)}, u32[]{:S(2)}, u32[]{:S(2)}) collective-permute-start(f32[512,256]{1,0:T(8,128)S(1)} %slice.43), channel_id=1, source_target_pairs={{0,1},{1,0},{2,3},{3,2},{4,5},{5,4},{6,7},{7,6},{8,9},{9,8},{10,11... | collective-permute-start | bytes 1572872 | tf_op jit(solution)/shard_map/ppermute | solution.py:22
  181.1 27.9 %all-to-all-start.6 = ((bf16[4,1024,128]{2,1,0:T(8,128)(2,1)}), bf16[4,1024,128]{2,1,0:T(8,128)(2,1)}, u32[]{:S(2)}, u32[]{:S(2)}) async-start(bf16[4,1024,128]{2,1,0:T(8,128)(2,1)} %broadcast_in_dim.14), calls=%async_computation.6 | async-start | bytes 2097152 | tf_op jit(solution)/shard_map/all_to_all | solution.py:26
  185.5 8.2 %collective-permute-start.14 = (f32[128,256]{1,0:T(8,128)S(1)}, f32[128,256]{1,0:T(8,128)S(1)}, u32[]{:S(2)}, u32[]{:S(2)}) collective-permute-start(f32[128,256]{1,0:T(8,128)S(1)} %get-tuple-element.10), channel_id=1, source_target_pairs={{0,6},{2,0},{4,2},{6,4},{1,7},{3,1},{5,3},{7,5},{8,14},{10,8},{12,... | collective-permute-start | bytes 393224 | tf_op jit(solution)/shard_map/ppermute | solution.py:18
  188.3 8.0 %collective-permute-start.12 = (f32[128,256]{1,0:T(8,128)S(1)}, f32[128,256]{1,0:T(8,128)S(1)}, u32[]{:S(2)}, u32[]{:S(2)}) collective-permute-start(f32[128,256]{1,0:T(8,128)S(1)} %get-tuple-element.11), channel_id=1, source_target_pairs={{0,2},{2,4},{4,6},{6,0},{1,3},{3,5},{5,7},{7,1},{8,10},{10,12},{12... | collective-permute-start | bytes 393224 | tf_op jit(solution)/shard_map/ppermute | solution.py:18
  190.8 8.0 %collective-permute-start.13 = (f32[128,256]{1,0:T(8,128)S(1)}, f32[128,256]{1,0:T(8,128)S(1)}, u32[]{:S(2)}, u32[]{:S(2)}) collective-permute-start(f32[128,256]{1,0:T(8,128)S(1)} %get-tuple-element.9), channel_id=1, source_target_pairs={{0,4},{2,6},{4,0},{6,2},{1,5},{3,7},{5,1},{7,3},{8,12},{10,14},{12... | collective-permute-start | bytes 393224 | tf_op jit(solution)/shard_map/ppermute | solution.py:18
  198.8 24.1 %collective-permute-start.15 = (f32[128,256]{1,0:T(8,128)S(1)}, f32[128,256]{1,0:T(8,128)S(1)}, u32[]{:S(2)}, u32[]{:S(2)}) collective-permute-start(f32[128,256]{1,0:T(8,128)S(1)} %slice_add_fusion.1), channel_id=1, source_target_pairs={{0,8},{8,0},{1,9},{9,1},{2,10},{10,2},{3,11},{11,3},{4,12},{12,4},... | collective-permute-start | bytes 393224 | tf_op jit(solution)/shard_map/ppermute | solution.py:22

commit v2 on v1

v2 whole, which is shorter than its diff:
```python
import jax
import jax.numpy as jnp
from jax import lax
from jax.experimental import pallas as pl
from jax.experimental.pallas import tpu as pltpu
from jax.sharding import Mesh, PartitionSpec as P

RANK = 32
DAMP = 0.01

X, ZL, ZH, Y, C = 4, 8, 2, 4, 2
BF = jnp.bfloat16
F32 = jnp.float32
KB = RANK // (Y * C)
XOR_ORDER = (0, 4, 2, 6, 1, 5, 3, 7)
VMEM = pl.BlockSpec(memory_space=pltpu.VMEM)
SMEM = pl.BlockSpec(memory_space=pltpu.SMEM)


def swap(v, axis, partner):
    return lax.ppermute(v, axis, [(i, partner(i)) for i in range(lax.axis_size(axis))])


def scatter(v, axis):
    return lax.all_to_all(v, axis, 0, 0, tiled=True)


def gather(v, axis):
    return scatter(jnp.broadcast_to(v[None], (lax.axis_size(axis),) + v.shape), axis)


def after(v, *others):
    return lax.optimization_barrier((v,) + others)[0]


def call(kernel, out, args, specs, flops, scratch=(), limit=24):
    many = isinstance(out, list)
    moved = sum(a.size * a.dtype.itemsize for a in args)
    return pl.pallas_call(
        kernel,
        out_shape=out,
        in_specs=specs,
        out_specs=[VMEM] * len(out) if many else VMEM,
        scratch_shapes=scratch,
        compiler_params=pltpu.CompilerParams(vmem_limit_bytes=limit * 2**20),
        cost_estimate=pl.CostEstimate(flops=flops, bytes_accessed=moved, transcendentals=0),
    )(*args)


def rotate_kernel(f, basis, rot):
    rows = jnp.concatenate(
        [jnp.concatenate([f[zl * Y * C + s] for zl in range(ZL)], axis=0) for s in range(Y * C)], axis=1
    )
    for i in range(X):
        for h in range(2):
            at = (i * 2 + h) * 128
            b = jnp.concatenate([basis[s, at:at + 128, :] for s in range(Y * C)], axis=0)
            rot[i, :, h * 128:(h + 1) * 128] = jnp.dot(rows, b, preferred_element_type=F32)


def precond_kernel(scaled, basis, pt):
    eigs = jnp.concatenate([scaled[i] for i in range(X)], axis=1)
    for s in range(Y * C):
        b = jnp.concatenate([basis[s, j * 128:(j + 1) * 128, :] for j in range(2 * X)], axis=1)
        pt[s] = lax.dot_general(b, eigs, (((1,), (1,)), ((), ())), preferred_element_type=F32).astype(BF)


def input_kernel(acts, pt, ins):
    p = jnp.concatenate([pt[s] for s in range(Y * C)], axis=0)
    for i in range(X):
        a = jnp.concatenate([acts[s, i * 256:(i + 1) * 256, :] for s in range(Y * C)], axis=1)
        ins[i] = jnp.dot(a, p, preferred_element_type=F32)


def output_kernel(pos, g0, g1, o0, o1, part, rows):
    for dx, held in enumerate((o0, o1)):
        low = jnp.bitwise_and(jnp.bitwise_xor(pos[0], dx), 1)
        for slot, j in enumerate(XOR_ORDER):
            dst = (jnp.bitwise_xor(pos[4], j) * 2 + low) * RANK
            rows[pl.ds(pl.multiple_of(dst, RANK), RANK), :] = held[slot * RANK:(slot + 1) * RANK, :]
    for i, g in enumerate((g0, g1)):
        both = lax.dot_general(rows[...], g[...], (((1,), (1,)), ((), ())), preferred_element_type=F32)
        for b in range(Y * C):
            dc = jnp.bitwise_xor(pos[3], b % C)
            dy = lax.rem(b // C - pos[2] + Y, Y)
            for q in range(2 * ZL):
                src = q * RANK + b * KB
                part[dc * Y + dy, q * KB:(q + 1) * KB, i * 256:(i + 1) * 256] = both[src:src + KB, :]


def sides_kernel(pos, parts, out_own, out_partner, keep, send):
    ins = (parts[0] + parts[1] + parts[2] + parts[3]).T
    a, b = out_own[...], out_partner[...]
    low_x = pos[0] < 2
    low, high = jnp.where(low_x, a, b), jnp.where(low_x, b, a)
    n = 2 * KB
    outs = jnp.concatenate(
        [v[zl * n:(zl + 1) * n, :] for zl in range(ZL) for v in (low, high)], axis=0
    )
    first = pos[1] == 0
    for i, v in enumerate((ins, outs)):
        keep[i] = jnp.where(first, v[:, :128], v[:, 128:])
        send[i] = jnp.where(first, v[:, 128:], v[:, :128])


def from_next(v, axis, by):
    n = lax.axis_size(axis)
    return lax.ppermute(v, axis, [(i, (i - by) % n) for i in range(n)])


def on_device(activations, output_grads, out_factors, in_factors, basis, eigvals):
    x, zl, zh = lax.axis_index("x"), lax.axis_index("zl"), lax.axis_index("zh")
    pos = jnp.stack([x, zh, lax.axis_index("y"), lax.axis_index("c"), zl])
    ff = output_grads.shape[1]

    mix = jnp.concatenate(
        [
            in_factors.reshape(RANK, X, 128).transpose(1, 0, 2),
            activations.reshape(256, X, 128).transpose(1, 0, 2),
            basis.reshape(X, 128, 2, 128).transpose(0, 2, 1, 3).reshape(X, 256, 128),
        ],
        axis=1,
    )
    mix = scatter(mix, "x")
    basis_all = lax.all_gather(mix[:, 288:].reshape(1024, 128), ("y", "c"))
    acts_all = lax.all_gather(mix[:, 32:288].reshape(1024, 128), ("y", "c"))
    o_in = swap(out_factors, "zl", lambda i: i ^ 4)

    f = mix[:, :32].reshape(X, Y * C, KB, 128).transpose(1, 0, 2, 3).reshape(1, Y * C, X * KB, 128)
    f = jnp.broadcast_to(f, (ZL, Y * C, X * KB, 128)).reshape(ZL * Y * C, X * KB, 128)
    grads_partner = swap(after(output_grads, f), "x", lambda i: 3 - i)
    f = scatter(f, ("zl", "y", "c"))

    rot = call(
        rotate_kernel, jax.ShapeDtypeStruct((X, 128, 256), F32), [f, basis_all], [VMEM] * 2, 2 * 128 * 1024 * 1024
    )
    rx = after(scatter(rot, "x"), grads_partner)
    o = jnp.concatenate([after(out_factors, rot), o_in], axis=0)
    o_in = swap(o, "zl", lambda i: i ^ 2)
    rot = jnp.sum(rx, axis=0)
    rotated = rot + after(swap(rot, "zh", lambda i: 1 - i), o_in)
    o = jnp.concatenate([after(o, rx), o_in], axis=0)
    o_in = swap(o, "zl", lambda i: i ^ 1)
    scaled = (rotated / (eigvals + DAMP)[None, :]).astype(BF)
    scaled = gather(scaled, "x")
    pt = call(
        precond_kernel, jax.ShapeDtypeStruct((Y * C, 128, 128), BF), [scaled, basis_all], [VMEM] * 2, 2 * 128 * 1024 * 1024
    )

    r2 = scatter(pt, "zl")
    o = jnp.concatenate([after(o, scaled), o_in], axis=0)
    o_other = swap(o, "x", lambda i: i ^ 1)

    part = call(
        output_kernel,
        jax.ShapeDtypeStruct((Y * C, 2 * ZL * KB, 512), F32),
        [pos, output_grads, grads_partner, after(o, pt), o_other],
        [SMEM] + [VMEM] * 4,
        2 * 512 * 512 * ff,
        [pltpu.VMEM((512, ff), BF)],
    )
    part = part[:Y] + swap(part[Y:], "c", lambda i: 1 - i)
    r2 = after(r2, part)
    s2 = jnp.sum(r2.astype(F32), axis=0).astype(BF)
    part = part[0] + sum(from_next(part[s], "y", -s) for s in (1, 2, 3))
    precond = after(gather(s2, "zl"), part)
    out_partner = swap(part[:, 256:], "x", lambda i: 3 - i)

    ins = call(
        input_kernel, jax.ShapeDtypeStruct((X, 256, 128), F32), [acts_all, precond], [VMEM] * 2, 2 * 128 * 1024 * 1024
    )
    keep, send = call(
        sides_kernel,
        [jax.ShapeDtypeStruct((2, 128, 128), F32)] * 2,
        [pos, scatter(ins, "x"), part[:, :256], out_partner],
        [SMEM] + [VMEM] * 3,
        128 * 1024,
    )
    sides = keep + swap(send, "zh", lambda i: 1 - i)
    shares = jnp.sum((sides[0] * sides[1]).reshape(ZL * X, KB, 128), axis=1)
    pieces = shares.reshape(ZL, X, Y * C, 16).transpose(2, 3, 1, 0).reshape(Y * C, 16 * X * ZL)
    return jnp.sum(scatter(pieces, ("y", "c")), axis=0).reshape(16, X * ZL)


def solution(mesh):
    fine = Mesh(mesh.devices.reshape(X, ZL, ZH, Y, C), ("x", "zl", "zh", "y", "c"))
    dp, feats = ("x", "zl"), ("zh", "y", "c")
    return jax.shard_map(
        on_device,
        mesh=fine,
        in_specs=(P(dp, feats), P(dp, feats), P(dp, feats), P(dp, feats), P(feats, dp), P(dp)),
        out_specs=P(dp + feats, None),
        check_vma=False,
    )
```

time: 249 us -> 224 us (0.90)
  the two profiles are of different devices: /device:TPU:161 before, /device:TPU:38 now
where the time goes in v2:
time: 224 us; the launch traced here: 223 us
  starting transfers between devices  96 us (43%)
  waiting for transfers between devices  65.8 us (29%)
  blocking collectives  29.5 us (13%)
  between operations  13.8 us (6%)
  local copies, waits for them, and re-layouts  9.18 us (4%)
  Pallas kernels  7.58 us (3%)
    all_to_all x5, starting transfers between devices, scatter(): return lax.all_to_all(v, axis, 0, 0, tiled=True)  46.8 us
    ppermute x9, waiting for transfers between devices, swap(): lax.ppermute(v, axis, [(i, partner(i)) for i in range(lax.axis_size(axis))])  41.6 us
    ppermute x9, starting transfers between devices, swap(): lax.ppermute(v, axis, [(i, partner(i)) for i in range(lax.axis_size(axis))])  40.3 us
    all_to_all x3, blocking collectives, scatter(): return lax.all_to_all(v, axis, 0, 0, tiled=True)  29.5 us
    all_to_all x5, waiting for transfers between devices, scatter(): return lax.all_to_all(v, axis, 0, 0, tiled=True)  19.5 us
    ppermute x3, starting transfers between devices, from_next(): return lax.ppermute(v, axis, [(i, (i - by) % n) for i in range(n)])  8.97 us
    pallas_call x5, Pallas kernels, call(): pl.pallas_call(kernel, out_shape=out, in_specs=specs, out_specs=[VMEM] *...  7.58 us
    ppermute x3, waiting for transfers between devices, from_next(): return lax.ppermute(v, axis, [(i, (i - by) % n) for i in range(n)])  4.66 us
  transfers between devices with their start and end apart: 19, of which 10 were waited for; matrix products, arithmetic and copies ran while one was open for 1% of the time, Pallas kernels for 2%

profile of v2, /device:TPU:38, one launch (start us, length us, event | category | flops | bytes accessed | tf_op | source)
XLA Modules:
  0.0 222.6 jit_solution(14843616387703741560)
XLA Ops:
  6.5 1.1 reshape.39
  7.6 0.3 copy.28
  7.9 0.2 reshape.40
  8.1 0.1 copy.27
  8.3 0.1 copy.29
  8.4 0.3 pad_maximum_fusion
  8.7 0.3 copy.30
  9.1 12.3 %all_to_all.45 = bf16[4,544,128]{2,1,0:T(8,128)(2,1)S(1)} all-to-all(bf16[4,544,128]{2,1,0:T(8,128)(2,1)S(1)} %copy.30), channel_id=1, replica_groups=mesh['x'=4,'zl'=8,'zh'=2,'y'=4,'c'=2] {'x'}, dimensions={0} | all-to-all | bytes 1114112 | tf_op jit(solution)/shard_map/all_to_all | solution.py:25
  21.4 0.8 fusion.1
  22.2 0.0 all-gather.5.cloned.1.call-update
  22.3 0.8 broadcast_in_dim.9
  23.1 15.8 %all-to-all-start.1 = ((bf16[64,16,128]{2,1,0:T(8,128)(2,1)}), bf16[64,16,128]{2,1,0:T(8,128)(2,1)S(1)}, u32[]{:S(2)}, u32[]{:S(2)}) async-start(bf16[64,16,128]{2,1,0:T(8,128)(2,1)} %bitcast.13), calls=%async_computation.1 | async-start | bytes 524288 | tf_op jit(solution)/shard_map/all_to_all | solution.py:25
  38.9 0.0 all-gather.3.cloned.1.call-start
  39.0 4.0 %collective-permute-start = (bf16[256,1792]{1,0:T(8,128)(2,1)S(1)}, bf16[256,1792]{1,0:T(8,128)(2,1)S(1)}, u32[]{:S(2)}, u32[]{:S(2)}) collective-permute-start(bf16[256,1792]{1,0:T(8,128)(2,1)S(1)} %copy-done.3), channel_id=1, source_target_pairs={{0,384},{128,256},{256,128},{384,0},{1,385},{129,257},{257,129},{3... | collective-permute-start | bytes 2752520 | tf_op jit(solution)/shard_map/ppermute | solution.py:21
  43.0 7.4 %collective-permute-start.2 = (bf16[32,1792]{1,0:T(8,128)(2,1)S(1)}, bf16[32,1792]{1,0:T(8,128)(2,1)S(1)}, u32[]{:S(2)}, u32[]{:S(2)}) collective-permute-start(bf16[32,1792]{1,0:T(8,128)(2,1)S(1)} %copy-done.5), channel_id=1, source_target_pairs={{0,64},{16,80},{32,96},{48,112},{64,0},{80,16},{96,32},{112,48},{1... | collective-permute-start | bytes 344072 | tf_op jit(solution)/shard_map/ppermute | solution.py:21
  50.4 0.0 all-gather.3.cloned.1.call-update
  50.4 12.1 %all-to-all-done.1.f = bf16[64,16,128]{2,1,0:T(8,128)(2,1)S(1)} async-done(((bf16[64,16,128]{2,1,0:T(8,128)(2,1)}), bf16[64,16,128]{2,1,0:T(8,128)(2,1)S(1)}, u32[]{:S(2)}, u32[]{:S(2)}) %all-to-all-start.1) | async-done | bytes 262176 | tf_op jit(solution)/shard_map/all_to_all | solution.py:25
  62.6 1.6 copy-done
  64.2 1.5 shard_map.64
  65.7 5.5 %all-to-all-start.2 = ((f32[4,128,256]{2,1,0:T(8,128)}), f32[4,128,256]{2,1,0:T(8,128)S(1)}, u32[]{:S(2)}, u32[]{:S(2)}) async-start(f32[4,128,256]{2,1,0:T(8,128)} %shard_map.64), calls=%async_computation.2 | async-start | bytes 1048576 | tf_op jit(solution)/shard_map/all_to_all | solution.py:25
  71.2 0.0 collective-permute-done.2
  71.2 3.4 %collective-permute-start.3 = (bf16[64,1792]{1,0:T(8,128)(2,1)S(1)}, bf16[64,1792]{1,0:T(8,128)(2,1)S(1)}, u32[]{:S(2)}, u32[]{:S(2)}) collective-permute-start(bf16[64,1792]{1,0:T(8,128)(2,1)S(1)} %constant_dynamic-update-slice_fusion), channel_id=1, source_target_pairs={{0,32},{16,48},{32,0},{48,16},{64,96},{80,112},{96,64},{112,80},{1... | collective-permute-start | bytes 688136 | tf_op jit(solution)/shard_map/ppermute | solution.py:21
  74.6 0.0 collective-permute-done.g1
  74.6 4.6 %all-to-all-done.2 = f32[4,128,256]{2,1,0:T(8,128)S(1)} async-done(((f32[4,128,256]{2,1,0:T(8,128)}), f32[4,128,256]{2,1,0:T(8,128)S(1)}, u32[]{:S(2)}, u32[]{:S(2)}) %all-to-all-start.2) | async-done | bytes 524320 | tf_op jit(solution)/shard_map/all_to_all | solution.py:25
  79.2 8.2 %collective-permute-start.1 = (f32[128,256]{1,0:T(8,128)S(1)}, f32[128,256]{1,0:T(8,128)S(1)}, u32[]{:S(2)}, u32[]{:S(2)}) collective-permute-start(f32[128,256]{1,0:T(8,128)S(1)} %reduce_sum.39), channel_id=1, source_target_pairs={{0,8},{8,0},{1,9},{9,1},{2,10},{10,2},{3,11},{11,3},{4,12},{12,4},... | collective-permute-start | bytes 393224 | tf_op jit(solution)/shard_map/ppermute | solution.py:21
  87.4 0.0 collective-permute-done.3
  87.5 3.7 %collective-permute-start.4 = (bf16[128,1792]{1,0:T(8,128)(2,1)S(1)}, bf16[128,1792]{1,0:T(8,128)(2,1)S(1)}, u32[]{:S(2)}, u32[]{:S(2)}) collective-permute-start(bf16[128,1792]{1,0:T(8,128)(2,1)S(1)} %constant_dynamic-update-slice_fusion.2), channel_id=1, source_target_pairs={{0,16},{16,0},{32,48},{48,32},{64,80},{80,64},{96,112},{112,96},{1... | collective-permute-start | bytes 1376264 | tf_op jit(solution)/shard_map/ppermute | solution.py:21
  91.2 10.3 %collective-permute-done.1 = f32[128,256]{1,0:T(8,128)S(1)} collective-permute-done((f32[128,256]{1,0:T(8,128)S(1)}, f32[128,256]{1,0:T(8,128)S(1)}, u32[]{:S(2)}, u32[]{:S(2)}) %collective-permute-start.1) | collective-permute-done | bytes 131104 | tf_op jit(solution)/shard_map/ppermute | solution.py:21
  101.5 0.0 copy-start.1
  101.5 9.4 %all_to_all.46.scaled = bf16[4,128,256]{2,1,0:T(8,128)(2,1)S(1)} all-to-all(bf16[4,128,256]{2,1,0:T(8,128)(2,1)S(1)} %broadcast_in_dim.10), channel_id=1, replica_groups=mesh['x'=4,'zl'=8,'zh'=2,'y'=4,'c'=2] {'x'}, dimensions={0} | all-to-all | bytes 524288 | tf_op jit(solution)/shard_map/all_to_all | solution.py:25
  111.0 0.0 collective-permute-done.4
  111.1 2.1 collective-permute-start.5
  113.2 1.4 shard_map.65
  114.6 10.3 %all-to-all-start.4 = ((bf16[8,128,128]{2,1,0:T(8,128)(2,1)}), bf16[8,128,128]{2,1,0:T(8,128)(2,1)S(1)}, u32[]{:S(2)}, u32[]{:S(2)}) async-start(bf16[8,128,128]{2,1,0:T(8,128)(2,1)} %shard_map.65), calls=%async_computation.4 | async-start | bytes 524288 | tf_op jit(solution)/shard_map/all_to_all | solution.py:25
  124.9 0.1 stack.23.pos
  125.0 8.6 %collective-permute-done.5.o1 = bf16[256,1792]{1,0:T(8,128)(2,1)} collective-permute-done((bf16[256,1792]{1,0:T(8,128)(2,1)S(1)}, bf16[256,1792]{1,0:T(8,128)(2,1)}, u32[]{:S(2)}, u32[]{:S(2)}) %collective-permute-start.5) | collective-permute-done | bytes 917536 | tf_op jit(solution)/shard_map/ppermute | solution.py:21
  133.6 2.5 %shard_map.66 = f32[8,64,512]{2,1,0:T(8,128)S(1)} custom-call(s32[5]{0:T(128)S(1)} %stack.23.pos, bf16[256,1792]{1,0:T(8,128)(2,1)S(1)} %copy-done.3, bf16[256,1792]{1,0:T(8,128)(2,1)S(1)} %collective-permute-done.g1, bf16[256,1792]{1,0:T(8,128)(2,1)S(1)} %constant_dynamic-update-slice_fusion.4.o0, bf16[256,1792]{1,0:T(8,128)(2,1)} %collective-permute-done.5.o1), custom_call_target="tpu_custom_call" | custom-call | flops 939524096 | bytes 3670036 | tf_op jit(solution)/shard_map/pallas_call | solution.py:39
  136.2 1.9 collective-permute-start.6
  138.1 1.9 collective-permute-done.6
  140.0 0.1 slice_add_fusion
  140.1 0.0 all-to-all-done.4
  140.1 0.7 broadcast_in_dim.11
  140.9 9.7 %all-to-all-start.5 = ((bf16[8,128,128]{2,1,0:T(8,128)(2,1)}), bf16[8,128,128]{2,1,0:T(8,128)(2,1)S(1)}, u32[]{:S(2)}, u32[]{:S(2)}) async-start(bf16[8,128,128]{2,1,0:T(8,128)(2,1)} %broadcast_in_dim.11), calls=%async_computation.5 | async-start | bytes 524288 | tf_op jit(solution)/shard_map/all_to_all | solution.py:25
  150.6 1.9 collective-permute-start.7
  152.5 3.3 %collective-permute-start.8 = (f32[64,512]{1,0:T(8,128)S(1)}, f32[64,512]{1,0:T(8,128)S(1)}, u32[]{:S(2)}, u32[]{:S(2)}) collective-permute-start(f32[64,512]{1,0:T(8,128)S(1)} %get-tuple-element.29), channel_id=1, source_target_pairs={{0,4},{2,6},{4,0},{6,2},{1,5},{3,7},{5,1},{7,3},{8,12},{10,14},{12... | collective-permute-start | bytes 393224 | tf_op jit(solution)/shard_map/ppermute | solution.py:108
  155.9 3.7 %collective-permute-start.9 = (f32[64,512]{1,0:T(8,128)S(1)}, f32[64,512]{1,0:T(8,128)S(1)}, u32[]{:S(2)}, u32[]{:S(2)}) collective-permute-start(f32[64,512]{1,0:T(8,128)S(1)} %get-tuple-element.30), channel_id=1, source_target_pairs={{0,6},{2,0},{4,2},{6,4},{1,7},{3,1},{5,3},{7,5},{8,14},{10,8},{12,... | collective-permute-start | bytes 393224 | tf_op jit(solution)/shard_map/ppermute | solution.py:108
  159.6 1.9 collective-permute-done.7
  161.5 0.0 collective-permute-done.8
  161.5 2.8 %collective-permute-done.9 = f32[64,512]{1,0:T(8,128)S(1)} collective-permute-done((f32[64,512]{1,0:T(8,128)S(1)}, f32[64,512]{1,0:T(8,128)S(1)}, u32[]{:S(2)}, u32[]{:S(2)}) %collective-permute-start.9) | collective-permute-done | bytes 131104 | tf_op jit(solution)/shard_map/ppermute | solution.py:108
  164.3 2.8 %all-to-all-done.5.pt = bf16[8,128,128]{2,1,0:T(8,128)(2,1)S(1)} async-done(((bf16[8,128,128]{2,1,0:T(8,128)(2,1)}), bf16[8,128,128]{2,1,0:T(8,128)(2,1)S(1)}, u32[]{:S(2)}, u32[]{:S(2)}) %all-to-all-start.5) | async-done | bytes 262176 | tf_op jit(solution)/shard_map/all_to_all | solution.py:25
  167.1 1.6 copy-done.2
  168.7 1.5 shard_map.67
  170.2 5.4 %all-to-all-start.6 = ((f32[4,256,128]{2,1,0:T(8,128)}), f32[4,256,128]{2,1,0:T(8,128)S(1)}, u32[]{:S(2)}, u32[]{:S(2)}) async-start(f32[4,256,128]{2,1,0:T(8,128)} %shard_map.67), calls=%async_computation.6 | async-start | bytes 1048576 | tf_op jit(solution)/shard_map/all_to_all | solution.py:25
  175.6 1.9 collective-permute-start.10
  177.6 5.4 %collective-permute-done.10.out_partner = f32[64,256]{1,0:T(8,128)S(1)} collective-permute-done((f32[64,256]{1,0:T(8,128)S(1)}, f32[64,256]{1,0:T(8,128)S(1)}, u32[]{:S(2)}, u32[]{:S(2)}) %collective-permute-start.10) | collective-permute-done | bytes 65568 | tf_op jit(solution)/shard_map/ppermute | solution.py:21
  183.0 0.0 all-to-all-done.6.parts
  183.0 0.6 shard_map.68
  183.7 7.6 %collective-permute-start.11 = (f32[2,128,128]{2,1,0:T(8,128)S(1)}, f32[2,128,128]{2,1,0:T(8,128)S(1)}, u32[]{:S(2)}, u32[]{:S(2)}) collective-permute-start(f32[2,128,128]{2,1,0:T(8,128)S(1)} %get-tuple-element.26), channel_id=1, source_target_pairs={{0,8},{8,0},{1,9},{9,1},{2,10},{10,2},{3,11},{11,3},{4,12},{12,4},... | collective-permute-start | bytes 393224 | tf_op jit(solution)/shard_map/ppermute | solution.py:21
  191.3 15.4 %collective-permute-done.11 = f32[2,128,128]{2,1,0:T(8,128)S(1)} collective-permute-done((f32[2,128,128]{2,1,0:T(8,128)S(1)}, f32[2,128,128]{2,1,0:T(8,128)S(1)}, u32[]{:S(2)}, u32[]{:S(2)}) %collective-permute-start.11) | collective-permute-done | bytes 131104 | tf_op jit(solution)/shard_map/ppermute | solution.py:21
  206.8 0.1 reshape.43
  206.9 0.2 copy.33
  207.0 0.3 all_to_all.36
  207.3 7.7 %all_to_all.47 = f32[8,1,512]{2,1,0:T(1,128)S(1)} all-to-all(f32[8,1,512]{2,1,0:T(1,128)S(1)} %all_to_all.36), channel_id=1, replica_groups=mesh['x'=4,'zl'=8,'zh'=2,'y'=4,'c'=2] {'y','c'}, dimensions={0} | all-to-all | bytes 32768 | tf_op jit(solution)/shard_map/all_to_all | solution.py:25
  215.1 0.7 reshape.44
  (39 shorter events, 0.5 us)
Async XLA Ops:
  6.5 1.6 copy-start.4
  6.5 1.7 copy-start.6
  6.5 56.0 %all-gather.5.cloned.1.call-start = ((), (), s32[]{:S(2)}) async-start(), calls=%async_computation.9 | async-start | bytes 2359296 | tf_op jit(solution)/shard_map/all_gather | solution.py:125
  21.4 17.6 %copy-start.3 = (bf16[256,1792]{1,0:T(8,128)(2,1)S(1)}, bf16[256,1792]{1,0:T(8,128)(2,1)}, u32[]{:S(2)}) copy-start(bf16[256,1792]{1,0:T(8,128)(2,1)} %g0.1) | copy-start | bytes 2752516
  21.4 21.5 %copy-start.5 = (bf16[32,1792]{1,0:T(8,128)(2,1)S(1)}, bf16[32,1792]{1,0:T(8,128)(2,1)}, u32[]{:S(2)}) copy-start(bf16[32,1792]{1,0:T(8,128)(2,1)} %param.8) | copy-start | bytes 344068
  21.4 29.0 %copy-start.7 = (f32[256]{0:T(256)S(1)}, f32[256]{0:T(256)}, u32[]{:S(2)}) copy-start(f32[256]{0:T(256)} %param.11) | copy-start | bytes 3076
  23.1 39.5 %all-to-all-start.1 = ((bf16[64,16,128]{2,1,0:T(8,128)(2,1)}), bf16[64,16,128]{2,1,0:T(8,128)(2,1)S(1)}, u32[]{:S(2)}, u32[]{:S(2)}) async-start(bf16[64,16,128]{2,1,0:T(8,128)(2,1)} %bitcast.13), calls=%async_computation.1 | async-start | bytes 524288 | tf_op jit(solution)/shard_map/all_to_all | solution.py:25
  38.9 128.2 %all-gather.3.cloned.1.call-start = ((), (), s32[]{:S(2)}) async-start(), calls=%async_computation.8 | async-start | bytes 2359296 | tf_op jit(solution)/shard_map/all_gather | solution.py:126
  39.0 35.6 %collective-permute-start = (bf16[256,1792]{1,0:T(8,128)(2,1)S(1)}, bf16[256,1792]{1,0:T(8,128)(2,1)S(1)}, u32[]{:S(2)}, u32[]{:S(2)}) collective-permute-start(bf16[256,1792]{1,0:T(8,128)(2,1)S(1)} %copy-done.3), channel_id=1, source_target_pairs={{0,384},{128,256},{256,128},{384,0},{1,385},{129,257},{257,129},{3... | collective-permute-start | bytes 2752520 | tf_op jit(solution)/shard_map/ppermute | solution.py:21
  43.0 28.2 %collective-permute-start.2 = (bf16[32,1792]{1,0:T(8,128)(2,1)S(1)}, bf16[32,1792]{1,0:T(8,128)(2,1)S(1)}, u32[]{:S(2)}, u32[]{:S(2)}) collective-permute-start(bf16[32,1792]{1,0:T(8,128)(2,1)S(1)} %copy-done.5), channel_id=1, source_target_pairs={{0,64},{16,80},{32,96},{48,112},{64,0},{80,16},{96,32},{112,48},{1... | collective-permute-start | bytes 344072 | tf_op jit(solution)/shard_map/ppermute | solution.py:21
  62.6 1.6 copy-start
  65.7 13.5 %all-to-all-start.2 = ((f32[4,128,256]{2,1,0:T(8,128)}), f32[4,128,256]{2,1,0:T(8,128)S(1)}, u32[]{:S(2)}, u32[]{:S(2)}) async-start(f32[4,128,256]{2,1,0:T(8,128)} %shard_map.64), calls=%async_computation.2 | async-start | bytes 1048576 | tf_op jit(solution)/shard_map/all_to_all | solution.py:25
  71.2 16.2 %collective-permute-start.3 = (bf16[64,1792]{1,0:T(8,128)(2,1)S(1)}, bf16[64,1792]{1,0:T(8,128)(2,1)S(1)}, u32[]{:S(2)}, u32[]{:S(2)}) collective-permute-start(bf16[64,1792]{1,0:T(8,128)(2,1)S(1)} %constant_dynamic-update-slice_fusion), channel_id=1, source_target_pairs={{0,32},{16,48},{32,0},{48,16},{64,96},{80,112},{96,64},{112,80},{1... | collective-permute-start | bytes 688136 | tf_op jit(solution)/shard_map/ppermute | solution.py:21
  79.2 22.3 %collective-permute-start.1 = (f32[128,256]{1,0:T(8,128)S(1)}, f32[128,256]{1,0:T(8,128)S(1)}, u32[]{:S(2)}, u32[]{:S(2)}) collective-permute-start(f32[128,256]{1,0:T(8,128)S(1)} %reduce_sum.39), channel_id=1, source_target_pairs={{0,8},{8,0},{1,9},{9,1},{2,10},{10,2},{3,11},{11,3},{4,12},{12,4},... | collective-permute-start | bytes 393224 | tf_op jit(solution)/shard_map/ppermute | solution.py:21
  87.5 23.6 %collective-permute-start.4 = (bf16[128,1792]{1,0:T(8,128)(2,1)S(1)}, bf16[128,1792]{1,0:T(8,128)(2,1)S(1)}, u32[]{:S(2)}, u32[]{:S(2)}) collective-permute-start(bf16[128,1792]{1,0:T(8,128)(2,1)S(1)} %constant_dynamic-update-slice_fusion.2), channel_id=1, source_target_pairs={{0,16},{16,0},{32,48},{48,32},{64,80},{80,64},{96,112},{112,96},{1... | collective-permute-start | bytes 1376264 | tf_op jit(solution)/shard_map/ppermute | solution.py:21
  101.5 11.7 %copy-start.1 = (bf16[8,1024,128]{2,1,0:T(8,128)(2,1)S(1)}, bf16[8,1024,128]{2,1,0:T(8,128)(2,1)}, u32[]{:S(2)}) copy-start(bf16[8,1024,128]{2,1,0:T(8,128)(2,1)} %all-gather.5.cloned.1.call-done.basis) | copy-start | bytes 6291460
  111.1 22.5 %collective-permute-start.5 = (bf16[256,1792]{1,0:T(8,128)(2,1)S(1)}, bf16[256,1792]{1,0:T(8,128)(2,1)}, u32[]{:S(2)}, u32[]{:S(2)}) collective-permute-start(bf16[256,1792]{1,0:T(8,128)(2,1)S(1)} %constant_dynamic-update-slice_fusion.4.o0), channel_id=1, source_target_pairs={{0,128},{128,0},{256,384},{384,256},{1,129},{129,1},{257,385},{385... | collective-permute-start | bytes 2752520 | tf_op jit(solution)/shard_map/ppermute | solution.py:21
  114.6 25.4 %all-to-all-start.4 = ((bf16[8,128,128]{2,1,0:T(8,128)(2,1)}), bf16[8,128,128]{2,1,0:T(8,128)(2,1)S(1)}, u32[]{:S(2)}, u32[]{:S(2)}) async-start(bf16[8,128,128]{2,1,0:T(8,128)(2,1)} %shard_map.65), calls=%async_computation.4 | async-start | bytes 524288 | tf_op jit(solution)/shard_map/all_to_all | solution.py:25
  136.2 3.8 %collective-permute-start.6 = (f32[4,64,512]{2,1,0:T(8,128)S(1)}, f32[4,64,512]{2,1,0:T(8,128)S(1)}, u32[]{:S(2)}, u32[]{:S(2)}) collective-permute-start(f32[4,64,512]{2,1,0:T(8,128)S(1)} %slice.56), channel_id=1, source_target_pairs={{0,1},{1,0},{2,3},{3,2},{4,5},{5,4},{6,7},{7,6},{8,9},{9,8},{10,11... | collective-permute-start | bytes 1572872 | tf_op jit(solution)/shard_map/ppermute | solution.py:21
  140.9 26.3 %all-to-all-start.5 = ((bf16[8,128,128]{2,1,0:T(8,128)(2,1)}), bf16[8,128,128]{2,1,0:T(8,128)(2,1)S(1)}, u32[]{:S(2)}, u32[]{:S(2)}) async-start(bf16[8,128,128]{2,1,0:T(8,128)(2,1)} %broadcast_in_dim.11), calls=%async_computation.5 | async-start | bytes 524288 | tf_op jit(solution)/shard_map/all_to_all | solution.py:25
  150.6 10.9 %collective-permute-start.7 = (f32[64,512]{1,0:T(8,128)S(1)}, f32[64,512]{1,0:T(8,128)S(1)}, u32[]{:S(2)}, u32[]{:S(2)}) collective-permute-start(f32[64,512]{1,0:T(8,128)S(1)} %get-tuple-element.31), channel_id=1, source_target_pairs={{0,2},{2,4},{4,6},{6,0},{1,3},{3,5},{5,7},{7,1},{8,10},{10,12},{12... | collective-permute-start | bytes 393224 | tf_op jit(solution)/shard_map/ppermute | solution.py:108
  152.5 9.0 %collective-permute-start.8 = (f32[64,512]{1,0:T(8,128)S(1)}, f32[64,512]{1,0:T(8,128)S(1)}, u32[]{:S(2)}, u32[]{:S(2)}) collective-permute-start(f32[64,512]{1,0:T(8,128)S(1)} %get-tuple-element.29), channel_id=1, source_target_pairs={{0,4},{2,6},{4,0},{6,2},{1,5},{3,7},{5,1},{7,3},{8,12},{10,14},{12... | collective-permute-start | bytes 393224 | tf_op jit(solution)/shard_map/ppermute | solution.py:108
  155.9 8.4 %collective-permute-start.9 = (f32[64,512]{1,0:T(8,128)S(1)}, f32[64,512]{1,0:T(8,128)S(1)}, u32[]{:S(2)}, u32[]{:S(2)}) collective-permute-start(f32[64,512]{1,0:T(8,128)S(1)} %get-tuple-element.30), channel_id=1, source_target_pairs={{0,6},{2,0},{4,2},{6,4},{1,7},{3,1},{5,3},{7,5},{8,14},{10,8},{12,... | collective-permute-start | bytes 393224 | tf_op jit(solution)/shard_map/ppermute | solution.py:108
  167.1 1.6 copy-start.2
  170.2 12.8 %all-to-all-start.6 = ((f32[4,256,128]{2,1,0:T(8,128)}), f32[4,256,128]{2,1,0:T(8,128)S(1)}, u32[]{:S(2)}, u32[]{:S(2)}) async-start(f32[4,256,128]{2,1,0:T(8,128)} %shard_map.67), calls=%async_computation.6 | async-start | bytes 1048576 | tf_op jit(solution)/shard_map/all_to_all | solution.py:25
  175.6 7.4 %collective-permute-start.10 = (f32[64,256]{1,0:T(8,128)S(1)}, f32[64,256]{1,0:T(8,128)S(1)}, u32[]{:S(2)}, u32[]{:S(2)}) collective-permute-start(f32[64,256]{1,0:T(8,128)S(1)} %get-tuple-element.32), channel_id=1, source_target_pairs={{0,384},{128,256},{256,128},{384,0},{1,385},{129,257},{257,129},{3... | collective-permute-start | bytes 196616 | tf_op jit(solution)/shard_map/ppermute | solution.py:21
  183.7 23.0 %collective-permute-start.11 = (f32[2,128,128]{2,1,0:T(8,128)S(1)}, f32[2,128,128]{2,1,0:T(8,128)S(1)}, u32[]{:S(2)}, u32[]{:S(2)}) collective-permute-start(f32[2,128,128]{2,1,0:T(8,128)S(1)} %get-tuple-element.26), channel_id=1, source_target_pairs={{0,8},{8,0},{1,9},{9,1},{2,10},{10,2},{3,11},{11,3},{4,12},{12,4},... | collective-permute-start | bytes 393224 | tf_op jit(solution)/shard_map/ppermute | solution.py:21
Sparse Core Ops, SparseCore 0:
  22.4 36.9 all-gather.4
  61.6 33.5 all-gather.2

commit v3 on v2

--- a/solution.py
+++ b/solution.py
@@ -45,6 +45,23 @@
         compiler_params=pltpu.CompilerParams(vmem_limit_bytes=limit * 2**20),
         cost_estimate=pl.CostEstimate(flops=flops, bytes_accessed=moved, transcendentals=0),
     )(*args)
+
+
+def cut_kernel(factors, acts, basis, mix):
+    for i in range(X):
+        q = slice(i * 128, (i + 1) * 128)
+        mix[i, :32, :] = factors[:, q]
+        mix[i, 32:288, :] = acts[:, q]
+        for h in range(2):
+            mix[i, 288 + h * 128:416 + h * 128, :] = basis[q, h * 128:(h + 1) * 128]
+
+
+def spread_kernel(mix, out):
+    rows = [mix[i, :32, :].astype(F32) for i in range(X)]
+    for b in range(Y * C):
+        piece = jnp.concatenate([v[b * KB:(b + 1) * KB, :] for v in rows], axis=0).astype(BF)
+        for zl in range(ZL):
+            out[zl * Y * C + b] = piece
 
 
 def rotate_kernel(f, basis, rot):
@@ -113,21 +130,15 @@
     pos = jnp.stack([x, zh, lax.axis_index("y"), lax.axis_index("c"), zl])
     ff = output_grads.shape[1]
 
-    mix = jnp.concatenate(
-        [
-            in_factors.reshape(RANK, X, 128).transpose(1, 0, 2),
-            activations.reshape(256, X, 128).transpose(1, 0, 2),
-            basis.reshape(X, 128, 2, 128).transpose(0, 2, 1, 3).reshape(X, 256, 128),
-        ],
-        axis=1,
+    mix = call(
+        cut_kernel, jax.ShapeDtypeStruct((X, 544, 128), BF), [in_factors, activations, basis], [VMEM] * 3, 0
     )
     mix = scatter(mix, "x")
     basis_all = lax.all_gather(mix[:, 288:].reshape(1024, 128), ("y", "c"))
     acts_all = lax.all_gather(mix[:, 32:288].reshape(1024, 128), ("y", "c"))
     o_in = swap(out_factors, "zl", lambda i: i ^ 4)
 
-    f = mix[:, :32].reshape(X, Y * C, KB, 128).transpose(1, 0, 2, 3).reshape(1, Y * C, X * KB, 128)
-    f = jnp.broadcast_to(f, (ZL, Y * C, X * KB, 128)).reshape(ZL * Y * C, X * KB, 128)
+    f = call(spread_kernel, jax.ShapeDtypeStruct((ZL * Y * C, X * KB, 128), BF), [mix], [VMEM], 0)
     grads_partner = swap(after(output_grads, f), "x", lambda i: 3 - i)
     f = scatter(f, ("zl", "y", "c"))
 
@@ -163,7 +174,7 @@
     r2 = after(r2, part)
     s2 = jnp.sum(r2.astype(F32), axis=0).astype(BF)
     part = part[0] + sum(from_next(part[s], "y", -s) for s in (1, 2, 3))
-    precond = after(gather(s2, "zl"), part)
+    precond = after(gather(s2, "zl"), part, acts_all)
     out_partner = swap(part[:, 256:], "x", lambda i: 3 - i)
 
     ins = call(

time: 224 us -> 223 us (level)
    unnamed x20 -> x21, local copies, waits for them, and re-layouts: 3.39 us -> 5.92 us
    pallas_call x5 -> x7, Pallas kernels: 7.58 us -> 8.41 us  [call(): pl.pallas_call(kernel, out_shape=out, in_specs=specs, out_specs=[VMEM] *...]
  transfers between devices with their start and end apart: 19 -> 19, of which waited for: 10 -> 10; matrix products, arithmetic and copies ran while one was open for 1% -> 1% of each run, Pallas kernels for 2% -> 3%
where the time goes in v3:
time: 223 us; the launch traced here: 222 us
  starting transfers between devices  96.3 us (43%)
  waiting for transfers between devices  65.1 us (29%)
  blocking collectives  29.4 us (13%)
  between operations  13.8 us (6%)
  local copies, waits for them, and re-layouts  8.93 us (4%)
  Pallas kernels  8.41 us (4%)
    all_to_all x5, starting transfers between devices, scatter(): return lax.all_to_all(v, axis, 0, 0, tiled=True)  46.2 us
    ppermute x9, starting transfers between devices, swap(): lax.ppermute(v, axis, [(i, partner(i)) for i in range(lax.axis_size(axis))])  41 us
    ppermute x9, waiting for transfers between devices, swap(): lax.ppermute(v, axis, [(i, partner(i)) for i in range(lax.axis_size(axis))])  40.9 us
    all_to_all x3, blocking collectives, scatter(): return lax.all_to_all(v, axis, 0, 0, tiled=True)  29.4 us
    all_to_all x5, waiting for transfers between devices, scatter(): return lax.all_to_all(v, axis, 0, 0, tiled=True)  19.5 us
    ppermute x3, starting transfers between devices, from_next(): return lax.ppermute(v, axis, [(i, (i - by) % n) for i in range(n)])  8.97 us
    pallas_call x7, Pallas kernels, call(): pl.pallas_call(kernel, out_shape=out, in_specs=specs, out_specs=[VMEM] *...  8.41 us
    unnamed x21, local copies, waits for them, and re-layouts  5.92 us
  transfers between devices with their start and end apart: 19, of which 10 were waited for; matrix products, arithmetic and copies ran while one was open for 1% of the time, Pallas kernels for 3%

profile of v3, /device:TPU:38, one launch (start us, length us, event | category | flops | bytes accessed | tf_op | source)
XLA Modules:
  0.0 222.2 jit_solution(9765273848385072078)
XLA Ops:
  6.5 0.9 copy-done.4
  7.5 0.9 copy-done.5
  8.4 0.8 copy-done.6
  9.2 0.1 shard_map.64
  9.3 0.0 copy-start.3
  9.3 0.0 copy-start.7
  9.3 0.0 copy-start.8
  9.3 12.5 %all_to_all.45.mix = bf16[4,544,128]{2,1,0:T(8,128)(2,1)S(1)} all-to-all(bf16[4,544,128]{2,1,0:T(8,128)(2,1)S(1)} %shard_map.64), channel_id=1, replica_groups=mesh['x'=4,'zl'=8,'zh'=2,'y'=4,'c'=2] {'x'}, dimensions={0} | all-to-all | bytes 1114112 | tf_op jit(solution)/shard_map/all_to_all | solution.py:25
  21.8 0.9 fusion.1
  22.6 0.0 all-gather.5.cloned.1.call-update
  22.7 0.7 shard_map.65
  23.4 15.8 %all-to-all-start.1 = ((bf16[64,16,128]{2,1,0:T(8,128)(2,1)}), bf16[64,16,128]{2,1,0:T(8,128)(2,1)S(1)}, u32[]{:S(2)}, u32[]{:S(2)}) async-start(bf16[64,16,128]{2,1,0:T(8,128)(2,1)} %shard_map.65), calls=%async_computation.1 | async-start | bytes 524288 | tf_op jit(solution)/shard_map/all_to_all | solution.py:25
  39.2 0.0 all-gather.3.cloned.1.call-start
  39.3 4.0 %collective-permute-start = (bf16[256,1792]{1,0:T(8,128)(2,1)S(1)}, bf16[256,1792]{1,0:T(8,128)(2,1)S(1)}, u32[]{:S(2)}, u32[]{:S(2)}) collective-permute-start(bf16[256,1792]{1,0:T(8,128)(2,1)S(1)} %copy-done.3), channel_id=1, source_target_pairs={{0,384},{128,256},{256,128},{384,0},{1,385},{129,257},{257,129},{3... | collective-permute-start | bytes 2752520 | tf_op jit(solution)/shard_map/ppermute | solution.py:21
  43.3 7.4 %collective-permute-start.2 = (bf16[32,1792]{1,0:T(8,128)(2,1)S(1)}, bf16[32,1792]{1,0:T(8,128)(2,1)S(1)}, u32[]{:S(2)}, u32[]{:S(2)}) collective-permute-start(bf16[32,1792]{1,0:T(8,128)(2,1)S(1)} %copy-done.7), channel_id=1, source_target_pairs={{0,64},{16,80},{32,96},{48,112},{64,0},{80,16},{96,32},{112,48},{1... | collective-permute-start | bytes 344072 | tf_op jit(solution)/shard_map/ppermute | solution.py:21
  50.8 0.0 all-gather.3.cloned.1.call-update
  50.8 12.1 %all-to-all-done.1.f = bf16[64,16,128]{2,1,0:T(8,128)(2,1)S(1)} async-done(((bf16[64,16,128]{2,1,0:T(8,128)(2,1)}), bf16[64,16,128]{2,1,0:T(8,128)(2,1)S(1)}, u32[]{:S(2)}, u32[]{:S(2)}) %all-to-all-start.1) | async-done | bytes 262176 | tf_op jit(solution)/shard_map/all_to_all | solution.py:25
  62.9 1.6 copy-done
  64.5 1.5 shard_map.66
  66.0 5.5 %all-to-all-start.2 = ((f32[4,128,256]{2,1,0:T(8,128)}), f32[4,128,256]{2,1,0:T(8,128)S(1)}, u32[]{:S(2)}, u32[]{:S(2)}) async-start(f32[4,128,256]{2,1,0:T(8,128)} %shard_map.66), calls=%async_computation.2 | async-start | bytes 1048576 | tf_op jit(solution)/shard_map/all_to_all | solution.py:25
  71.5 0.0 collective-permute-done.2
  71.6 3.3 %collective-permute-start.3 = (bf16[64,1792]{1,0:T(8,128)(2,1)S(1)}, bf16[64,1792]{1,0:T(8,128)(2,1)S(1)}, u32[]{:S(2)}, u32[]{:S(2)}) collective-permute-start(bf16[64,1792]{1,0:T(8,128)(2,1)S(1)} %constant_dynamic-update-slice_fusion), channel_id=1, source_target_pairs={{0,32},{16,48},{32,0},{48,16},{64,96},{80,112},{96,64},{112,80},{1... | collective-permute-start | bytes 688136 | tf_op jit(solution)/shard_map/ppermute | solution.py:21
  74.9 0.0 collective-permute-done.g1
  74.9 4.6 %all-to-all-done.2 = f32[4,128,256]{2,1,0:T(8,128)S(1)} async-done(((f32[4,128,256]{2,1,0:T(8,128)}), f32[4,128,256]{2,1,0:T(8,128)S(1)}, u32[]{:S(2)}, u32[]{:S(2)}) %all-to-all-start.2) | async-done | bytes 524320 | tf_op jit(solution)/shard_map/all_to_all | solution.py:25
  79.5 8.4 %collective-permute-start.1 = (f32[128,256]{1,0:T(8,128)S(1)}, f32[128,256]{1,0:T(8,128)S(1)}, u32[]{:S(2)}, u32[]{:S(2)}) collective-permute-start(f32[128,256]{1,0:T(8,128)S(1)} %reduce_sum.39), channel_id=1, source_target_pairs={{0,8},{8,0},{1,9},{9,1},{2,10},{10,2},{3,11},{11,3},{4,12},{12,4},... | collective-permute-start | bytes 393224 | tf_op jit(solution)/shard_map/ppermute | solution.py:21
  87.9 0.0 collective-permute-done.3
  87.9 3.7 %collective-permute-start.4 = (bf16[128,1792]{1,0:T(8,128)(2,1)S(1)}, bf16[128,1792]{1,0:T(8,128)(2,1)S(1)}, u32[]{:S(2)}, u32[]{:S(2)}) collective-permute-start(bf16[128,1792]{1,0:T(8,128)(2,1)S(1)} %constant_dynamic-update-slice_fusion.2), channel_id=1, source_target_pairs={{0,16},{16,0},{32,48},{48,32},{64,80},{80,64},{96,112},{112,96},{1... | collective-permute-start | bytes 1376264 | tf_op jit(solution)/shard_map/ppermute | solution.py:21
  91.6 10.6 %collective-permute-done.1 = f32[128,256]{1,0:T(8,128)S(1)} collective-permute-done((f32[128,256]{1,0:T(8,128)S(1)}, f32[128,256]{1,0:T(8,128)S(1)}, u32[]{:S(2)}, u32[]{:S(2)}) %collective-permute-start.1) | collective-permute-done | bytes 131104 | tf_op jit(solution)/shard_map/ppermute | solution.py:21
  102.3 9.2 %all_to_all.46.scaled = bf16[4,128,256]{2,1,0:T(8,128)(2,1)S(1)} all-to-all(bf16[4,128,256]{2,1,0:T(8,128)(2,1)S(1)} %broadcast_in_dim.4), channel_id=1, replica_groups=mesh['x'=4,'zl'=8,'zh'=2,'y'=4,'c'=2] {'x'}, dimensions={0} | all-to-all | bytes 524288 | tf_op jit(solution)/shard_map/all_to_all | solution.py:25
  111.5 0.0 collective-permute-done.4
  111.6 2.1 collective-permute-start.5
  113.7 1.4 shard_map.67
  115.1 10.2 %all-to-all-start.4 = ((bf16[8,128,128]{2,1,0:T(8,128)(2,1)}), bf16[8,128,128]{2,1,0:T(8,128)(2,1)S(1)}, u32[]{:S(2)}, u32[]{:S(2)}) async-start(bf16[8,128,128]{2,1,0:T(8,128)(2,1)} %shard_map.67), calls=%async_computation.4 | async-start | bytes 524288 | tf_op jit(solution)/shard_map/all_to_all | solution.py:25
  125.3 0.1 stack.23.pos
  125.4 8.6 %collective-permute-done.5.o1 = bf16[256,1792]{1,0:T(8,128)(2,1)} collective-permute-done((bf16[256,1792]{1,0:T(8,128)(2,1)S(1)}, bf16[256,1792]{1,0:T(8,128)(2,1)}, u32[]{:S(2)}, u32[]{:S(2)}) %collective-permute-start.5) | collective-permute-done | bytes 917536 | tf_op jit(solution)/shard_map/ppermute | solution.py:21
  134.0 2.5 %shard_map.68 = f32[8,64,512]{2,1,0:T(8,128)S(1)} custom-call(s32[5]{0:T(128)S(1)} %stack.23.pos, bf16[256,1792]{1,0:T(8,128)(2,1)S(1)} %copy-done.3, bf16[256,1792]{1,0:T(8,128)(2,1)S(1)} %collective-permute-done.g1, bf16[256,1792]{1,0:T(8,128)(2,1)S(1)} %constant_dynamic-update-slice_fusion.4.o0, bf16[256,1792]{1,0:T(8,128)(2,1)} %collective-permute-done.5.o1), custom_call_target="tpu_custom_call" | custom-call | flops 939524096 | bytes 3670036 | tf_op jit(solution)/shard_map/pallas_call | solution.py:39
  136.6 1.9 collective-permute-start.6
  138.5 1.9 collective-permute-done.6
  140.4 0.1 slice_add_fusion
  140.4 0.0 all-to-all-done.4
  140.5 0.7 broadcast_in_dim.5
  141.2 9.2 %all-to-all-start.5 = ((bf16[8,128,128]{2,1,0:T(8,128)(2,1)}), bf16[8,128,128]{2,1,0:T(8,128)(2,1)S(1)}, u32[]{:S(2)}, u32[]{:S(2)}) async-start(bf16[8,128,128]{2,1,0:T(8,128)(2,1)} %broadcast_in_dim.5), calls=%async_computation.5 | async-start | bytes 524288 | tf_op jit(solution)/shard_map/all_to_all | solution.py:25
  150.5 1.9 collective-permute-start.7
  152.4 2.7 %collective-permute-start.8 = (f32[64,512]{1,0:T(8,128)S(1)}, f32[64,512]{1,0:T(8,128)S(1)}, u32[]{:S(2)}, u32[]{:S(2)}) collective-permute-start(f32[64,512]{1,0:T(8,128)S(1)} %get-tuple-element.29), channel_id=1, source_target_pairs={{0,4},{2,6},{4,0},{6,2},{1,5},{3,7},{5,1},{7,3},{8,12},{10,14},{12... | collective-permute-start | bytes 393224 | tf_op jit(solution)/shard_map/ppermute | solution.py:125
  155.1 4.3 %collective-permute-start.9 = (f32[64,512]{1,0:T(8,128)S(1)}, f32[64,512]{1,0:T(8,128)S(1)}, u32[]{:S(2)}, u32[]{:S(2)}) collective-permute-start(f32[64,512]{1,0:T(8,128)S(1)} %get-tuple-element.30), channel_id=1, source_target_pairs={{0,6},{2,0},{4,2},{6,4},{1,7},{3,1},{5,3},{7,5},{8,14},{10,8},{12,... | collective-permute-start | bytes 393224 | tf_op jit(solution)/shard_map/ppermute | solution.py:125
  159.5 1.9 collective-permute-done.7
  161.4 0.0 collective-permute-done.8
  161.4 2.8 %collective-permute-done.9 = f32[64,512]{1,0:T(8,128)S(1)} collective-permute-done((f32[64,512]{1,0:T(8,128)S(1)}, f32[64,512]{1,0:T(8,128)S(1)}, u32[]{:S(2)}, u32[]{:S(2)}) %collective-permute-start.9) | collective-permute-done | bytes 131104 | tf_op jit(solution)/shard_map/ppermute | solution.py:125
  164.2 0.0 all-gather.3.cloned.1.call-done.acts
  164.2 2.8 %all-to-all-done.5.pt = bf16[8,128,128]{2,1,0:T(8,128)(2,1)S(1)} async-done(((bf16[8,128,128]{2,1,0:T(8,128)(2,1)}), bf16[8,128,128]{2,1,0:T(8,128)(2,1)S(1)}, u32[]{:S(2)}, u32[]{:S(2)}) %all-to-all-start.5) | async-done | bytes 262176 | tf_op jit(solution)/shard_map/all_to_all | solution.py:25
  167.0 1.6 copy-done.2
  168.6 1.5 shard_map.69
  170.1 5.5 %all-to-all-start.6 = ((f32[4,256,128]{2,1,0:T(8,128)}), f32[4,256,128]{2,1,0:T(8,128)S(1)}, u32[]{:S(2)}, u32[]{:S(2)}) async-start(f32[4,256,128]{2,1,0:T(8,128)} %shard_map.69), calls=%async_computation.6 | async-start | bytes 1048576 | tf_op jit(solution)/shard_map/all_to_all | solution.py:25
  175.6 1.9 collective-permute-start.10
  177.5 5.4 %collective-permute-done.10.out_partner = f32[64,256]{1,0:T(8,128)S(1)} collective-permute-done((f32[64,256]{1,0:T(8,128)S(1)}, f32[64,256]{1,0:T(8,128)S(1)}, u32[]{:S(2)}, u32[]{:S(2)}) %collective-permute-start.10) | collective-permute-done | bytes 65568 | tf_op jit(solution)/shard_map/ppermute | solution.py:21
  182.9 0.0 all-to-all-done.6.parts
  183.0 0.6 shard_map.70
  183.6 8.2 %collective-permute-start.11 = (f32[2,128,128]{2,1,0:T(8,128)S(1)}, f32[2,128,128]{2,1,0:T(8,128)S(1)}, u32[]{:S(2)}, u32[]{:S(2)}) collective-permute-start(f32[2,128,128]{2,1,0:T(8,128)S(1)} %get-tuple-element.26), channel_id=1, source_target_pairs={{0,8},{8,0},{1,9},{9,1},{2,10},{10,2},{3,11},{11,3},{4,12},{12,4},... | collective-permute-start | bytes 393224 | tf_op jit(solution)/shard_map/ppermute | solution.py:21
  191.9 14.4 %collective-permute-done.11 = f32[2,128,128]{2,1,0:T(8,128)S(1)} collective-permute-done((f32[2,128,128]{2,1,0:T(8,128)S(1)}, f32[2,128,128]{2,1,0:T(8,128)S(1)}, u32[]{:S(2)}, u32[]{:S(2)}) %collective-permute-start.11) | collective-permute-done | bytes 131104 | tf_op jit(solution)/shard_map/ppermute | solution.py:21
  206.4 0.1 reshape.17
  206.5 0.2 copy.8
  206.6 0.3 all_to_all.36
  206.9 7.7 %all_to_all.47 = f32[8,1,512]{2,1,0:T(1,128)S(1)} all-to-all(f32[8,1,512]{2,1,0:T(1,128)S(1)} %all_to_all.36), channel_id=1, replica_groups=mesh['x'=4,'zl'=8,'zh'=2,'y'=4,'c'=2] {'y','c'}, dimensions={0} | all-to-all | bytes 32768 | tf_op jit(solution)/shard_map/all_to_all | solution.py:25
  214.7 0.7 reshape.18
  (31 shorter events, 0.5 us)
Async XLA Ops:
  6.5 56.4 %all-gather.5.cloned.1.call-start = ((), (), s32[]{:S(2)}) async-start(), calls=%async_computation.9 | async-start | bytes 2359296 | tf_op jit(solution)/shard_map/all_gather | solution.py:137
  6.5 0.9 copy-start.4
  7.5 0.9 copy-start.5
  8.4 0.8 copy-start.6
  9.3 30.0 %copy-start.3 = (bf16[256,1792]{1,0:T(8,128)(2,1)S(1)}, bf16[256,1792]{1,0:T(8,128)(2,1)}, u32[]{:S(2)}) copy-start(bf16[256,1792]{1,0:T(8,128)(2,1)} %g0.1) | copy-start | bytes 2752516
  9.3 34.0 %copy-start.7 = (bf16[32,1792]{1,0:T(8,128)(2,1)S(1)}, bf16[32,1792]{1,0:T(8,128)(2,1)}, u32[]{:S(2)}) copy-start(bf16[32,1792]{1,0:T(8,128)(2,1)} %param.8) | copy-start | bytes 344068
  9.3 41.4 %copy-start.8 = (f32[256]{0:T(256)S(1)}, f32[256]{0:T(256)}, u32[]{:S(2)}) copy-start(f32[256]{0:T(256)} %param.11) | copy-start | bytes 3076
  23.4 39.5 %all-to-all-start.1 = ((bf16[64,16,128]{2,1,0:T(8,128)(2,1)}), bf16[64,16,128]{2,1,0:T(8,128)(2,1)S(1)}, u32[]{:S(2)}, u32[]{:S(2)}) async-start(bf16[64,16,128]{2,1,0:T(8,128)(2,1)} %shard_map.65), calls=%async_computation.1 | async-start | bytes 524288 | tf_op jit(solution)/shard_map/all_to_all | solution.py:25
  39.2 124.9 %all-gather.3.cloned.1.call-start = ((), (), s32[]{:S(2)}) async-start(), calls=%async_computation.8 | async-start | bytes 2359296 | tf_op jit(solution)/shard_map/all_gather | solution.py:138
  39.3 35.6 %collective-permute-start = (bf16[256,1792]{1,0:T(8,128)(2,1)S(1)}, bf16[256,1792]{1,0:T(8,128)(2,1)S(1)}, u32[]{:S(2)}, u32[]{:S(2)}) collective-permute-start(bf16[256,1792]{1,0:T(8,128)(2,1)S(1)} %copy-done.3), channel_id=1, source_target_pairs={{0,384},{128,256},{256,128},{384,0},{1,385},{129,257},{257,129},{3... | collective-permute-start | bytes 2752520 | tf_op jit(solution)/shard_map/ppermute | solution.py:21
  43.3 28.2 %collective-permute-start.2 = (bf16[32,1792]{1,0:T(8,128)(2,1)S(1)}, bf16[32,1792]{1,0:T(8,128)(2,1)S(1)}, u32[]{:S(2)}, u32[]{:S(2)}) collective-permute-start(bf16[32,1792]{1,0:T(8,128)(2,1)S(1)} %copy-done.7), channel_id=1, source_target_pairs={{0,64},{16,80},{32,96},{48,112},{64,0},{80,16},{96,32},{112,48},{1... | collective-permute-start | bytes 344072 | tf_op jit(solution)/shard_map/ppermute | solution.py:21
  62.9 1.6 copy-start
  66.0 13.5 %all-to-all-start.2 = ((f32[4,128,256]{2,1,0:T(8,128)}), f32[4,128,256]{2,1,0:T(8,128)S(1)}, u32[]{:S(2)}, u32[]{:S(2)}) async-start(f32[4,128,256]{2,1,0:T(8,128)} %shard_map.66), calls=%async_computation.2 | async-start | bytes 1048576 | tf_op jit(solution)/shard_map/all_to_all | solution.py:25
  71.6 16.4 %collective-permute-start.3 = (bf16[64,1792]{1,0:T(8,128)(2,1)S(1)}, bf16[64,1792]{1,0:T(8,128)(2,1)S(1)}, u32[]{:S(2)}, u32[]{:S(2)}) collective-permute-start(bf16[64,1792]{1,0:T(8,128)(2,1)S(1)} %constant_dynamic-update-slice_fusion), channel_id=1, source_target_pairs={{0,32},{16,48},{32,0},{48,16},{64,96},{80,112},{96,64},{112,80},{1... | collective-permute-start | bytes 688136 | tf_op jit(solution)/shard_map/ppermute | solution.py:21
  79.5 34.2 %copy-start.1 = (bf16[8,1024,128]{2,1,0:T(8,128)(2,1)S(1)}, bf16[8,1024,128]{2,1,0:T(8,128)(2,1)}, u32[]{:S(2)}) copy-start(bf16[8,1024,128]{2,1,0:T(8,128)(2,1)} %all-gather.5.cloned.1.call-done.basis) | copy-start | bytes 6291460
  79.5 22.7 %collective-permute-start.1 = (f32[128,256]{1,0:T(8,128)S(1)}, f32[128,256]{1,0:T(8,128)S(1)}, u32[]{:S(2)}, u32[]{:S(2)}) collective-permute-start(f32[128,256]{1,0:T(8,128)S(1)} %reduce_sum.39), channel_id=1, source_target_pairs={{0,8},{8,0},{1,9},{9,1},{2,10},{10,2},{3,11},{11,3},{4,12},{12,4},... | collective-permute-start | bytes 393224 | tf_op jit(solution)/shard_map/ppermute | solution.py:21
  87.9 23.6 %collective-permute-start.4 = (bf16[128,1792]{1,0:T(8,128)(2,1)S(1)}, bf16[128,1792]{1,0:T(8,128)(2,1)S(1)}, u32[]{:S(2)}, u32[]{:S(2)}) collective-permute-start(bf16[128,1792]{1,0:T(8,128)(2,1)S(1)} %constant_dynamic-update-slice_fusion.2), channel_id=1, source_target_pairs={{0,16},{16,0},{32,48},{48,32},{64,80},{80,64},{96,112},{112,96},{1... | collective-permute-start | bytes 1376264 | tf_op jit(solution)/shard_map/ppermute | solution.py:21
  111.6 22.4 %collective-permute-start.5 = (bf16[256,1792]{1,0:T(8,128)(2,1)S(1)}, bf16[256,1792]{1,0:T(8,128)(2,1)}, u32[]{:S(2)}, u32[]{:S(2)}) collective-permute-start(bf16[256,1792]{1,0:T(8,128)(2,1)S(1)} %constant_dynamic-update-slice_fusion.4.o0), channel_id=1, source_target_pairs={{0,128},{128,0},{256,384},{384,256},{1,129},{129,1},{257,385},{385... | collective-permute-start | bytes 2752520 | tf_op jit(solution)/shard_map/ppermute | solution.py:21
  115.1 25.3 %all-to-all-start.4 = ((bf16[8,128,128]{2,1,0:T(8,128)(2,1)}), bf16[8,128,128]{2,1,0:T(8,128)(2,1)S(1)}, u32[]{:S(2)}, u32[]{:S(2)}) async-start(bf16[8,128,128]{2,1,0:T(8,128)(2,1)} %shard_map.67), calls=%async_computation.4 | async-start | bytes 524288 | tf_op jit(solution)/shard_map/all_to_all | solution.py:25
  136.6 3.8 %collective-permute-start.6 = (f32[4,64,512]{2,1,0:T(8,128)S(1)}, f32[4,64,512]{2,1,0:T(8,128)S(1)}, u32[]{:S(2)}, u32[]{:S(2)}) collective-permute-start(f32[4,64,512]{2,1,0:T(8,128)S(1)} %slice.51), channel_id=1, source_target_pairs={{0,1},{1,0},{2,3},{3,2},{4,5},{5,4},{6,7},{7,6},{8,9},{9,8},{10,11... | collective-permute-start | bytes 1572872 | tf_op jit(solution)/shard_map/ppermute | solution.py:21
  141.2 25.7 %all-to-all-start.5 = ((bf16[8,128,128]{2,1,0:T(8,128)(2,1)}), bf16[8,128,128]{2,1,0:T(8,128)(2,1)S(1)}, u32[]{:S(2)}, u32[]{:S(2)}) async-start(bf16[8,128,128]{2,1,0:T(8,128)(2,1)} %broadcast_in_dim.5), calls=%async_computation.5 | async-start | bytes 524288 | tf_op jit(solution)/shard_map/all_to_all | solution.py:25
  150.5 10.9 %collective-permute-start.7 = (f32[64,512]{1,0:T(8,128)S(1)}, f32[64,512]{1,0:T(8,128)S(1)}, u32[]{:S(2)}, u32[]{:S(2)}) collective-permute-start(f32[64,512]{1,0:T(8,128)S(1)} %get-tuple-element.31), channel_id=1, source_target_pairs={{0,2},{2,4},{4,6},{6,0},{1,3},{3,5},{5,7},{7,1},{8,10},{10,12},{12... | collective-permute-start | bytes 393224 | tf_op jit(solution)/shard_map/ppermute | solution.py:125
  152.4 9.0 %collective-permute-start.8 = (f32[64,512]{1,0:T(8,128)S(1)}, f32[64,512]{1,0:T(8,128)S(1)}, u32[]{:S(2)}, u32[]{:S(2)}) collective-permute-start(f32[64,512]{1,0:T(8,128)S(1)} %get-tuple-element.29), channel_id=1, source_target_pairs={{0,4},{2,6},{4,0},{6,2},{1,5},{3,7},{5,1},{7,3},{8,12},{10,14},{12... | collective-permute-start | bytes 393224 | tf_op jit(solution)/shard_map/ppermute | solution.py:125
  155.1 9.0 %collective-permute-start.9 = (f32[64,512]{1,0:T(8,128)S(1)}, f32[64,512]{1,0:T(8,128)S(1)}, u32[]{:S(2)}, u32[]{:S(2)}) collective-permute-start(f32[64,512]{1,0:T(8,128)S(1)} %get-tuple-element.30), channel_id=1, source_target_pairs={{0,6},{2,0},{4,2},{6,4},{1,7},{3,1},{5,3},{7,5},{8,14},{10,8},{12,... | collective-permute-start | bytes 393224 | tf_op jit(solution)/shard_map/ppermute | solution.py:125
  167.0 1.6 copy-start.2
  170.1 12.9 %all-to-all-start.6 = ((f32[4,256,128]{2,1,0:T(8,128)}), f32[4,256,128]{2,1,0:T(8,128)S(1)}, u32[]{:S(2)}, u32[]{:S(2)}) async-start(f32[4,256,128]{2,1,0:T(8,128)} %shard_map.69), calls=%async_computation.6 | async-start | bytes 1048576 | tf_op jit(solution)/shard_map/all_to_all | solution.py:25
  175.6 7.4 %collective-permute-start.10 = (f32[64,256]{1,0:T(8,128)S(1)}, f32[64,256]{1,0:T(8,128)S(1)}, u32[]{:S(2)}, u32[]{:S(2)}) collective-permute-start(f32[64,256]{1,0:T(8,128)S(1)} %get-tuple-element.32), channel_id=1, source_target_pairs={{0,384},{128,256},{256,128},{384,0},{1,385},{129,257},{257,129},{3... | collective-permute-start | bytes 196616 | tf_op jit(solution)/shard_map/ppermute | solution.py:21
  183.6 22.7 %collective-permute-start.11 = (f32[2,128,128]{2,1,0:T(8,128)S(1)}, f32[2,128,128]{2,1,0:T(8,128)S(1)}, u32[]{:S(2)}, u32[]{:S(2)}) collective-permute-start(f32[2,128,128]{2,1,0:T(8,128)S(1)} %get-tuple-element.26), channel_id=1, source_target_pairs={{0,8},{8,0},{1,9},{9,1},{2,10},{10,2},{3,11},{11,3},{4,12},{12,4},... | collective-permute-start | bytes 393224 | tf_op jit(solution)/shard_map/ppermute | solution.py:21
Sparse Core Ops, SparseCore 0:
  22.8 37.0 all-gather.4
  62.0 33.4 all-gather.2

commit v4 on v3

--- a/solution.py
+++ b/solution.py
@@ -15,6 +15,7 @@
 XOR_ORDER = (0, 4, 2, 6, 1, 5, 3, 7)
 VMEM = pl.BlockSpec(memory_space=pltpu.VMEM)
 SMEM = pl.BlockSpec(memory_space=pltpu.SMEM)
+ANY = pl.BlockSpec(memory_space=pl.ANY)
 
 
 def swap(v, axis, partner):
@@ -47,13 +48,19 @@
     )(*args)
 
 
-def cut_kernel(factors, acts, basis, mix):
+def cut_kernel(factors, acts, basis, mix, sems):
+    pairs = []
     for i in range(X):
-        q = slice(i * 128, (i + 1) * 128)
-        mix[i, :32, :] = factors[:, q]
-        mix[i, 32:288, :] = acts[:, q]
+        q = pl.ds(i * 128, 128)
+        pairs.append((acts.at[:, q], mix.at[i, pl.ds(32, 256), :]))
         for h in range(2):
-            mix[i, 288 + h * 128:416 + h * 128, :] = basis[q, h * 128:(h + 1) * 128]
+            pairs.append((basis.at[q, pl.ds(h * 128, 128)], mix.at[i, pl.ds(288 + h * 128, 128), :]))
+        pairs.append((factors.at[:, q], mix.at[i, pl.ds(0, 32), :]))
+    copies = [pltpu.make_async_copy(src, dst, sems.at[n]) for n, (src, dst) in enumerate(pairs)]
+    for copy in copies:
+        copy.start()
+    for copy in copies:
+        copy.wait()
 
 
 def spread_kernel(mix, out):
@@ -64,14 +71,24 @@
             out[zl * Y * C + b] = piece
 
 
-def rotate_kernel(f, basis, rot):
+def fetch_quarters(src, held, sems):
+    copies = [
+        pltpu.make_async_copy(src.at[:, pl.ds(i * 256, 256), :], held.at[i], sems.at[i]) for i in range(X)
+    ]
+    for copy in copies:
+        copy.start()
+    return copies
+
+
+def rotate_kernel(f, basis, rot, held, sems):
+    copies = fetch_quarters(basis, held, sems)
     rows = jnp.concatenate(
         [jnp.concatenate([f[zl * Y * C + s] for zl in range(ZL)], axis=0) for s in range(Y * C)], axis=1
     )
     for i in range(X):
+        copies[i].wait()
         for h in range(2):
-            at = (i * 2 + h) * 128
-            b = jnp.concatenate([basis[s, at:at + 128, :] for s in range(Y * C)], axis=0)
+            b = jnp.concatenate([held[i, s, h * 128:(h + 1) * 128, :] for s in range(Y * C)], axis=0)
             rot[i, :, h * 128:(h + 1) * 128] = jnp.dot(rows, b, preferred_element_type=F32)
 
 
@@ -82,10 +99,12 @@
         pt[s] = lax.dot_general(b, eigs, (((1,), (1,)), ((), ())), preferred_element_type=F32).astype(BF)
 
 
-def input_kernel(acts, pt, ins):
+def input_kernel(acts, pt, ins, held, sems):
+    copies = fetch_quarters(acts, held, sems)
     p = jnp.concatenate([pt[s] for s in range(Y * C)], axis=0)
     for i in range(X):
-        a = jnp.concatenate([acts[s, i * 256:(i + 1) * 256, :] for s in range(Y * C)], axis=1)
+        copies[i].wait()
+        a = jnp.concatenate([held[i, s] for s in range(Y * C)], axis=1)
         ins[i] = jnp.dot(a, p, preferred_element_type=F32)
 
 
@@ -131,7 +150,8 @@
     ff = output_grads.shape[1]
 
     mix = call(
-        cut_kernel, jax.ShapeDtypeStruct((X, 544, 128), BF), [in_factors, activations, basis], [VMEM] * 3, 0
+        cut_kernel, jax.ShapeDtypeStruct((X, 544, 128), BF), [in_factors, activations, basis], [ANY] * 3, 0,
+        [pltpu.SemaphoreType.DMA((4 * X,))],
     )
     mix = scatter(mix, "x")
     basis_all = lax.all_gather(mix[:, 288:].reshape(1024, 128), ("y", "c"))
@@ -142,8 +162,10 @@
     grads_partner = swap(after(output_grads, f), "x", lambda i: 3 - i)
     f = scatter(f, ("zl", "y", "c"))
 
+    quarters = [pltpu.VMEM((X, Y * C, 256, 128), BF), pltpu.SemaphoreType.DMA((X,))]
     rot = call(
-        rotate_kernel, jax.ShapeDtypeStruct((X, 128, 256), F32), [f, basis_all], [VMEM] * 2, 2 * 128 * 1024 * 1024
+        rotate_kernel, jax.ShapeDtypeStruct((X, 128, 256), F32), [f, basis_all], [VMEM, ANY],
+        2 * 128 * 1024 * 1024, quarters,
     )
     rx = after(scatter(rot, "x"), grads_partner)
     o = jnp.concatenate([after(out_factors, rot), o_in], axis=0)
@@ -178,7 +200,8 @@
     out_partner = swap(part[:, 256:], "x", lambda i: 3 - i)
 
     ins = call(
-        input_kernel, jax.ShapeDtypeStruct((X, 256, 128), F32), [acts_all, precond], [VMEM] * 2, 2 * 128 * 1024 * 1024
+        input_kernel, jax.ShapeDtypeStruct((X, 256, 128), F32), [acts_all, precond], [ANY, VMEM],
+        2 * 128 * 1024 * 1024, quarters,
     )
     keep, send = call(
         sides_kernel,

time: 223 us -> 225 us (level)
  no operation moved by 1% of the time
where the time goes in v4:
time: 225 us; the launch traced here: 224 us
  starting transfers between devices  96.2 us (43%)
  waiting for transfers between devices  65.3 us (29%)
  blocking collectives  29.4 us (13%)
  between operations  13.8 us (6%)
  Pallas kernels  9.88 us (4%)
  local copies, waits for them, and re-layouts  8.93 us (4%)
    all_to_all x5, starting transfers between devices, scatter(): return lax.all_to_all(v, axis, 0, 0, tiled=True)  46.3 us
    ppermute x9, waiting for transfers between devices, swap(): lax.ppermute(v, axis, [(i, partner(i)) for i in range(lax.axis_size(axis))])  41.2 us
    ppermute x9, starting transfers between devices, swap(): lax.ppermute(v, axis, [(i, partner(i)) for i in range(lax.axis_size(axis))])  40.9 us
    all_to_all x3, blocking collectives, scatter(): return lax.all_to_all(v, axis, 0, 0, tiled=True)  29.4 us
    all_to_all x5, waiting for transfers between devices, scatter(): return lax.all_to_all(v, axis, 0, 0, tiled=True)  19.5 us
    pallas_call x7, Pallas kernels, call(): pl.pallas_call(kernel, out_shape=out, in_specs=specs, out_specs=[VMEM] *...  9.88 us
    ppermute x3, starting transfers between devices, from_next(): return lax.ppermute(v, axis, [(i, (i - by) % n) for i in range(n)])  8.97 us
    unnamed x21, local copies, waits for them, and re-layouts  5.92 us
  transfers between devices with their start and end apart: 19, of which 10 were waited for; matrix products, arithmetic and copies ran while one was open for 1% of the time, Pallas kernels for 3%

profile of v4, /device:TPU:38, one launch (start us, length us, event | category | flops | bytes accessed | tf_op | source)
XLA Modules:
  0.0 223.8 jit_solution(1512908938057590323)
XLA Ops:
  6.5 0.9 copy-done.4
  7.5 0.9 copy-done.5
  8.4 0.8 copy-done.6
  9.2 0.3 shard_map.64
  9.5 0.0 copy-start.3
  9.5 0.0 copy-start.7
  9.5 0.0 copy-start.8
  9.5 12.5 %all_to_all.45.mix = bf16[4,544,128]{2,1,0:T(8,128)(2,1)S(1)} all-to-all(bf16[4,544,128]{2,1,0:T(8,128)(2,1)S(1)} %shard_map.64), channel_id=1, replica_groups=mesh['x'=4,'zl'=8,'zh'=2,'y'=4,'c'=2] {'x'}, dimensions={0} | all-to-all | bytes 1114112 | tf_op jit(solution)/shard_map/all_to_all | solution.py:26
  22.0 0.9 fusion.1
  22.8 0.0 all-gather.5.cloned.1.call-update
  22.9 0.7 shard_map.65
  23.6 15.8 %all-to-all-start.1 = ((bf16[64,16,128]{2,1,0:T(8,128)(2,1)}), bf16[64,16,128]{2,1,0:T(8,128)(2,1)S(1)}, u32[]{:S(2)}, u32[]{:S(2)}) async-start(bf16[64,16,128]{2,1,0:T(8,128)(2,1)} %shard_map.65), calls=%async_computation.1 | async-start | bytes 524288 | tf_op jit(solution)/shard_map/all_to_all | solution.py:26
  39.4 0.0 all-gather.3.cloned.1.call-start
  39.5 4.0 %collective-permute-start = (bf16[256,1792]{1,0:T(8,128)(2,1)S(1)}, bf16[256,1792]{1,0:T(8,128)(2,1)S(1)}, u32[]{:S(2)}, u32[]{:S(2)}) collective-permute-start(bf16[256,1792]{1,0:T(8,128)(2,1)S(1)} %copy-done.3), channel_id=1, source_target_pairs={{0,384},{128,256},{256,128},{384,0},{1,385},{129,257},{257,129},{3... | collective-permute-start | bytes 2752520 | tf_op jit(solution)/shard_map/ppermute | solution.py:22
  43.5 7.4 %collective-permute-start.2 = (bf16[32,1792]{1,0:T(8,128)(2,1)S(1)}, bf16[32,1792]{1,0:T(8,128)(2,1)S(1)}, u32[]{:S(2)}, u32[]{:S(2)}) collective-permute-start(bf16[32,1792]{1,0:T(8,128)(2,1)S(1)} %copy-done.7), channel_id=1, source_target_pairs={{0,64},{16,80},{32,96},{48,112},{64,0},{80,16},{96,32},{112,48},{1... | collective-permute-start | bytes 344072 | tf_op jit(solution)/shard_map/ppermute | solution.py:22
  50.9 0.0 all-gather.3.cloned.1.call-update
  51.0 12.1 %all-to-all-done.1.f = bf16[64,16,128]{2,1,0:T(8,128)(2,1)S(1)} async-done(((bf16[64,16,128]{2,1,0:T(8,128)(2,1)}), bf16[64,16,128]{2,1,0:T(8,128)(2,1)S(1)}, u32[]{:S(2)}, u32[]{:S(2)}) %all-to-all-start.1) | async-done | bytes 262176 | tf_op jit(solution)/shard_map/all_to_all | solution.py:26
  63.1 1.6 copy-done
  64.7 2.2 shard_map.66
  66.8 5.5 %all-to-all-start.2 = ((f32[4,128,256]{2,1,0:T(8,128)}), f32[4,128,256]{2,1,0:T(8,128)S(1)}, u32[]{:S(2)}, u32[]{:S(2)}) async-start(f32[4,128,256]{2,1,0:T(8,128)} %shard_map.66), calls=%async_computation.2 | async-start | bytes 1048576 | tf_op jit(solution)/shard_map/all_to_all | solution.py:26
  72.4 0.0 collective-permute-done.2
  72.4 3.3 %collective-permute-start.3 = (bf16[64,1792]{1,0:T(8,128)(2,1)S(1)}, bf16[64,1792]{1,0:T(8,128)(2,1)S(1)}, u32[]{:S(2)}, u32[]{:S(2)}) collective-permute-start(bf16[64,1792]{1,0:T(8,128)(2,1)S(1)} %constant_dynamic-update-slice_fusion), channel_id=1, source_target_pairs={{0,32},{16,48},{32,0},{48,16},{64,96},{80,112},{96,64},{112,80},{1... | collective-permute-start | bytes 688136 | tf_op jit(solution)/shard_map/ppermute | solution.py:22
  75.8 0.0 collective-permute-done.g1
  75.8 4.6 %all-to-all-done.2 = f32[4,128,256]{2,1,0:T(8,128)S(1)} async-done(((f32[4,128,256]{2,1,0:T(8,128)}), f32[4,128,256]{2,1,0:T(8,128)S(1)}, u32[]{:S(2)}, u32[]{:S(2)}) %all-to-all-start.2) | async-done | bytes 524320 | tf_op jit(solution)/shard_map/all_to_all | solution.py:26
  80.4 8.4 %collective-permute-start.1 = (f32[128,256]{1,0:T(8,128)S(1)}, f32[128,256]{1,0:T(8,128)S(1)}, u32[]{:S(2)}, u32[]{:S(2)}) collective-permute-start(f32[128,256]{1,0:T(8,128)S(1)} %reduce_sum.39), channel_id=1, source_target_pairs={{0,8},{8,0},{1,9},{9,1},{2,10},{10,2},{3,11},{11,3},{4,12},{12,4},... | collective-permute-start | bytes 393224 | tf_op jit(solution)/shard_map/ppermute | solution.py:22
  88.8 0.0 collective-permute-done.3
  88.8 3.7 %collective-permute-start.4 = (bf16[128,1792]{1,0:T(8,128)(2,1)S(1)}, bf16[128,1792]{1,0:T(8,128)(2,1)S(1)}, u32[]{:S(2)}, u32[]{:S(2)}) collective-permute-start(bf16[128,1792]{1,0:T(8,128)(2,1)S(1)} %constant_dynamic-update-slice_fusion.2), channel_id=1, source_target_pairs={{0,16},{16,0},{32,48},{48,32},{64,80},{80,64},{96,112},{112,96},{1... | collective-permute-start | bytes 1376264 | tf_op jit(solution)/shard_map/ppermute | solution.py:22
  92.5 10.6 %collective-permute-done.1 = f32[128,256]{1,0:T(8,128)S(1)} collective-permute-done((f32[128,256]{1,0:T(8,128)S(1)}, f32[128,256]{1,0:T(8,128)S(1)}, u32[]{:S(2)}, u32[]{:S(2)}) %collective-permute-start.1) | collective-permute-done | bytes 131104 | tf_op jit(solution)/shard_map/ppermute | solution.py:22
  103.1 9.2 %all_to_all.46.scaled = bf16[4,128,256]{2,1,0:T(8,128)(2,1)S(1)} all-to-all(bf16[4,128,256]{2,1,0:T(8,128)(2,1)S(1)} %broadcast_in_dim.4), channel_id=1, replica_groups=mesh['x'=4,'zl'=8,'zh'=2,'y'=4,'c'=2] {'x'}, dimensions={0} | all-to-all | bytes 524288 | tf_op jit(solution)/shard_map/all_to_all | solution.py:26
  112.4 0.0 collective-permute-done.4
  112.4 2.1 collective-permute-start.5
  114.6 1.4 shard_map.67
  116.0 10.2 %all-to-all-start.4 = ((bf16[8,128,128]{2,1,0:T(8,128)(2,1)}), bf16[8,128,128]{2,1,0:T(8,128)(2,1)S(1)}, u32[]{:S(2)}, u32[]{:S(2)}) async-start(bf16[8,128,128]{2,1,0:T(8,128)(2,1)} %shard_map.67), calls=%async_computation.4 | async-start | bytes 524288 | tf_op jit(solution)/shard_map/all_to_all | solution.py:26
  126.2 0.1 stack.23.pos
  126.3 8.6 %collective-permute-done.5.o1 = bf16[256,1792]{1,0:T(8,128)(2,1)} collective-permute-done((bf16[256,1792]{1,0:T(8,128)(2,1)S(1)}, bf16[256,1792]{1,0:T(8,128)(2,1)}, u32[]{:S(2)}, u32[]{:S(2)}) %collective-permute-start.5) | collective-permute-done | bytes 917536 | tf_op jit(solution)/shard_map/ppermute | solution.py:22
  134.8 2.5 %shard_map.68 = f32[8,64,512]{2,1,0:T(8,128)S(1)} custom-call(s32[5]{0:T(128)S(1)} %stack.23.pos, bf16[256,1792]{1,0:T(8,128)(2,1)S(1)} %copy-done.3, bf16[256,1792]{1,0:T(8,128)(2,1)S(1)} %collective-permute-done.g1, bf16[256,1792]{1,0:T(8,128)(2,1)S(1)} %constant_dynamic-update-slice_fusion.4.o0, bf16[256,1792]{1,0:T(8,128)(2,1)} %collective-permute-done.5.o1), custom_call_target="tpu_custom_call" | custom-call | flops 939524096 | bytes 3670036 | tf_op jit(solution)/shard_map/pallas_call | solution.py:40
  137.4 1.9 collective-permute-start.6
  139.3 1.9 collective-permute-done.6
  141.2 0.1 slice_add_fusion
  141.3 0.0 all-to-all-done.4
  141.4 0.7 broadcast_in_dim.5
  142.1 9.2 %all-to-all-start.5 = ((bf16[8,128,128]{2,1,0:T(8,128)(2,1)}), bf16[8,128,128]{2,1,0:T(8,128)(2,1)S(1)}, u32[]{:S(2)}, u32[]{:S(2)}) async-start(bf16[8,128,128]{2,1,0:T(8,128)(2,1)} %broadcast_in_dim.5), calls=%async_computation.5 | async-start | bytes 524288 | tf_op jit(solution)/shard_map/all_to_all | solution.py:26
  151.3 1.9 collective-permute-start.7
  153.3 2.7 %collective-permute-start.8 = (f32[64,512]{1,0:T(8,128)S(1)}, f32[64,512]{1,0:T(8,128)S(1)}, u32[]{:S(2)}, u32[]{:S(2)}) collective-permute-start(f32[64,512]{1,0:T(8,128)S(1)} %get-tuple-element.29), channel_id=1, source_target_pairs={{0,4},{2,6},{4,0},{6,2},{1,5},{3,7},{5,1},{7,3},{8,12},{10,14},{12... | collective-permute-start | bytes 393224 | tf_op jit(solution)/shard_map/ppermute | solution.py:144
  156.0 4.3 %collective-permute-start.9 = (f32[64,512]{1,0:T(8,128)S(1)}, f32[64,512]{1,0:T(8,128)S(1)}, u32[]{:S(2)}, u32[]{:S(2)}) collective-permute-start(f32[64,512]{1,0:T(8,128)S(1)} %get-tuple-element.30), channel_id=1, source_target_pairs={{0,6},{2,0},{4,2},{6,4},{1,7},{3,1},{5,3},{7,5},{8,14},{10,8},{12,... | collective-permute-start | bytes 393224 | tf_op jit(solution)/shard_map/ppermute | solution.py:144
  160.3 1.9 collective-permute-done.7
  162.2 0.0 collective-permute-done.8
  162.2 2.8 %collective-permute-done.9 = f32[64,512]{1,0:T(8,128)S(1)} collective-permute-done((f32[64,512]{1,0:T(8,128)S(1)}, f32[64,512]{1,0:T(8,128)S(1)}, u32[]{:S(2)}, u32[]{:S(2)}) %collective-permute-start.9) | collective-permute-done | bytes 131104 | tf_op jit(solution)/shard_map/ppermute | solution.py:144
  165.0 0.0 all-gather.3.cloned.1.call-done.acts
  165.1 2.8 %all-to-all-done.5.pt = bf16[8,128,128]{2,1,0:T(8,128)(2,1)S(1)} async-done(((bf16[8,128,128]{2,1,0:T(8,128)(2,1)}), bf16[8,128,128]{2,1,0:T(8,128)(2,1)S(1)}, u32[]{:S(2)}, u32[]{:S(2)}) %all-to-all-start.5) | async-done | bytes 262176 | tf_op jit(solution)/shard_map/all_to_all | solution.py:26
  167.8 1.6 copy-done.2
  169.4 2.1 shard_map.69
  171.6 5.5 %all-to-all-start.6 = ((f32[4,256,128]{2,1,0:T(8,128)}), f32[4,256,128]{2,1,0:T(8,128)S(1)}, u32[]{:S(2)}, u32[]{:S(2)}) async-start(f32[4,256,128]{2,1,0:T(8,128)} %shard_map.69), calls=%async_computation.6 | async-start | bytes 1048576 | tf_op jit(solution)/shard_map/all_to_all | solution.py:26
  177.1 1.9 collective-permute-start.10
  179.1 5.4 %collective-permute-done.10.out_partner = f32[64,256]{1,0:T(8,128)S(1)} collective-permute-done((f32[64,256]{1,0:T(8,128)S(1)}, f32[64,256]{1,0:T(8,128)S(1)}, u32[]{:S(2)}, u32[]{:S(2)}) %collective-permute-start.10) | collective-permute-done | bytes 65568 | tf_op jit(solution)/shard_map/ppermute | solution.py:22
  184.5 0.0 all-to-all-done.6.parts
  184.5 0.6 shard_map.70
  185.1 8.1 %collective-permute-start.11 = (f32[2,128,128]{2,1,0:T(8,128)S(1)}, f32[2,128,128]{2,1,0:T(8,128)S(1)}, u32[]{:S(2)}, u32[]{:S(2)}) collective-permute-start(f32[2,128,128]{2,1,0:T(8,128)S(1)} %get-tuple-element.26), channel_id=1, source_target_pairs={{0,8},{8,0},{1,9},{9,1},{2,10},{10,2},{3,11},{11,3},{4,12},{12,4},... | collective-permute-start | bytes 393224 | tf_op jit(solution)/shard_map/ppermute | solution.py:22
  193.3 14.7 %collective-permute-done.11 = f32[2,128,128]{2,1,0:T(8,128)S(1)} collective-permute-done((f32[2,128,128]{2,1,0:T(8,128)S(1)}, f32[2,128,128]{2,1,0:T(8,128)S(1)}, u32[]{:S(2)}, u32[]{:S(2)}) %collective-permute-start.11) | collective-permute-done | bytes 131104 | tf_op jit(solution)/shard_map/ppermute | solution.py:22
  208.0 0.1 reshape.17
  208.1 0.2 copy.8
  208.3 0.3 all_to_all.36
  208.6 7.7 %all_to_all.47 = f32[8,1,512]{2,1,0:T(1,128)S(1)} all-to-all(f32[8,1,512]{2,1,0:T(1,128)S(1)} %all_to_all.36), channel_id=1, replica_groups=mesh['x'=4,'zl'=8,'zh'=2,'y'=4,'c'=2] {'y','c'}, dimensions={0} | all-to-all | bytes 32768 | tf_op jit(solution)/shard_map/all_to_all | solution.py:26
  216.3 0.7 reshape.18
  (31 shorter events, 0.5 us)
Async XLA Ops:
  6.5 56.5 %all-gather.5.cloned.1.call-start = ((), (), s32[]{:S(2)}) async-start(), calls=%async_computation.9 | async-start | bytes 2359296 | tf_op jit(solution)/shard_map/all_gather | solution.py:157
  6.5 0.9 copy-start.4
  7.5 0.9 copy-start.5
  8.4 0.8 copy-start.6
  9.5 30.0 %copy-start.3 = (bf16[256,1792]{1,0:T(8,128)(2,1)S(1)}, bf16[256,1792]{1,0:T(8,128)(2,1)}, u32[]{:S(2)}) copy-start(bf16[256,1792]{1,0:T(8,128)(2,1)} %g0.1) | copy-start | bytes 2752516
  9.5 34.0 %copy-start.7 = (bf16[32,1792]{1,0:T(8,128)(2,1)S(1)}, bf16[32,1792]{1,0:T(8,128)(2,1)}, u32[]{:S(2)}) copy-start(bf16[32,1792]{1,0:T(8,128)(2,1)} %param.8) | copy-start | bytes 344068
  9.5 41.4 %copy-start.8 = (f32[256]{0:T(256)S(1)}, f32[256]{0:T(256)}, u32[]{:S(2)}) copy-start(f32[256]{0:T(256)} %param.11) | copy-start | bytes 3076
  23.6 39.5 %all-to-all-start.1 = ((bf16[64,16,128]{2,1,0:T(8,128)(2,1)}), bf16[64,16,128]{2,1,0:T(8,128)(2,1)S(1)}, u32[]{:S(2)}, u32[]{:S(2)}) async-start(bf16[64,16,128]{2,1,0:T(8,128)(2,1)} %shard_map.65), calls=%async_computation.1 | async-start | bytes 524288 | tf_op jit(solution)/shard_map/all_to_all | solution.py:26
  39.4 125.6 %all-gather.3.cloned.1.call-start = ((), (), s32[]{:S(2)}) async-start(), calls=%async_computation.8 | async-start | bytes 2359296 | tf_op jit(solution)/shard_map/all_gather | solution.py:158
  39.5 36.3 %collective-permute-start = (bf16[256,1792]{1,0:T(8,128)(2,1)S(1)}, bf16[256,1792]{1,0:T(8,128)(2,1)S(1)}, u32[]{:S(2)}, u32[]{:S(2)}) collective-permute-start(bf16[256,1792]{1,0:T(8,128)(2,1)S(1)} %copy-done.3), channel_id=1, source_target_pairs={{0,384},{128,256},{256,128},{384,0},{1,385},{129,257},{257,129},{3... | collective-permute-start | bytes 2752520 | tf_op jit(solution)/shard_map/ppermute | solution.py:22
  43.5 28.9 %collective-permute-start.2 = (bf16[32,1792]{1,0:T(8,128)(2,1)S(1)}, bf16[32,1792]{1,0:T(8,128)(2,1)S(1)}, u32[]{:S(2)}, u32[]{:S(2)}) collective-permute-start(bf16[32,1792]{1,0:T(8,128)(2,1)S(1)} %copy-done.7), channel_id=1, source_target_pairs={{0,64},{16,80},{32,96},{48,112},{64,0},{80,16},{96,32},{112,48},{1... | collective-permute-start | bytes 344072 | tf_op jit(solution)/shard_map/ppermute | solution.py:22
  63.1 1.6 copy-start
  66.8 13.5 %all-to-all-start.2 = ((f32[4,128,256]{2,1,0:T(8,128)}), f32[4,128,256]{2,1,0:T(8,128)S(1)}, u32[]{:S(2)}, u32[]{:S(2)}) async-start(f32[4,128,256]{2,1,0:T(8,128)} %shard_map.66), calls=%async_computation.2 | async-start | bytes 1048576 | tf_op jit(solution)/shard_map/all_to_all | solution.py:26
  72.4 16.4 %collective-permute-start.3 = (bf16[64,1792]{1,0:T(8,128)(2,1)S(1)}, bf16[64,1792]{1,0:T(8,128)(2,1)S(1)}, u32[]{:S(2)}, u32[]{:S(2)}) collective-permute-start(bf16[64,1792]{1,0:T(8,128)(2,1)S(1)} %constant_dynamic-update-slice_fusion), channel_id=1, source_target_pairs={{0,32},{16,48},{32,0},{48,16},{64,96},{80,112},{96,64},{112,80},{1... | collective-permute-start | bytes 688136 | tf_op jit(solution)/shard_map/ppermute | solution.py:22
  80.4 34.2 %copy-start.1 = (bf16[8,1024,128]{2,1,0:T(8,128)(2,1)S(1)}, bf16[8,1024,128]{2,1,0:T(8,128)(2,1)}, u32[]{:S(2)}) copy-start(bf16[8,1024,128]{2,1,0:T(8,128)(2,1)} %all-gather.5.cloned.1.call-done.basis) | copy-start | bytes 6291460
  80.4 22.7 %collective-permute-start.1 = (f32[128,256]{1,0:T(8,128)S(1)}, f32[128,256]{1,0:T(8,128)S(1)}, u32[]{:S(2)}, u32[]{:S(2)}) collective-permute-start(f32[128,256]{1,0:T(8,128)S(1)} %reduce_sum.39), channel_id=1, source_target_pairs={{0,8},{8,0},{1,9},{9,1},{2,10},{10,2},{3,11},{11,3},{4,12},{12,4},... | collective-permute-start | bytes 393224 | tf_op jit(solution)/shard_map/ppermute | solution.py:22
  88.8 23.6 %collective-permute-start.4 = (bf16[128,1792]{1,0:T(8,128)(2,1)S(1)}, bf16[128,1792]{1,0:T(8,128)(2,1)S(1)}, u32[]{:S(2)}, u32[]{:S(2)}) collective-permute-start(bf16[128,1792]{1,0:T(8,128)(2,1)S(1)} %constant_dynamic-update-slice_fusion.2), channel_id=1, source_target_pairs={{0,16},{16,0},{32,48},{48,32},{64,80},{80,64},{96,112},{112,96},{1... | collective-permute-start | bytes 1376264 | tf_op jit(solution)/shard_map/ppermute | solution.py:22
  112.4 22.4 %collective-permute-start.5 = (bf16[256,1792]{1,0:T(8,128)(2,1)S(1)}, bf16[256,1792]{1,0:T(8,128)(2,1)}, u32[]{:S(2)}, u32[]{:S(2)}) collective-permute-start(bf16[256,1792]{1,0:T(8,128)(2,1)S(1)} %constant_dynamic-update-slice_fusion.4.o0), channel_id=1, source_target_pairs={{0,128},{128,0},{256,384},{384,256},{1,129},{129,1},{257,385},{385... | collective-permute-start | bytes 2752520 | tf_op jit(solution)/shard_map/ppermute | solution.py:22
  116.0 25.3 %all-to-all-start.4 = ((bf16[8,128,128]{2,1,0:T(8,128)(2,1)}), bf16[8,128,128]{2,1,0:T(8,128)(2,1)S(1)}, u32[]{:S(2)}, u32[]{:S(2)}) async-start(bf16[8,128,128]{2,1,0:T(8,128)(2,1)} %shard_map.67), calls=%async_computation.4 | async-start | bytes 524288 | tf_op jit(solution)/shard_map/all_to_all | solution.py:26
  137.4 3.8 %collective-permute-start.6 = (f32[4,64,512]{2,1,0:T(8,128)S(1)}, f32[4,64,512]{2,1,0:T(8,128)S(1)}, u32[]{:S(2)}, u32[]{:S(2)}) collective-permute-start(f32[4,64,512]{2,1,0:T(8,128)S(1)} %slice.51), channel_id=1, source_target_pairs={{0,1},{1,0},{2,3},{3,2},{4,5},{5,4},{6,7},{7,6},{8,9},{9,8},{10,11... | collective-permute-start | bytes 1572872 | tf_op jit(solution)/shard_map/ppermute | solution.py:22
  142.1 25.8 %all-to-all-start.5 = ((bf16[8,128,128]{2,1,0:T(8,128)(2,1)}), bf16[8,128,128]{2,1,0:T(8,128)(2,1)S(1)}, u32[]{:S(2)}, u32[]{:S(2)}) async-start(bf16[8,128,128]{2,1,0:T(8,128)(2,1)} %broadcast_in_dim.5), calls=%async_computation.5 | async-start | bytes 524288 | tf_op jit(solution)/shard_map/all_to_all | solution.py:26
  151.3 10.9 %collective-permute-start.7 = (f32[64,512]{1,0:T(8,128)S(1)}, f32[64,512]{1,0:T(8,128)S(1)}, u32[]{:S(2)}, u32[]{:S(2)}) collective-permute-start(f32[64,512]{1,0:T(8,128)S(1)} %get-tuple-element.31), channel_id=1, source_target_pairs={{0,2},{2,4},{4,6},{6,0},{1,3},{3,5},{5,7},{7,1},{8,10},{10,12},{12... | collective-permute-start | bytes 393224 | tf_op jit(solution)/shard_map/ppermute | solution.py:144
  153.3 9.0 %collective-permute-start.8 = (f32[64,512]{1,0:T(8,128)S(1)}, f32[64,512]{1,0:T(8,128)S(1)}, u32[]{:S(2)}, u32[]{:S(2)}) collective-permute-start(f32[64,512]{1,0:T(8,128)S(1)} %get-tuple-element.29), channel_id=1, source_target_pairs={{0,4},{2,6},{4,0},{6,2},{1,5},{3,7},{5,1},{7,3},{8,12},{10,14},{12... | collective-permute-start | bytes 393224 | tf_op jit(solution)/shard_map/ppermute | solution.py:144
  156.0 9.0 %collective-permute-start.9 = (f32[64,512]{1,0:T(8,128)S(1)}, f32[64,512]{1,0:T(8,128)S(1)}, u32[]{:S(2)}, u32[]{:S(2)}) collective-permute-start(f32[64,512]{1,0:T(8,128)S(1)} %get-tuple-element.30), channel_id=1, source_target_pairs={{0,6},{2,0},{4,2},{6,4},{1,7},{3,1},{5,3},{7,5},{8,14},{10,8},{12,... | collective-permute-start | bytes 393224 | tf_op jit(solution)/shard_map/ppermute | solution.py:144
  167.8 1.6 copy-start.2
  171.6 12.9 %all-to-all-start.6 = ((f32[4,256,128]{2,1,0:T(8,128)}), f32[4,256,128]{2,1,0:T(8,128)S(1)}, u32[]{:S(2)}, u32[]{:S(2)}) async-start(f32[4,256,128]{2,1,0:T(8,128)} %shard_map.69), calls=%async_computation.6 | async-start | bytes 1048576 | tf_op jit(solution)/shard_map/all_to_all | solution.py:26
  177.1 7.4 %collective-permute-start.10 = (f32[64,256]{1,0:T(8,128)S(1)}, f32[64,256]{1,0:T(8,128)S(1)}, u32[]{:S(2)}, u32[]{:S(2)}) collective-permute-start(f32[64,256]{1,0:T(8,128)S(1)} %get-tuple-element.32), channel_id=1, source_target_pairs={{0,384},{128,256},{256,128},{384,0},{1,385},{129,257},{257,129},{3... | collective-permute-start | bytes 196616 | tf_op jit(solution)/shard_map/ppermute | solution.py:22
  185.1 22.8 %collective-permute-start.11 = (f32[2,128,128]{2,1,0:T(8,128)S(1)}, f32[2,128,128]{2,1,0:T(8,128)S(1)}, u32[]{:S(2)}, u32[]{:S(2)}) collective-permute-start(f32[2,128,128]{2,1,0:T(8,128)S(1)} %get-tuple-element.26), channel_id=1, source_target_pairs={{0,8},{8,0},{1,9},{9,1},{2,10},{10,2},{3,11},{11,3},{4,12},{12,4},... | collective-permute-start | bytes 393224 | tf_op jit(solution)/shard_map/ppermute | solution.py:22
Sparse Core Ops, SparseCore 0:
  23.0 37.0 all-gather.4
  62.2 33.4 all-gather.2

commit v5 on v3

--- a/solution.py
+++ b/solution.py
@@ -136,11 +136,11 @@
     mix = scatter(mix, "x")
     basis_all = lax.all_gather(mix[:, 288:].reshape(1024, 128), ("y", "c"))
     acts_all = lax.all_gather(mix[:, 32:288].reshape(1024, 128), ("y", "c"))
-    o_in = swap(out_factors, "zl", lambda i: i ^ 4)
 
     f = call(spread_kernel, jax.ShapeDtypeStruct((ZL * Y * C, X * KB, 128), BF), [mix], [VMEM], 0)
     grads_partner = swap(after(output_grads, f), "x", lambda i: 3 - i)
     f = scatter(f, ("zl", "y", "c"))
+    o_in = swap(after(out_factors, f), "zl", lambda i: i ^ 4)
 
     rot = call(
         rotate_kernel, jax.ShapeDtypeStruct((X, 128, 256), F32), [f, basis_all], [VMEM] * 2, 2 * 128 * 1024 * 1024

time: 223 us -> 222 us (level)
  starting transfers between devices: 96.3 us -> 82.1 us
  waiting for transfers between devices: 65.1 us -> 73.8 us
  blocking collectives: 29.4 us -> 34 us
    ppermute x9, waiting for transfers between devices: 40.9 us -> 49.7 us  [swap(): lax.ppermute(v, axis, [(i, partner(i)) for i in range(lax.axis_size(axis))])]
    all_to_all x5, starting transfers between devices: 46.2 us -> 38.5 us  [scatter(): return lax.all_to_all(v, axis, 0, 0, tiled=True)]
    ppermute x9, starting transfers between devices: 41 us -> 34.6 us  [swap(): lax.ppermute(v, axis, [(i, partner(i)) for i in range(lax.axis_size(axis))])]
    all_to_all x3, blocking collectives: 29.4 us -> 34 us  [scatter(): return lax.all_to_all(v, axis, 0, 0, tiled=True)]
  transfers between devices with their start and end apart: 19 -> 19, of which waited for: 10 -> 11; matrix products, arithmetic and copies ran while one was open for 1% -> 1% of each run, Pallas kernels for 3% -> 3%
where the time goes in v5:
time: 222 us; the launch traced here: 221 us
  starting transfers between devices  82.1 us (37%)
  waiting for transfers between devices  73.8 us (33%)
  blocking collectives  34 us (15%)
  between operations  13.8 us (6%)
  local copies, waits for them, and re-layouts  8.92 us (4%)
  Pallas kernels  8.41 us (4%)
    ppermute x9, waiting for transfers between devices, swap(): lax.ppermute(v, axis, [(i, partner(i)) for i in range(lax.axis_size(axis))])  49.7 us
    all_to_all x5, starting transfers between devices, scatter(): return lax.all_to_all(v, axis, 0, 0, tiled=True)  38.5 us
    ppermute x9, starting transfers between devices, swap(): lax.ppermute(v, axis, [(i, partner(i)) for i in range(lax.axis_size(axis))])  34.6 us
    all_to_all x3, blocking collectives, scatter(): return lax.all_to_all(v, axis, 0, 0, tiled=True)  34 us
    all_to_all x5, waiting for transfers between devices, scatter(): return lax.all_to_all(v, axis, 0, 0, tiled=True)  19.2 us
    ppermute x3, starting transfers between devices, from_next(): return lax.ppermute(v, axis, [(i, (i - by) % n) for i in range(n)])  8.97 us
    pallas_call x7, Pallas kernels, call(): pl.pallas_call(kernel, out_shape=out, in_specs=specs, out_specs=[VMEM] *...  8.41 us
    unnamed x21, local copies, waits for them, and re-layouts  5.91 us
  transfers between devices with their start and end apart: 19, of which 11 were waited for; matrix products, arithmetic and copies ran while one was open for 1% of the time, Pallas kernels for 3%

profile of v5, /device:TPU:38, one launch (start us, length us, event | category | flops | bytes accessed | tf_op | source)
XLA Modules:
  0.0 221.2 jit_solution(1320779489932876821)
XLA Ops:
  6.5 0.9 copy-done.4
  7.5 0.9 copy-done.5
  8.4 0.8 copy-done.6
  9.2 0.1 shard_map.64
  9.3 0.0 copy-start.3
  9.3 0.0 copy-start.8
  9.3 0.0 copy-start.7
  9.3 12.5 %all_to_all.45.mix = bf16[4,544,128]{2,1,0:T(8,128)(2,1)S(1)} all-to-all(bf16[4,544,128]{2,1,0:T(8,128)(2,1)S(1)} %shard_map.64), channel_id=1, replica_groups=mesh['x'=4,'zl'=8,'zh'=2,'y'=4,'c'=2] {'x'}, dimensions={0} | all-to-all | bytes 1114112 | tf_op jit(solution)/shard_map/all_to_all | solution.py:25
  21.8 0.9 fusion.1
  22.6 0.0 all-gather.5.cloned.1.call-update
  22.7 0.7 shard_map.65
  23.4 15.8 %all-to-all-start.1 = ((bf16[64,16,128]{2,1,0:T(8,128)(2,1)}), bf16[64,16,128]{2,1,0:T(8,128)(2,1)S(1)}, u32[]{:S(2)}, u32[]{:S(2)}) async-start(bf16[64,16,128]{2,1,0:T(8,128)(2,1)} %shard_map.65), calls=%async_computation.1 | async-start | bytes 524288 | tf_op jit(solution)/shard_map/all_to_all | solution.py:25
  39.2 0.0 all-gather.3.cloned.1.call-start
  39.3 4.0 %collective-permute-start = (bf16[256,1792]{1,0:T(8,128)(2,1)S(1)}, bf16[256,1792]{1,0:T(8,128)(2,1)S(1)}, u32[]{:S(2)}, u32[]{:S(2)}) collective-permute-start(bf16[256,1792]{1,0:T(8,128)(2,1)S(1)} %copy-done.3), channel_id=1, source_target_pairs={{0,384},{128,256},{256,128},{384,0},{1,385},{129,257},{257,129},{3... | collective-permute-start | bytes 2752520 | tf_op jit(solution)/shard_map/ppermute | solution.py:21
  43.3 0.0 all-gather.3.cloned.1.call-update
  43.3 14.7 %all-to-all-done.1.f = bf16[64,16,128]{2,1,0:T(8,128)(2,1)S(1)} async-done(((bf16[64,16,128]{2,1,0:T(8,128)(2,1)}), bf16[64,16,128]{2,1,0:T(8,128)(2,1)S(1)}, u32[]{:S(2)}, u32[]{:S(2)}) %all-to-all-start.1) | async-done | bytes 262176 | tf_op jit(solution)/shard_map/all_to_all | solution.py:25
  58.0 2.7 %collective-permute-start.2 = (bf16[32,1792]{1,0:T(8,128)(2,1)S(1)}, bf16[32,1792]{1,0:T(8,128)(2,1)S(1)}, u32[]{:S(2)}, u32[]{:S(2)}) collective-permute-start(bf16[32,1792]{1,0:T(8,128)(2,1)S(1)} %copy-done.7), channel_id=1, source_target_pairs={{0,64},{16,80},{32,96},{48,112},{64,0},{80,16},{96,32},{112,48},{1... | collective-permute-start | bytes 344072 | tf_op jit(solution)/shard_map/ppermute | solution.py:21
  60.7 0.0 all-gather.5.cloned.1.call-done.basis
  60.7 1.6 copy-done
  62.3 1.5 shard_map.66
  63.8 5.5 %all-to-all-start.2 = ((f32[4,128,256]{2,1,0:T(8,128)}), f32[4,128,256]{2,1,0:T(8,128)S(1)}, u32[]{:S(2)}, u32[]{:S(2)}) async-start(f32[4,128,256]{2,1,0:T(8,128)} %shard_map.66), calls=%async_computation.2 | async-start | bytes 1048576 | tf_op jit(solution)/shard_map/all_to_all | solution.py:25
  69.3 3.3 %collective-permute-done.2 = bf16[32,1792]{1,0:T(8,128)(2,1)S(1)} collective-permute-done((bf16[32,1792]{1,0:T(8,128)(2,1)S(1)}, bf16[32,1792]{1,0:T(8,128)(2,1)S(1)}, u32[]{:S(2)}, u32[]{:S(2)}) %collective-permute-start.2) | collective-permute-done | bytes 114720 | tf_op jit(solution)/shard_map/ppermute | solution.py:21
  72.6 2.3 %collective-permute-start.3 = (bf16[64,1792]{1,0:T(8,128)(2,1)S(1)}, bf16[64,1792]{1,0:T(8,128)(2,1)S(1)}, u32[]{:S(2)}, u32[]{:S(2)}) collective-permute-start(bf16[64,1792]{1,0:T(8,128)(2,1)S(1)} %constant_dynamic-update-slice_fusion), channel_id=1, source_target_pairs={{0,32},{16,48},{32,0},{48,16},{64,96},{80,112},{96,64},{112,80},{1... | collective-permute-start | bytes 688136 | tf_op jit(solution)/shard_map/ppermute | solution.py:21
  74.9 0.0 collective-permute-done.g1
  74.9 2.0 all-to-all-done.2
  76.9 10.7 %collective-permute-start.1 = (f32[128,256]{1,0:T(8,128)S(1)}, f32[128,256]{1,0:T(8,128)S(1)}, u32[]{:S(2)}, u32[]{:S(2)}) collective-permute-start(f32[128,256]{1,0:T(8,128)S(1)} %reduce_sum.39), channel_id=1, source_target_pairs={{0,8},{8,0},{1,9},{9,1},{2,10},{10,2},{3,11},{11,3},{4,12},{12,4},... | collective-permute-start | bytes 393224 | tf_op jit(solution)/shard_map/ppermute | solution.py:21
  87.6 0.0 collective-permute-done.3
  87.7 3.5 %collective-permute-start.4 = (bf16[128,1792]{1,0:T(8,128)(2,1)S(1)}, bf16[128,1792]{1,0:T(8,128)(2,1)S(1)}, u32[]{:S(2)}, u32[]{:S(2)}) collective-permute-start(bf16[128,1792]{1,0:T(8,128)(2,1)S(1)} %constant_dynamic-update-slice_fusion.2), channel_id=1, source_target_pairs={{0,16},{16,0},{32,48},{48,32},{64,80},{80,64},{96,112},{112,96},{1... | collective-permute-start | bytes 1376264 | tf_op jit(solution)/shard_map/ppermute | solution.py:21
  91.2 12.5 %collective-permute-done.1 = f32[128,256]{1,0:T(8,128)S(1)} collective-permute-done((f32[128,256]{1,0:T(8,128)S(1)}, f32[128,256]{1,0:T(8,128)S(1)}, u32[]{:S(2)}, u32[]{:S(2)}) %collective-permute-start.1) | collective-permute-done | bytes 131104 | tf_op jit(solution)/shard_map/ppermute | solution.py:21
  103.8 9.4 %all_to_all.46.scaled = bf16[4,128,256]{2,1,0:T(8,128)(2,1)S(1)} all-to-all(bf16[4,128,256]{2,1,0:T(8,128)(2,1)S(1)} %broadcast_in_dim.4), channel_id=1, replica_groups=mesh['x'=4,'zl'=8,'zh'=2,'y'=4,'c'=2] {'x'}, dimensions={0} | all-to-all | bytes 524288 | tf_op jit(solution)/shard_map/all_to_all | solution.py:25
  113.2 0.0 collective-permute-done.4
  113.3 2.1 collective-permute-start.5
  115.4 1.4 shard_map.67
  116.8 5.9 %all-to-all-start.4 = ((bf16[8,128,128]{2,1,0:T(8,128)(2,1)}), bf16[8,128,128]{2,1,0:T(8,128)(2,1)S(1)}, u32[]{:S(2)}, u32[]{:S(2)}) async-start(bf16[8,128,128]{2,1,0:T(8,128)(2,1)} %shard_map.67), calls=%async_computation.4 | async-start | bytes 524288 | tf_op jit(solution)/shard_map/all_to_all | solution.py:25
  122.7 0.1 stack.23.pos
  122.8 13.5 %collective-permute-done.5.o1 = bf16[256,1792]{1,0:T(8,128)(2,1)} collective-permute-done((bf16[256,1792]{1,0:T(8,128)(2,1)S(1)}, bf16[256,1792]{1,0:T(8,128)(2,1)}, u32[]{:S(2)}, u32[]{:S(2)}) %collective-permute-start.5) | collective-permute-done | bytes 917536 | tf_op jit(solution)/shard_map/ppermute | solution.py:21
  136.3 2.5 %shard_map.68 = f32[8,64,512]{2,1,0:T(8,128)S(1)} custom-call(s32[5]{0:T(128)S(1)} %stack.23.pos, bf16[256,1792]{1,0:T(8,128)(2,1)S(1)} %copy-done.3, bf16[256,1792]{1,0:T(8,128)(2,1)S(1)} %collective-permute-done.g1, bf16[256,1792]{1,0:T(8,128)(2,1)S(1)} %constant_dynamic-update-slice_fusion.4.o0, bf16[256,1792]{1,0:T(8,128)(2,1)} %collective-permute-done.5.o1), custom_call_target="tpu_custom_call" | custom-call | flops 939524096 | bytes 3670036 | tf_op jit(solution)/shard_map/pallas_call | solution.py:39
  138.9 1.9 collective-permute-start.6
  140.8 1.9 collective-permute-done.6
  142.7 0.1 slice_add_fusion
  142.8 0.0 all-to-all-done.4
  142.8 0.7 broadcast_in_dim.5
  143.6 5.7 %all-to-all-start.5 = ((bf16[8,128,128]{2,1,0:T(8,128)(2,1)}), bf16[8,128,128]{2,1,0:T(8,128)(2,1)S(1)}, u32[]{:S(2)}, u32[]{:S(2)}) async-start(bf16[8,128,128]{2,1,0:T(8,128)(2,1)} %broadcast_in_dim.5), calls=%async_computation.5 | async-start | bytes 524288 | tf_op jit(solution)/shard_map/all_to_all | solution.py:25
  149.3 1.9 collective-permute-start.7
  151.3 5.1 %collective-permute-start.8 = (f32[64,512]{1,0:T(8,128)S(1)}, f32[64,512]{1,0:T(8,128)S(1)}, u32[]{:S(2)}, u32[]{:S(2)}) collective-permute-start(f32[64,512]{1,0:T(8,128)S(1)} %get-tuple-element.31), channel_id=1, source_target_pairs={{0,4},{2,6},{4,0},{6,2},{1,5},{3,7},{5,1},{7,3},{8,12},{10,14},{12... | collective-permute-start | bytes 393224 | tf_op jit(solution)/shard_map/ppermute | solution.py:125
  156.3 2.0 collective-permute-start.9
  158.3 1.9 collective-permute-done.7
  160.2 3.0 %collective-permute-done.9 = f32[64,512]{1,0:T(8,128)S(1)} collective-permute-done((f32[64,512]{1,0:T(8,128)S(1)}, f32[64,512]{1,0:T(8,128)S(1)}, u32[]{:S(2)}, u32[]{:S(2)}) %collective-permute-start.9) | collective-permute-done | bytes 131104 | tf_op jit(solution)/shard_map/ppermute | solution.py:125
  163.2 0.0 all-gather.3.cloned.1.call-done.acts
  163.2 2.6 %all-to-all-done.5.pt = bf16[8,128,128]{2,1,0:T(8,128)(2,1)S(1)} async-done(((bf16[8,128,128]{2,1,0:T(8,128)(2,1)}), bf16[8,128,128]{2,1,0:T(8,128)(2,1)S(1)}, u32[]{:S(2)}, u32[]{:S(2)}) %all-to-all-start.5) | async-done | bytes 262176 | tf_op jit(solution)/shard_map/all_to_all | solution.py:25
  165.8 1.6 copy-done.2
  167.4 1.5 shard_map.69
  168.9 5.5 %all-to-all-start.6 = ((f32[4,256,128]{2,1,0:T(8,128)}), f32[4,256,128]{2,1,0:T(8,128)S(1)}, u32[]{:S(2)}, u32[]{:S(2)}) async-start(f32[4,256,128]{2,1,0:T(8,128)} %shard_map.69), calls=%async_computation.6 | async-start | bytes 1048576 | tf_op jit(solution)/shard_map/all_to_all | solution.py:25
  174.5 1.9 collective-permute-start.10
  176.4 5.4 %collective-permute-done.10.out_partner = f32[64,256]{1,0:T(8,128)S(1)} collective-permute-done((f32[64,256]{1,0:T(8,128)S(1)}, f32[64,256]{1,0:T(8,128)S(1)}, u32[]{:S(2)}, u32[]{:S(2)}) %collective-permute-start.10) | collective-permute-done | bytes 65568 | tf_op jit(solution)/shard_map/ppermute | solution.py:21
  181.8 0.0 all-to-all-done.6.parts
  181.8 0.6 shard_map.70
  182.5 5.4 %collective-permute-start.11 = (f32[2,128,128]{2,1,0:T(8,128)S(1)}, f32[2,128,128]{2,1,0:T(8,128)S(1)}, u32[]{:S(2)}, u32[]{:S(2)}) collective-permute-start(f32[2,128,128]{2,1,0:T(8,128)S(1)} %get-tuple-element.28), channel_id=1, source_target_pairs={{0,8},{8,0},{1,9},{9,1},{2,10},{10,2},{3,11},{11,3},{4,12},{12,4},... | collective-permute-start | bytes 393224 | tf_op jit(solution)/shard_map/ppermute | solution.py:21
  187.9 13.1 %collective-permute-done.11 = f32[2,128,128]{2,1,0:T(8,128)S(1)} collective-permute-done((f32[2,128,128]{2,1,0:T(8,128)S(1)}, f32[2,128,128]{2,1,0:T(8,128)S(1)}, u32[]{:S(2)}, u32[]{:S(2)}) %collective-permute-start.11) | collective-permute-done | bytes 131104 | tf_op jit(solution)/shard_map/ppermute | solution.py:21
  201.1 0.1 reshape.17
  201.2 0.2 copy.8
  201.3 0.3 all_to_all.36
  201.6 12.1 %all_to_all.47 = f32[8,1,512]{2,1,0:T(1,128)S(1)} all-to-all(f32[8,1,512]{2,1,0:T(1,128)S(1)} %all_to_all.36), channel_id=1, replica_groups=mesh['x'=4,'zl'=8,'zh'=2,'y'=4,'c'=2] {'y','c'}, dimensions={0} | all-to-all | bytes 32768 | tf_op jit(solution)/shard_map/all_to_all | solution.py:25
  213.7 0.7 reshape.18
  (31 shorter events, 0.5 us)
Async XLA Ops:
  6.5 54.1 %all-gather.5.cloned.1.call-start = ((), (), s32[]{:S(2)}) async-start(), calls=%async_computation.9 | async-start | bytes 2359296 | tf_op jit(solution)/shard_map/all_gather | solution.py:137
  6.5 0.9 copy-start.4
  7.5 0.9 copy-start.5
  8.4 0.8 copy-start.6
  9.3 30.0 %copy-start.3 = (bf16[256,1792]{1,0:T(8,128)(2,1)S(1)}, bf16[256,1792]{1,0:T(8,128)(2,1)}, u32[]{:S(2)}) copy-start(bf16[256,1792]{1,0:T(8,128)(2,1)} %g0.1) | copy-start | bytes 2752516
  9.3 34.0 %copy-start.8 = (f32[256]{0:T(256)S(1)}, f32[256]{0:T(256)}, u32[]{:S(2)}) copy-start(f32[256]{0:T(256)} %param.11) | copy-start | bytes 3076
  9.3 48.7 %copy-start.7 = (bf16[32,1792]{1,0:T(8,128)(2,1)S(1)}, bf16[32,1792]{1,0:T(8,128)(2,1)}, u32[]{:S(2)}) copy-start(bf16[32,1792]{1,0:T(8,128)(2,1)} %param.8) | copy-start | bytes 344068
  23.4 34.6 %all-to-all-start.1 = ((bf16[64,16,128]{2,1,0:T(8,128)(2,1)}), bf16[64,16,128]{2,1,0:T(8,128)(2,1)S(1)}, u32[]{:S(2)}, u32[]{:S(2)}) async-start(bf16[64,16,128]{2,1,0:T(8,128)(2,1)} %shard_map.65), calls=%async_computation.1 | async-start | bytes 524288 | tf_op jit(solution)/shard_map/all_to_all | solution.py:25
  39.2 124.0 %all-gather.3.cloned.1.call-start = ((), (), s32[]{:S(2)}) async-start(), calls=%async_computation.8 | async-start | bytes 2359296 | tf_op jit(solution)/shard_map/all_gather | solution.py:138
  39.3 35.6 %collective-permute-start = (bf16[256,1792]{1,0:T(8,128)(2,1)S(1)}, bf16[256,1792]{1,0:T(8,128)(2,1)S(1)}, u32[]{:S(2)}, u32[]{:S(2)}) collective-permute-start(bf16[256,1792]{1,0:T(8,128)(2,1)S(1)} %copy-done.3), channel_id=1, source_target_pairs={{0,384},{128,256},{256,128},{384,0},{1,385},{129,257},{257,129},{3... | collective-permute-start | bytes 2752520 | tf_op jit(solution)/shard_map/ppermute | solution.py:21
  58.0 14.6 %collective-permute-start.2 = (bf16[32,1792]{1,0:T(8,128)(2,1)S(1)}, bf16[32,1792]{1,0:T(8,128)(2,1)S(1)}, u32[]{:S(2)}, u32[]{:S(2)}) collective-permute-start(bf16[32,1792]{1,0:T(8,128)(2,1)S(1)} %copy-done.7), channel_id=1, source_target_pairs={{0,64},{16,80},{32,96},{48,112},{64,0},{80,16},{96,32},{112,48},{1... | collective-permute-start | bytes 344072 | tf_op jit(solution)/shard_map/ppermute | solution.py:21
  60.7 1.6 copy-start
  63.8 13.1 %all-to-all-start.2 = ((f32[4,128,256]{2,1,0:T(8,128)}), f32[4,128,256]{2,1,0:T(8,128)S(1)}, u32[]{:S(2)}, u32[]{:S(2)}) async-start(f32[4,128,256]{2,1,0:T(8,128)} %shard_map.66), calls=%async_computation.2 | async-start | bytes 1048576 | tf_op jit(solution)/shard_map/all_to_all | solution.py:25
  72.6 15.0 %collective-permute-start.3 = (bf16[64,1792]{1,0:T(8,128)(2,1)S(1)}, bf16[64,1792]{1,0:T(8,128)(2,1)S(1)}, u32[]{:S(2)}, u32[]{:S(2)}) collective-permute-start(bf16[64,1792]{1,0:T(8,128)(2,1)S(1)} %constant_dynamic-update-slice_fusion), channel_id=1, source_target_pairs={{0,32},{16,48},{32,0},{48,16},{64,96},{80,112},{96,64},{112,80},{1... | collective-permute-start | bytes 688136 | tf_op jit(solution)/shard_map/ppermute | solution.py:21
  76.9 38.5 %copy-start.1 = (bf16[8,1024,128]{2,1,0:T(8,128)(2,1)S(1)}, bf16[8,1024,128]{2,1,0:T(8,128)(2,1)}, u32[]{:S(2)}) copy-start(bf16[8,1024,128]{2,1,0:T(8,128)(2,1)} %all-gather.5.cloned.1.call-done.basis) | copy-start | bytes 6291460
  76.9 26.8 %collective-permute-start.1 = (f32[128,256]{1,0:T(8,128)S(1)}, f32[128,256]{1,0:T(8,128)S(1)}, u32[]{:S(2)}, u32[]{:S(2)}) collective-permute-start(f32[128,256]{1,0:T(8,128)S(1)} %reduce_sum.39), channel_id=1, source_target_pairs={{0,8},{8,0},{1,9},{9,1},{2,10},{10,2},{3,11},{11,3},{4,12},{12,4},... | collective-permute-start | bytes 393224 | tf_op jit(solution)/shard_map/ppermute | solution.py:21
  87.7 25.6 %collective-permute-start.4 = (bf16[128,1792]{1,0:T(8,128)(2,1)S(1)}, bf16[128,1792]{1,0:T(8,128)(2,1)S(1)}, u32[]{:S(2)}, u32[]{:S(2)}) collective-permute-start(bf16[128,1792]{1,0:T(8,128)(2,1)S(1)} %constant_dynamic-update-slice_fusion.2), channel_id=1, source_target_pairs={{0,16},{16,0},{32,48},{48,32},{64,80},{80,64},{96,112},{112,96},{1... | collective-permute-start | bytes 1376264 | tf_op jit(solution)/shard_map/ppermute | solution.py:21
  113.3 23.0 %collective-permute-start.5 = (bf16[256,1792]{1,0:T(8,128)(2,1)S(1)}, bf16[256,1792]{1,0:T(8,128)(2,1)}, u32[]{:S(2)}, u32[]{:S(2)}) collective-permute-start(bf16[256,1792]{1,0:T(8,128)(2,1)S(1)} %constant_dynamic-update-slice_fusion.4.o0), channel_id=1, source_target_pairs={{0,128},{128,0},{256,384},{384,256},{1,129},{129,1},{257,385},{385... | collective-permute-start | bytes 2752520 | tf_op jit(solution)/shard_map/ppermute | solution.py:21
  116.8 25.9 %all-to-all-start.4 = ((bf16[8,128,128]{2,1,0:T(8,128)(2,1)}), bf16[8,128,128]{2,1,0:T(8,128)(2,1)S(1)}, u32[]{:S(2)}, u32[]{:S(2)}) async-start(bf16[8,128,128]{2,1,0:T(8,128)(2,1)} %shard_map.67), calls=%async_computation.4 | async-start | bytes 524288 | tf_op jit(solution)/shard_map/all_to_all | solution.py:25
  138.9 3.8 %collective-permute-start.6 = (f32[4,64,512]{2,1,0:T(8,128)S(1)}, f32[4,64,512]{2,1,0:T(8,128)S(1)}, u32[]{:S(2)}, u32[]{:S(2)}) collective-permute-start(f32[4,64,512]{2,1,0:T(8,128)S(1)} %slice.51), channel_id=1, source_target_pairs={{0,1},{1,0},{2,3},{3,2},{4,5},{5,4},{6,7},{7,6},{8,9},{9,8},{10,11... | collective-permute-start | bytes 1572872 | tf_op jit(solution)/shard_map/ppermute | solution.py:21
  143.6 22.3 %all-to-all-start.5 = ((bf16[8,128,128]{2,1,0:T(8,128)(2,1)}), bf16[8,128,128]{2,1,0:T(8,128)(2,1)S(1)}, u32[]{:S(2)}, u32[]{:S(2)}) async-start(bf16[8,128,128]{2,1,0:T(8,128)(2,1)} %broadcast_in_dim.5), calls=%async_computation.5 | async-start | bytes 524288 | tf_op jit(solution)/shard_map/all_to_all | solution.py:25
  149.3 10.9 %collective-permute-start.7 = (f32[64,512]{1,0:T(8,128)S(1)}, f32[64,512]{1,0:T(8,128)S(1)}, u32[]{:S(2)}, u32[]{:S(2)}) collective-permute-start(f32[64,512]{1,0:T(8,128)S(1)} %get-tuple-element.33), channel_id=1, source_target_pairs={{0,2},{2,4},{4,6},{6,0},{1,3},{3,5},{5,7},{7,1},{8,10},{10,12},{12... | collective-permute-start | bytes 393224 | tf_op jit(solution)/shard_map/ppermute | solution.py:125
  151.3 9.0 %collective-permute-start.8 = (f32[64,512]{1,0:T(8,128)S(1)}, f32[64,512]{1,0:T(8,128)S(1)}, u32[]{:S(2)}, u32[]{:S(2)}) collective-permute-start(f32[64,512]{1,0:T(8,128)S(1)} %get-tuple-element.31), channel_id=1, source_target_pairs={{0,4},{2,6},{4,0},{6,2},{1,5},{3,7},{5,1},{7,3},{8,12},{10,14},{12... | collective-permute-start | bytes 393224 | tf_op jit(solution)/shard_map/ppermute | solution.py:125
  156.3 6.9 %collective-permute-start.9 = (f32[64,512]{1,0:T(8,128)S(1)}, f32[64,512]{1,0:T(8,128)S(1)}, u32[]{:S(2)}, u32[]{:S(2)}) collective-permute-start(f32[64,512]{1,0:T(8,128)S(1)} %get-tuple-element.32), channel_id=1, source_target_pairs={{0,6},{2,0},{4,2},{6,4},{1,7},{3,1},{5,3},{7,5},{8,14},{10,8},{12,... | collective-permute-start | bytes 393224 | tf_op jit(solution)/shard_map/ppermute | solution.py:125
  165.8 1.6 copy-start.2
  168.9 12.9 %all-to-all-start.6 = ((f32[4,256,128]{2,1,0:T(8,128)}), f32[4,256,128]{2,1,0:T(8,128)S(1)}, u32[]{:S(2)}, u32[]{:S(2)}) async-start(f32[4,256,128]{2,1,0:T(8,128)} %shard_map.69), calls=%async_computation.6 | async-start | bytes 1048576 | tf_op jit(solution)/shard_map/all_to_all | solution.py:25
  174.5 7.4 %collective-permute-start.10 = (f32[64,256]{1,0:T(8,128)S(1)}, f32[64,256]{1,0:T(8,128)S(1)}, u32[]{:S(2)}, u32[]{:S(2)}) collective-permute-start(f32[64,256]{1,0:T(8,128)S(1)} %get-tuple-element.34), channel_id=1, source_target_pairs={{0,384},{128,256},{256,128},{384,0},{1,385},{129,257},{257,129},{3... | collective-permute-start | bytes 196616 | tf_op jit(solution)/shard_map/ppermute | solution.py:21
  182.5 18.5 %collective-permute-start.11 = (f32[2,128,128]{2,1,0:T(8,128)S(1)}, f32[2,128,128]{2,1,0:T(8,128)S(1)}, u32[]{:S(2)}, u32[]{:S(2)}) collective-permute-start(f32[2,128,128]{2,1,0:T(8,128)S(1)} %get-tuple-element.28), channel_id=1, source_target_pairs={{0,8},{8,0},{1,9},{9,1},{2,10},{10,2},{3,11},{11,3},{4,12},{12,4},... | collective-permute-start | bytes 393224 | tf_op jit(solution)/shard_map/ppermute | solution.py:21
Sparse Core Ops, SparseCore 0:
  22.8 37.0 all-gather.4
  62.1 33.3 all-gather.2

commit v6 on v5

--- a/solution.py
+++ b/solution.py
@@ -170,8 +170,8 @@
         2 * 512 * 512 * ff,
         [pltpu.VMEM((512, ff), BF)],
     )
+    r2 = after(r2, part)
     part = part[:Y] + swap(part[Y:], "c", lambda i: 1 - i)
-    r2 = after(r2, part)
     s2 = jnp.sum(r2.astype(F32), axis=0).astype(BF)
     part = part[0] + sum(from_next(part[s], "y", -s) for s in (1, 2, 3))
     precond = after(gather(s2, "zl"), part, acts_all)

time: 222 us -> 221 us (level)
  waiting for transfers between devices: 73.8 us -> 69.7 us
  local copies, waits for them, and re-layouts: 8.92 us -> 12.2 us
    ppermute x9, waiting for transfers between devices: 49.7 us -> 45.8 us  [swap(): lax.ppermute(v, axis, [(i, partner(i)) for i in range(lax.axis_size(axis))])]
    unnamed x21 -> x29, local copies, waits for them, and re-layouts: 5.91 us -> 9.22 us
  transfers between devices with their start and end apart: 19 -> 19, of which waited for: 11 -> 10; matrix products, arithmetic and copies ran while one was open for 1% -> 1% of each run, Pallas kernels for 3% -> 2%
where the time goes in v6:
time: 221 us; the launch traced here: 220 us
  starting transfers between devices  82 us (37%)
  waiting for transfers between devices  69.7 us (32%)
  blocking collectives  34.3 us (16%)
  between operations  13.8 us (6%)
  local copies, waits for them, and re-layouts  12.2 us (6%)
  Pallas kernels  7.73 us (3%)
    ppermute x9, waiting for transfers between devices, swap(): lax.ppermute(v, axis, [(i, partner(i)) for i in range(lax.axis_size(axis))])  45.8 us
    all_to_all x5, starting transfers between devices, scatter(): return lax.all_to_all(v, axis, 0, 0, tiled=True)  36.9 us
    ppermute x9, starting transfers between devices, swap(): lax.ppermute(v, axis, [(i, partner(i)) for i in range(lax.axis_size(axis))])  35.6 us
    all_to_all x3, blocking collectives, scatter(): return lax.all_to_all(v, axis, 0, 0, tiled=True)  34.3 us
    all_to_all x5, waiting for transfers between devices, scatter(): return lax.all_to_all(v, axis, 0, 0, tiled=True)  18.9 us
    ppermute x3, starting transfers between devices, from_next(): return lax.ppermute(v, axis, [(i, (i - by) % n) for i in range(n)])  9.44 us
    unnamed x29, local copies, waits for them, and re-layouts  9.22 us
    pallas_call x7, Pallas kernels, call(): pl.pallas_call(kernel, out_shape=out, in_specs=specs, out_specs=[VMEM] *...  7.73 us
  transfers between devices with their start and end apart: 19, of which 10 were waited for; matrix products, arithmetic and copies ran while one was open for 1% of the time, Pallas kernels for 2%

profile of v6, /device:TPU:38, one launch (start us, length us, event | category | flops | bytes accessed | tf_op | source)
XLA Modules:
  0.0 220.0 jit_solution(2142259228477306551)
XLA Ops:
  6.5 0.9 copy-done.8
  7.5 0.9 copy-done.9
  8.4 0.8 copy-done.10
  9.2 0.1 shard_map.64
  9.3 0.0 copy-start.3
  9.3 0.0 copy-start.12
  9.3 0.0 copy-start.11
  9.3 12.5 %all_to_all.45.mix = bf16[4,544,128]{2,1,0:T(8,128)(2,1)S(1)} all-to-all(bf16[4,544,128]{2,1,0:T(8,128)(2,1)S(1)} %shard_map.64), channel_id=1, replica_groups=mesh['x'=4,'zl'=8,'zh'=2,'y'=4,'c'=2] {'x'}, dimensions={0} | all-to-all | bytes 1114112 | tf_op jit(solution)/shard_map/all_to_all | solution.py:25
  21.8 0.8 fusion.1
  22.6 0.0 all-gather.5.cloned.1.call-update
  22.6 0.7 shard_map.65
  23.4 15.8 %all-to-all-start.1 = ((bf16[64,16,128]{2,1,0:T(8,128)(2,1)}), bf16[64,16,128]{2,1,0:T(8,128)(2,1)S(1)}, u32[]{:S(2)}, u32[]{:S(2)}) async-start(bf16[64,16,128]{2,1,0:T(8,128)(2,1)} %shard_map.65), calls=%async_computation.1 | async-start | bytes 524288 | tf_op jit(solution)/shard_map/all_to_all | solution.py:25
  39.2 0.0 all-gather.3.cloned.1.call-start
  39.3 4.0 %collective-permute-start = (bf16[256,1792]{1,0:T(8,128)(2,1)S(1)}, bf16[256,1792]{1,0:T(8,128)(2,1)S(1)}, u32[]{:S(2)}, u32[]{:S(2)}) collective-permute-start(bf16[256,1792]{1,0:T(8,128)(2,1)S(1)} %copy-done.3), channel_id=1, source_target_pairs={{0,384},{128,256},{256,128},{384,0},{1,385},{129,257},{257,129},{3... | collective-permute-start | bytes 2752520 | tf_op jit(solution)/shard_map/ppermute | solution.py:21
  43.3 0.0 all-gather.3.cloned.1.call-update
  43.3 14.7 %all-to-all-done.1.f = bf16[64,16,128]{2,1,0:T(8,128)(2,1)S(1)} async-done(((bf16[64,16,128]{2,1,0:T(8,128)(2,1)}), bf16[64,16,128]{2,1,0:T(8,128)(2,1)S(1)}, u32[]{:S(2)}, u32[]{:S(2)}) %all-to-all-start.1) | async-done | bytes 262176 | tf_op jit(solution)/shard_map/all_to_all | solution.py:25
  58.0 2.7 %collective-permute-start.2 = (bf16[32,1792]{1,0:T(8,128)(2,1)S(1)}, bf16[32,1792]{1,0:T(8,128)(2,1)S(1)}, u32[]{:S(2)}, u32[]{:S(2)}) collective-permute-start(bf16[32,1792]{1,0:T(8,128)(2,1)S(1)} %copy-done.11), channel_id=1, source_target_pairs={{0,64},{16,80},{32,96},{48,112},{64,0},{80,16},{96,32},{112,48},{1... | collective-permute-start | bytes 344072 | tf_op jit(solution)/shard_map/ppermute | solution.py:21
  60.6 0.0 all-gather.5.cloned.1.call-done.basis
  60.7 1.6 copy-done
  62.2 1.5 shard_map.66
  63.7 5.5 %all-to-all-start.2 = ((f32[4,128,256]{2,1,0:T(8,128)}), f32[4,128,256]{2,1,0:T(8,128)S(1)}, u32[]{:S(2)}, u32[]{:S(2)}) async-start(f32[4,128,256]{2,1,0:T(8,128)} %shard_map.66), calls=%async_computation.2 | async-start | bytes 1048576 | tf_op jit(solution)/shard_map/all_to_all | solution.py:25
  69.3 3.3 %collective-permute-done.2 = bf16[32,1792]{1,0:T(8,128)(2,1)S(1)} collective-permute-done((bf16[32,1792]{1,0:T(8,128)(2,1)S(1)}, bf16[32,1792]{1,0:T(8,128)(2,1)S(1)}, u32[]{:S(2)}, u32[]{:S(2)}) %collective-permute-start.2) | collective-permute-done | bytes 114720 | tf_op jit(solution)/shard_map/ppermute | solution.py:21
  72.6 2.3 %collective-permute-start.3 = (bf16[64,1792]{1,0:T(8,128)(2,1)S(1)}, bf16[64,1792]{1,0:T(8,128)(2,1)S(1)}, u32[]{:S(2)}, u32[]{:S(2)}) collective-permute-start(bf16[64,1792]{1,0:T(8,128)(2,1)S(1)} %constant_dynamic-update-slice_fusion), channel_id=1, source_target_pairs={{0,32},{16,48},{32,0},{48,16},{64,96},{80,112},{96,64},{112,80},{1... | collective-permute-start | bytes 688136 | tf_op jit(solution)/shard_map/ppermute | solution.py:21
  74.9 0.0 collective-permute-done.g1
  74.9 1.9 all-to-all-done.2
  76.9 10.7 %collective-permute-start.1 = (f32[128,256]{1,0:T(8,128)S(1)}, f32[128,256]{1,0:T(8,128)S(1)}, u32[]{:S(2)}, u32[]{:S(2)}) collective-permute-start(f32[128,256]{1,0:T(8,128)S(1)} %reduce_sum.39), channel_id=1, source_target_pairs={{0,8},{8,0},{1,9},{9,1},{2,10},{10,2},{3,11},{11,3},{4,12},{12,4},... | collective-permute-start | bytes 393224 | tf_op jit(solution)/shard_map/ppermute | solution.py:21
  87.6 0.0 collective-permute-done.3
  87.6 3.5 %collective-permute-start.4 = (bf16[128,1792]{1,0:T(8,128)(2,1)S(1)}, bf16[128,1792]{1,0:T(8,128)(2,1)S(1)}, u32[]{:S(2)}, u32[]{:S(2)}) collective-permute-start(bf16[128,1792]{1,0:T(8,128)(2,1)S(1)} %constant_dynamic-update-slice_fusion.2), channel_id=1, source_target_pairs={{0,16},{16,0},{32,48},{48,32},{64,80},{80,64},{96,112},{112,96},{1... | collective-permute-start | bytes 1376264 | tf_op jit(solution)/shard_map/ppermute | solution.py:21
  91.2 12.4 %collective-permute-done.1 = f32[128,256]{1,0:T(8,128)S(1)} collective-permute-done((f32[128,256]{1,0:T(8,128)S(1)}, f32[128,256]{1,0:T(8,128)S(1)}, u32[]{:S(2)}, u32[]{:S(2)}) %collective-permute-start.1) | collective-permute-done | bytes 131104 | tf_op jit(solution)/shard_map/ppermute | solution.py:21
  103.6 9.4 %all_to_all.46.scaled = bf16[4,128,256]{2,1,0:T(8,128)(2,1)S(1)} all-to-all(bf16[4,128,256]{2,1,0:T(8,128)(2,1)S(1)} %broadcast_in_dim.4), channel_id=1, replica_groups=mesh['x'=4,'zl'=8,'zh'=2,'y'=4,'c'=2] {'x'}, dimensions={0} | all-to-all | bytes 524288 | tf_op jit(solution)/shard_map/all_to_all | solution.py:25
  113.1 2.1 collective-permute-start.5
  115.3 1.4 shard_map.67
  116.7 5.8 %all-to-all-start.4 = ((bf16[8,128,128]{2,1,0:T(8,128)(2,1)}), bf16[8,128,128]{2,1,0:T(8,128)(2,1)S(1)}, u32[]{:S(2)}, u32[]{:S(2)}) async-start(bf16[8,128,128]{2,1,0:T(8,128)(2,1)} %shard_map.67), calls=%async_computation.4 | async-start | bytes 524288 | tf_op jit(solution)/shard_map/all_to_all | solution.py:25
  122.4 0.1 stack.23.pos
  122.5 13.8 %collective-permute-done.5.o1 = bf16[256,1792]{1,0:T(8,128)(2,1)S(1)} collective-permute-done((bf16[256,1792]{1,0:T(8,128)(2,1)S(1)}, bf16[256,1792]{1,0:T(8,128)(2,1)S(1)}, u32[]{:S(2)}, u32[]{:S(2)}) %collective-permute-start.5) | collective-permute-done | bytes 917536 | tf_op jit(solution)/shard_map/ppermute | solution.py:21
  136.3 0.9 copy-done.6
  137.3 1.2 copy-done.5
  138.5 1.2 copy-done.7
  139.7 1.9 shard_map.68
  141.6 1.9 collective-permute-start.6
  143.5 0.0 all-to-all-done.4
  143.6 0.7 broadcast_in_dim.5
  144.3 4.3 %all-to-all-start.5 = ((bf16[8,128,128]{2,1,0:T(8,128)(2,1)}), bf16[8,128,128]{2,1,0:T(8,128)(2,1)S(1)}, u32[]{:S(2)}, u32[]{:S(2)}) async-start(bf16[8,128,128]{2,1,0:T(8,128)(2,1)} %broadcast_in_dim.5), calls=%async_computation.5 | async-start | bytes 524288 | tf_op jit(solution)/shard_map/all_to_all | solution.py:25
  148.6 0.1 slice_add_fusion
  148.7 1.9 collective-permute-start.7
  150.7 5.6 %collective-permute-start.8 = (f32[64,512]{1,0:T(8,128)S(1)}, f32[64,512]{1,0:T(8,128)S(1)}, u32[]{:S(2)}, u32[]{:S(2)}) collective-permute-start(f32[64,512]{1,0:T(8,128)S(1)} %get-tuple-element.31), channel_id=1, source_target_pairs={{0,4},{2,6},{4,0},{6,2},{1,5},{3,7},{5,1},{7,3},{8,12},{10,14},{12... | collective-permute-start | bytes 393224 | tf_op jit(solution)/shard_map/ppermute | solution.py:125
  156.3 1.9 collective-permute-start.9
  158.2 2.2 %collective-permute-done.8 = f32[64,512]{1,0:T(8,128)S(1)} collective-permute-done((f32[64,512]{1,0:T(8,128)S(1)}, f32[64,512]{1,0:T(8,128)S(1)}, u32[]{:S(2)}, u32[]{:S(2)}) %collective-permute-start.8) | collective-permute-done | bytes 131104 | tf_op jit(solution)/shard_map/ppermute | solution.py:125
  160.5 2.7 %collective-permute-done.9 = f32[64,512]{1,0:T(8,128)S(1)} collective-permute-done((f32[64,512]{1,0:T(8,128)S(1)}, f32[64,512]{1,0:T(8,128)S(1)}, u32[]{:S(2)}, u32[]{:S(2)}) %collective-permute-start.9) | collective-permute-done | bytes 131104 | tf_op jit(solution)/shard_map/ppermute | solution.py:125
  163.2 0.0 all-gather.3.cloned.1.call-done.acts
  163.2 2.3 %all-to-all-done.5.pt = bf16[8,128,128]{2,1,0:T(8,128)(2,1)S(1)} async-done(((bf16[8,128,128]{2,1,0:T(8,128)(2,1)}), bf16[8,128,128]{2,1,0:T(8,128)(2,1)S(1)}, u32[]{:S(2)}, u32[]{:S(2)}) %all-to-all-start.5) | async-done | bytes 262176 | tf_op jit(solution)/shard_map/all_to_all | solution.py:25
  165.5 1.6 copy-done.2
  167.1 1.5 shard_map.69
  168.6 5.5 %all-to-all-start.6 = ((f32[4,256,128]{2,1,0:T(8,128)}), f32[4,256,128]{2,1,0:T(8,128)S(1)}, u32[]{:S(2)}, u32[]{:S(2)}) async-start(f32[4,256,128]{2,1,0:T(8,128)} %shard_map.69), calls=%async_computation.6 | async-start | bytes 1048576 | tf_op jit(solution)/shard_map/all_to_all | solution.py:25
  174.1 1.9 collective-permute-start.10
  176.0 5.7 %collective-permute-done.10.out_partner = f32[64,256]{1,0:T(8,128)S(1)} collective-permute-done((f32[64,256]{1,0:T(8,128)S(1)}, f32[64,256]{1,0:T(8,128)S(1)}, u32[]{:S(2)}, u32[]{:S(2)}) %collective-permute-start.10) | collective-permute-done | bytes 65568 | tf_op jit(solution)/shard_map/ppermute | solution.py:21
  181.7 0.6 shard_map.70
  182.4 6.5 %collective-permute-start.11 = (f32[2,128,128]{2,1,0:T(8,128)S(1)}, f32[2,128,128]{2,1,0:T(8,128)S(1)}, u32[]{:S(2)}, u32[]{:S(2)}) collective-permute-start(f32[2,128,128]{2,1,0:T(8,128)S(1)} %get-tuple-element.28), channel_id=1, source_target_pairs={{0,8},{8,0},{1,9},{9,1},{2,10},{10,2},{3,11},{11,3},{4,12},{12,4},... | collective-permute-start | bytes 393224 | tf_op jit(solution)/shard_map/ppermute | solution.py:21
  188.9 10.6 %collective-permute-done.11 = f32[2,128,128]{2,1,0:T(8,128)S(1)} collective-permute-done((f32[2,128,128]{2,1,0:T(8,128)S(1)}, f32[2,128,128]{2,1,0:T(8,128)S(1)}, u32[]{:S(2)}, u32[]{:S(2)}) %collective-permute-start.11) | collective-permute-done | bytes 131104 | tf_op jit(solution)/shard_map/ppermute | solution.py:21
  199.5 0.1 reshape.17
  199.6 0.2 copy.8
  199.8 0.3 all_to_all.36
  200.0 12.4 %all_to_all.47 = f32[8,1,512]{2,1,0:T(1,128)S(1)} all-to-all(f32[8,1,512]{2,1,0:T(1,128)S(1)} %all_to_all.36), channel_id=1, replica_groups=mesh['x'=4,'zl'=8,'zh'=2,'y'=4,'c'=2] {'y','c'}, dimensions={0} | all-to-all | bytes 32768 | tf_op jit(solution)/shard_map/all_to_all | solution.py:25
  212.5 0.7 reshape.18
  (39 shorter events, 0.5 us)
Async XLA Ops:
  6.5 54.1 %all-gather.5.cloned.1.call-start = ((), (), s32[]{:S(2)}) async-start(), calls=%async_computation.9 | async-start | bytes 2359296 | tf_op jit(solution)/shard_map/all_gather | solution.py:137
  6.5 0.9 copy-start.8
  7.5 0.9 copy-start.9
  8.4 0.8 copy-start.10
  9.3 30.0 %copy-start.3 = (bf16[256,1792]{1,0:T(8,128)(2,1)S(1)}, bf16[256,1792]{1,0:T(8,128)(2,1)}, u32[]{:S(2)}) copy-start(bf16[256,1792]{1,0:T(8,128)(2,1)} %g0.1) | copy-start | bytes 2752516
  9.3 33.9 %copy-start.12 = (f32[256]{0:T(256)S(1)}, f32[256]{0:T(256)}, u32[]{:S(2)}) copy-start(f32[256]{0:T(256)} %param.11) | copy-start | bytes 3076
  9.3 48.6 %copy-start.11 = (bf16[32,1792]{1,0:T(8,128)(2,1)S(1)}, bf16[32,1792]{1,0:T(8,128)(2,1)}, u32[]{:S(2)}) copy-start(bf16[32,1792]{1,0:T(8,128)(2,1)} %param.8) | copy-start | bytes 344068
  23.4 34.6 %all-to-all-start.1 = ((bf16[64,16,128]{2,1,0:T(8,128)(2,1)}), bf16[64,16,128]{2,1,0:T(8,128)(2,1)S(1)}, u32[]{:S(2)}, u32[]{:S(2)}) async-start(bf16[64,16,128]{2,1,0:T(8,128)(2,1)} %shard_map.65), calls=%async_computation.1 | async-start | bytes 524288 | tf_op jit(solution)/shard_map/all_to_all | solution.py:25
  39.2 124.0 %all-gather.3.cloned.1.call-start = ((), (), s32[]{:S(2)}) async-start(), calls=%async_computation.8 | async-start | bytes 2359296 | tf_op jit(solution)/shard_map/all_gather | solution.py:138
  39.3 35.6 %collective-permute-start = (bf16[256,1792]{1,0:T(8,128)(2,1)S(1)}, bf16[256,1792]{1,0:T(8,128)(2,1)S(1)}, u32[]{:S(2)}, u32[]{:S(2)}) collective-permute-start(bf16[256,1792]{1,0:T(8,128)(2,1)S(1)} %copy-done.3), channel_id=1, source_target_pairs={{0,384},{128,256},{256,128},{384,0},{1,385},{129,257},{257,129},{3... | collective-permute-start | bytes 2752520 | tf_op jit(solution)/shard_map/ppermute | solution.py:21
  58.0 14.6 %collective-permute-start.2 = (bf16[32,1792]{1,0:T(8,128)(2,1)S(1)}, bf16[32,1792]{1,0:T(8,128)(2,1)S(1)}, u32[]{:S(2)}, u32[]{:S(2)}) collective-permute-start(bf16[32,1792]{1,0:T(8,128)(2,1)S(1)} %copy-done.11), channel_id=1, source_target_pairs={{0,64},{16,80},{32,96},{48,112},{64,0},{80,16},{96,32},{112,48},{1... | collective-permute-start | bytes 344072 | tf_op jit(solution)/shard_map/ppermute | solution.py:21
  60.7 1.6 copy-start
  63.7 13.1 %all-to-all-start.2 = ((f32[4,128,256]{2,1,0:T(8,128)}), f32[4,128,256]{2,1,0:T(8,128)S(1)}, u32[]{:S(2)}, u32[]{:S(2)}) async-start(f32[4,128,256]{2,1,0:T(8,128)} %shard_map.66), calls=%async_computation.2 | async-start | bytes 1048576 | tf_op jit(solution)/shard_map/all_to_all | solution.py:25
  72.6 15.0 %collective-permute-start.3 = (bf16[64,1792]{1,0:T(8,128)(2,1)S(1)}, bf16[64,1792]{1,0:T(8,128)(2,1)S(1)}, u32[]{:S(2)}, u32[]{:S(2)}) collective-permute-start(bf16[64,1792]{1,0:T(8,128)(2,1)S(1)} %constant_dynamic-update-slice_fusion), channel_id=1, source_target_pairs={{0,32},{16,48},{32,0},{48,16},{64,96},{80,112},{96,64},{112,80},{1... | collective-permute-start | bytes 688136 | tf_op jit(solution)/shard_map/ppermute | solution.py:21
  74.9 28.7 %copy-start.4 = (bf16[256,1792]{1,0:T(8,128)(2,1)}, bf16[256,1792]{1,0:T(8,128)(2,1)S(1)}, u32[]{:S(2)}) copy-start(bf16[256,1792]{1,0:T(8,128)(2,1)S(1)} %collective-permute-done.g1) | copy-start | bytes 2752516
  76.9 38.4 %copy-start.1 = (bf16[8,1024,128]{2,1,0:T(8,128)(2,1)S(1)}, bf16[8,1024,128]{2,1,0:T(8,128)(2,1)}, u32[]{:S(2)}) copy-start(bf16[8,1024,128]{2,1,0:T(8,128)(2,1)} %all-gather.5.cloned.1.call-done.basis) | copy-start | bytes 6291460
  76.9 26.7 %collective-permute-start.1 = (f32[128,256]{1,0:T(8,128)S(1)}, f32[128,256]{1,0:T(8,128)S(1)}, u32[]{:S(2)}, u32[]{:S(2)}) collective-permute-start(f32[128,256]{1,0:T(8,128)S(1)} %reduce_sum.39), channel_id=1, source_target_pairs={{0,8},{8,0},{1,9},{9,1},{2,10},{10,2},{3,11},{11,3},{4,12},{12,4},... | collective-permute-start | bytes 393224 | tf_op jit(solution)/shard_map/ppermute | solution.py:21
  87.6 25.5 %collective-permute-start.4 = (bf16[128,1792]{1,0:T(8,128)(2,1)S(1)}, bf16[128,1792]{1,0:T(8,128)(2,1)S(1)}, u32[]{:S(2)}, u32[]{:S(2)}) collective-permute-start(bf16[128,1792]{1,0:T(8,128)(2,1)S(1)} %constant_dynamic-update-slice_fusion.2), channel_id=1, source_target_pairs={{0,16},{16,0},{32,48},{48,32},{64,80},{80,64},{96,112},{112,96},{1... | collective-permute-start | bytes 1376264 | tf_op jit(solution)/shard_map/ppermute | solution.py:21
  113.1 23.2 %collective-permute-start.5 = (bf16[256,1792]{1,0:T(8,128)(2,1)S(1)}, bf16[256,1792]{1,0:T(8,128)(2,1)S(1)}, u32[]{:S(2)}, u32[]{:S(2)}) collective-permute-start(bf16[256,1792]{1,0:T(8,128)(2,1)S(1)} %constant_dynamic-update-slice_fusion.4.o0), channel_id=1, source_target_pairs={{0,128},{128,0},{256,384},{384,256},{1,129},{129,1},{257,385},{385... | collective-permute-start | bytes 2752520 | tf_op jit(solution)/shard_map/ppermute | solution.py:21
  116.7 26.8 %all-to-all-start.4 = ((bf16[8,128,128]{2,1,0:T(8,128)(2,1)}), bf16[8,128,128]{2,1,0:T(8,128)(2,1)S(1)}, u32[]{:S(2)}, u32[]{:S(2)}) async-start(bf16[8,128,128]{2,1,0:T(8,128)(2,1)} %shard_map.67), calls=%async_computation.4 | async-start | bytes 524288 | tf_op jit(solution)/shard_map/all_to_all | solution.py:25
  136.3 0.9 copy-start.6
  137.3 1.2 copy-start.5
  138.5 1.2 copy-start.7
  141.6 7.0 %collective-permute-start.6 = (f32[4,64,512]{2,1,0:T(8,128)S(1)}, f32[4,64,512]{2,1,0:T(8,128)S(1)}, u32[]{:S(2)}, u32[]{:S(2)}) collective-permute-start(f32[4,64,512]{2,1,0:T(8,128)S(1)} %slice.51), channel_id=1, source_target_pairs={{0,1},{1,0},{2,3},{3,2},{4,5},{5,4},{6,7},{7,6},{8,9},{9,8},{10,11... | collective-permute-start | bytes 1572872 | tf_op jit(solution)/shard_map/ppermute | solution.py:21
  144.3 21.2 %all-to-all-start.5 = ((bf16[8,128,128]{2,1,0:T(8,128)(2,1)}), bf16[8,128,128]{2,1,0:T(8,128)(2,1)S(1)}, u32[]{:S(2)}, u32[]{:S(2)}) async-start(bf16[8,128,128]{2,1,0:T(8,128)(2,1)} %broadcast_in_dim.5), calls=%async_computation.5 | async-start | bytes 524288 | tf_op jit(solution)/shard_map/all_to_all | solution.py:25
  148.7 9.5 %collective-permute-start.7 = (f32[64,512]{1,0:T(8,128)S(1)}, f32[64,512]{1,0:T(8,128)S(1)}, u32[]{:S(2)}, u32[]{:S(2)}) collective-permute-start(f32[64,512]{1,0:T(8,128)S(1)} %get-tuple-element.33), channel_id=1, source_target_pairs={{0,2},{2,4},{4,6},{6,0},{1,3},{3,5},{5,7},{7,1},{8,10},{10,12},{12... | collective-permute-start | bytes 393224 | tf_op jit(solution)/shard_map/ppermute | solution.py:125
  150.7 9.8 %collective-permute-start.8 = (f32[64,512]{1,0:T(8,128)S(1)}, f32[64,512]{1,0:T(8,128)S(1)}, u32[]{:S(2)}, u32[]{:S(2)}) collective-permute-start(f32[64,512]{1,0:T(8,128)S(1)} %get-tuple-element.31), channel_id=1, source_target_pairs={{0,4},{2,6},{4,0},{6,2},{1,5},{3,7},{5,1},{7,3},{8,12},{10,14},{12... | collective-permute-start | bytes 393224 | tf_op jit(solution)/shard_map/ppermute | solution.py:125
  156.3 6.9 %collective-permute-start.9 = (f32[64,512]{1,0:T(8,128)S(1)}, f32[64,512]{1,0:T(8,128)S(1)}, u32[]{:S(2)}, u32[]{:S(2)}) collective-permute-start(f32[64,512]{1,0:T(8,128)S(1)} %get-tuple-element.32), channel_id=1, source_target_pairs={{0,6},{2,0},{4,2},{6,4},{1,7},{3,1},{5,3},{7,5},{8,14},{10,8},{12,... | collective-permute-start | bytes 393224 | tf_op jit(solution)/shard_map/ppermute | solution.py:125
  165.5 1.6 copy-start.2
  168.6 13.1 %all-to-all-start.6 = ((f32[4,256,128]{2,1,0:T(8,128)}), f32[4,256,128]{2,1,0:T(8,128)S(1)}, u32[]{:S(2)}, u32[]{:S(2)}) async-start(f32[4,256,128]{2,1,0:T(8,128)} %shard_map.69), calls=%async_computation.6 | async-start | bytes 1048576 | tf_op jit(solution)/shard_map/all_to_all | solution.py:25
  174.1 7.6 %collective-permute-start.10 = (f32[64,256]{1,0:T(8,128)S(1)}, f32[64,256]{1,0:T(8,128)S(1)}, u32[]{:S(2)}, u32[]{:S(2)}) collective-permute-start(f32[64,256]{1,0:T(8,128)S(1)} %get-tuple-element.34), channel_id=1, source_target_pairs={{0,384},{128,256},{256,128},{384,0},{1,385},{129,257},{257,129},{3... | collective-permute-start | bytes 196616 | tf_op jit(solution)/shard_map/ppermute | solution.py:21
  182.4 17.1 %collective-permute-start.11 = (f32[2,128,128]{2,1,0:T(8,128)S(1)}, f32[2,128,128]{2,1,0:T(8,128)S(1)}, u32[]{:S(2)}, u32[]{:S(2)}) collective-permute-start(f32[2,128,128]{2,1,0:T(8,128)S(1)} %get-tuple-element.28), channel_id=1, source_target_pairs={{0,8},{8,0},{1,9},{9,1},{2,10},{10,2},{3,11},{11,3},{4,12},{12,4},... | collective-permute-start | bytes 393224 | tf_op jit(solution)/shard_map/ppermute | solution.py:21
Sparse Core Ops, SparseCore 0:
  22.8 37.0 all-gather.4
  62.0 33.3 all-gather.2
